TPU v7x, 32 devices: a whole 2x2x4 slice. The times are simulated.
32 devices in a mesh: shard: 4 (over y, x), context: 8 (over z, core).
Axes of the slice: x: 2, y: 2, z: 4, core: 2. Of those that a mesh axis runs over, the one named last changes fastest.
Arguments:
- inputs: bfloat16 [4096, 2560], P(('shard', 'context')), may hold values from -6 to 6
- doc_ids: int32 [4096], P('shard'), may hold values from 0 to 11, as said below
- cotangent: bfloat16 [4096, 2560], P(('shard', 'context')), may hold values from -6 to 6
- attn_gain: bfloat16 [2560], P('shard'), may hold values from 0.5 to 1.5
- query_weight: bfloat16 [2560, 2560], P('shard'), may hold values from -0.25 to 0.25
- keyval_weight: bfloat16 [2560, 512], P('shard'), may hold values from -0.125 to 0.125
- output_weight: bfloat16 [2560, 2560], P('shard'), may hold values from -1 to 1
- output_bias: bfloat16 [2560], P('shard'), may hold values from -1.796875 to 1.796875
- feed_gain: bfloat16 [2560], P('shard'), may hold values from 0.5 to 1.5
- gate_up_weight: bfloat16 [2560, 15360], P('shard'), may hold values from -0.125 to 0.125
- gate_up_bias: bfloat16 [15360], P('shard'), may hold values from -1.796875 to 1.796875
- down_weight: bfloat16 [7680, 2560], P('shard'), may hold values from -0.0625 to 0.0625
- down_bias: bfloat16 [2560], P('shard'), may hold values from -1.796875 to 1.796875
Outputs:
- block_out: bfloat16 [4096, 2560], P(('shard', 'context'))
- input_grad: float32 [4096, 2560], P(('shard', 'context'))
- attn_gain_grad: float32 [2560], P(('shard', 'context'))
- query_grad: float32 [2560, 2560], P(('shard', 'context'))
- keyval_grad: float32 [2560, 512], P(('shard', 'context'))
- output_weight_grad: float32 [2560, 2560], P(None, ('shard', 'context'))
- output_bias_grad: float32 [2560], P(('shard', 'context'))
- feed_gain_grad: float32 [2560], P(('shard', 'context'))
- gate_up_grad: float32 [2560, 15360], P(('shard', 'context'))
- gate_up_bias_grad: float32 [15360], P(('shard', 'context'))
- down_weight_grad: float32 [7680, 2560], P(None, ('shard', 'context'))
- down_bias_grad: float32 [2560], P(('shard', 'context'))
Inputs may be any that keep to these rules, and one draw needn't show every extreme that they name: `doc_ids`: ids never fall along the slots; group g (slots g * 1024 to (g + 1) * 1024 - 1) holds documents 3 g, 3 g + 1 and 3 g + 2, each nonempty, the first and the last shorter than 128 slots.
All inputs are finite; a program needn't handle non-finite values.
Results may differ from a plain program's by a relative error of at most 0.014.
The roundings to bfloat16 on the way count: a program that leaves them out, or rounds other values in their place, can miss the bound.
Values may be sent and summed in bfloat16 or wider, within the bound.
A program may use at most 640 MiB of HBM per device.

v0:
```python
import math

import jax
import jax.numpy as jnp
from jax import lax
from jax.sharding import PartitionSpec as P

HEADS = 10
DH = 256
FF = 7680
WINDOW = 2048


EPS = 1e-06
NEG = -1e30
ROPE_LOG = math.log(10000.0)


def passed_along(value, axis, steps):
    count = lax.axis_size(axis)
    first, last = (max(0, -steps), min(count, count - steps))
    return lax.ppermute(value, axis, [(source, source + steps) for source in range(first, last)])


def frequencies(head_dim):
    quarter = head_dim // 4
    steps = jnp.arange(quarter).astype(jnp.float32)
    return jnp.exp(-ROPE_LOG * (2.0 * steps) / (head_dim // 2))


def rotate(field, cosine, sine):
    width = field.shape[-1] // 2
    quarter = width // 2
    first = field[..., :quarter]
    second = field[..., quarter:width]
    return jnp.concatenate(
        [first * cosine - second * sine, second * cosine + first * sine, field[..., width:]],
        axis=-1,
    )


def rms_norm(field, gain):
    return field * lax.rsqrt(jnp.mean(field * field, axis=-1, keepdims=True) + EPS) * gain


def geglu(gate_up):
    half = gate_up.shape[-1] // 2
    return jax.nn.gelu(gate_up[:, :half], approximate=True) * gate_up[:, half:]


def over_rows(left, right):
    return lax.dot_general(
        left, right, (((0,), (0,)), ((), ())), preferred_element_type=jnp.float32
    )


def against(left, weight):
    return lax.dot_general(
        left, weight, (((1,), (1,)), ((), ())), preferred_element_type=jnp.float32
    )


def select_block(stack, index):
    return lax.dynamic_index_in_dim(stack, index, 0, keepdims=False)


def window_mask(query_slots, query_docs, anchor, doc_ids, tok_rows):
    key_slots = anchor * tok_rows + jnp.arange(tok_rows, dtype=jnp.int32)
    key_docs = lax.dynamic_slice_in_dim(doc_ids, jnp.maximum(anchor, 0) * tok_rows, tok_rows)
    distance = query_slots[:, None] - key_slots[None, :]
    return (
        (query_docs[:, None] == key_docs[None, :])
        & (key_slots[None, :] >= 0)
        & (distance >= 0)
        & (distance < WINDOW)
    )


def block_scores(queries, block, allowed):
    scores = jnp.einsum("thd,sd->ths", queries, block[:, :DH], preferred_element_type=jnp.float32)
    return jnp.where(allowed[:, None, :], scores, NEG)


def regroup(field, shard_count, context_count):
    rows_now, width = field.shape
    owned = width // (shard_count * context_count)
    return (
        field.reshape(rows_now, shard_count, context_count, owned)
        .transpose(0, 2, 1, 3)
        .reshape(rows_now, width)
    )


def gradient_terms(row_set, col_set):
    return jnp.concatenate(
        [
            over_rows(row_set[0], col_set[0]),
            over_rows(row_set[0], col_set[1]),
            over_rows(row_set[1], col_set[2]),
            over_rows(row_set[2], col_set[3]),
            over_rows(row_set[3], col_set[4]),
        ],
        axis=1,
    )


def body(
    inputs,
    doc_ids,
    cotangent,
    attn_gain,
    query_weight,
    keyval_weight,
    output_weight,
    output_bias,
    feed_gain,
    gate_up_weight,
    gate_up_bias,
    down_weight,
    down_bias,
):
    tok_rows = inputs.shape[0]
    place = lax.axis_index("context")
    depth = min((WINDOW + tok_rows - 1) // tok_rows - 1, lax.axis_size("context") - 1)
    query_slots = place * tok_rows + jnp.arange(tok_rows, dtype=jnp.int32)
    query_docs = lax.dynamic_slice_in_dim(doc_ids, place * tok_rows, tok_rows)
    angles = query_slots.astype(jnp.float32)[:, None] * frequencies(DH)[None, :]
    cosine = jnp.cos(angles)
    sine = jnp.sin(angles)
    attn_set = (
        lax.all_gather(attn_gain, "shard", axis=0, tiled=True),
        lax.all_gather(query_weight, "shard", axis=0, tiled=True),
        lax.all_gather(keyval_weight, "shard", axis=0, tiled=True),
        lax.all_gather(output_weight, "shard", axis=0, tiled=True),
        lax.all_gather(output_bias, "shard", axis=0, tiled=True),
    )
    gain_one = attn_set[0].astype(jnp.float32)
    bias_out = attn_set[4].astype(jnp.float32)
    source = inputs.astype(jnp.float32)
    attn_in = rms_norm(source, gain_one).astype(jnp.bfloat16)
    query_raw = jnp.dot(attn_in, attn_set[1], preferred_element_type=jnp.float32)
    keyval_raw = jnp.dot(attn_in, attn_set[2], preferred_element_type=jnp.float32)
    queries = (
        rotate(query_raw.reshape(tok_rows, HEADS, DH), cosine[:, None, :], sine[:, None, :])
        * DH ** (-0.5)
    ).astype(jnp.bfloat16)
    local_block = jnp.concatenate(
        [rotate(keyval_raw[:, :DH], cosine, sine), keyval_raw[:, DH:]], axis=1
    ).astype(jnp.bfloat16)
    first_stack = jnp.zeros((depth + 1, tok_rows, 2 * DH), jnp.bfloat16)
    first_stack = lax.dynamic_update_index_in_dim(first_stack, local_block, 0, 0)

    def pass_on(index, carry):
        moving, stack = carry
        moving = passed_along(moving, "context", 1)
        return (moving, lax.dynamic_update_index_in_dim(stack, moving, index, 0))

    window = lax.fori_loop(1, depth + 1, pass_on, (local_block, first_stack))[1]

    def scored(index):
        block = select_block(window, index)
        allowed = window_mask(query_slots, query_docs, place - index, doc_ids, tok_rows)
        return (block, allowed, block_scores(queries, block, allowed))

    def gather_stats(index, carry):
        top, total = carry
        block, allowed, scores = scored(index)
        new_top = jnp.maximum(top, jnp.max(scores, axis=2))
        total = total * jnp.exp(top - new_top) + jnp.sum(
            jnp.exp(scores - new_top[:, :, None]), axis=2
        )
        return (new_top, total)

    start_top = jnp.full((tok_rows, HEADS), NEG, jnp.float32)
    top, total = lax.fori_loop(
        0, depth + 1, gather_stats, (start_top, jnp.zeros((tok_rows, HEADS), jnp.float32))
    )
    log_total = top + jnp.log(total)

    def probabilities(scores, allowed):
        return jnp.where(allowed[:, None, :], jnp.exp(scores - log_total[:, :, None]), 0.0)

    def mix_values(index, carry):
        block, allowed, scores = scored(index)
        weights_low = probabilities(scores, allowed).astype(jnp.bfloat16)
        return carry + jnp.einsum(
            "ths,sd->thd", weights_low, block[:, DH:], preferred_element_type=jnp.float32
        )

    mixed = lax.fori_loop(0, depth + 1, mix_values, jnp.zeros((tok_rows, HEADS, DH), jnp.float32))
    mixed_low = mixed.reshape(tok_rows, HEADS * DH).astype(jnp.bfloat16)
    resid = source + jnp.dot(mixed_low, attn_set[3], preferred_element_type=jnp.float32) + bias_out
    feed_set = (
        lax.all_gather(feed_gain, "shard", axis=0, tiled=True),
        lax.all_gather(gate_up_weight, "shard", axis=0, tiled=True),
        lax.all_gather(gate_up_bias, "shard", axis=0, tiled=True),
        lax.all_gather(down_weight, "shard", axis=0, tiled=True),
        lax.all_gather(down_bias, "shard", axis=0, tiled=True),
    )
    gain_two = feed_set[0].astype(jnp.float32)
    feed_in = rms_norm(resid, gain_two).astype(jnp.bfloat16)
    gate_up = jnp.dot(feed_in, feed_set[1], preferred_element_type=jnp.float32) + feed_set[
        2
    ].astype(jnp.float32)
    hidden = geglu(gate_up).astype(jnp.bfloat16)
    result = (
        resid
        + jnp.dot(hidden, feed_set[3], preferred_element_type=jnp.float32)
        + feed_set[4].astype(jnp.float32)
    )
    block_out = result.astype(jnp.bfloat16)
    feed_again = (
        lax.all_gather(gate_up_weight, "shard", axis=0, tiled=True),
        lax.all_gather(down_weight, "shard", axis=0, tiled=True),
    )
    gate_up_back_weight = feed_again[0]
    down_back_weight = feed_again[1]
    grad_out = cotangent.astype(jnp.float32)
    hidden_grad = against(cotangent, down_back_weight)
    geglu_pull = jax.vjp(geglu, gate_up)[1]
    gate_up_low = geglu_pull(hidden_grad)[0].astype(jnp.bfloat16)
    feed_in_grad = against(gate_up_low, gate_up_back_weight)
    norm_two_pull = jax.vjp(rms_norm, resid, gain_two)[1]
    resid_part, gain_two_grad = norm_two_pull(feed_in_grad)
    resid_grad = grad_out + resid_part
    attn_grad_low = resid_grad.astype(jnp.bfloat16)
    attn_again = (
        lax.all_gather(query_weight, "shard", axis=0, tiled=True),
        lax.all_gather(keyval_weight, "shard", axis=0, tiled=True),
        lax.all_gather(output_weight, "shard", axis=0, tiled=True),
    )
    query_back_weight = attn_again[0]
    keyval_back_weight = attn_again[1]
    output_back_weight = attn_again[2]
    mixed_grad_low = (
        against(attn_grad_low, output_back_weight).reshape(tok_rows, HEADS, DH).astype(jnp.bfloat16)
    )

    def sum_products(index, carry):
        block, allowed, scores = scored(index)
        weights = probabilities(scores, allowed)
        value_score = jnp.einsum(
            "thd,sd->ths", mixed_grad_low, block[:, DH:], preferred_element_type=jnp.float32
        )
        return carry + jnp.sum(weights * value_score, axis=2)

    delta = lax.fori_loop(0, depth + 1, sum_products, jnp.zeros((tok_rows, HEADS), jnp.float32))

    def backward_block(index, carry):
        query_acc, pieces = carry
        block, allowed, scores = scored(index)
        weights = probabilities(scores, allowed)
        value_score = jnp.einsum(
            "thd,sd->ths", mixed_grad_low, block[:, DH:], preferred_element_type=jnp.float32
        )
        score_back = (weights * (value_score - delta[:, :, None])).astype(jnp.bfloat16)
        query_acc = query_acc + jnp.einsum(
            "ths,sd->thd", score_back, block[:, :DH], preferred_element_type=jnp.float32
        )
        key_piece = jnp.einsum(
            "ths,thd->sd", score_back, queries, preferred_element_type=jnp.float32
        )
        value_piece = jnp.einsum(
            "ths,thd->sd",
            weights.astype(jnp.bfloat16),
            mixed_grad_low,
            preferred_element_type=jnp.float32,
        )
        pieces = lax.dynamic_update_index_in_dim(
            pieces, jnp.concatenate([key_piece, value_piece], axis=1), index, 0
        )
        return (query_acc, pieces)

    start_pieces = jnp.zeros((depth + 1, tok_rows, 2 * DH), jnp.float32)
    query_acc, pieces = lax.fori_loop(
        0, depth + 1, backward_block, (jnp.zeros((tok_rows, HEADS, DH), jnp.float32), start_pieces)
    )

    def send_home(index, moving):
        moving = passed_along(moving, "context", -1)
        return moving + select_block(pieces, depth - 1 - index)

    keyval_sum = lax.fori_loop(0, depth, send_home, select_block(pieces, depth))
    keyval_grad_low = jnp.concatenate(
        [rotate(keyval_sum[:, :DH], cosine, -sine), keyval_sum[:, DH:]], axis=1
    ).astype(jnp.bfloat16)
    query_grad_low = (
        (rotate(query_acc, cosine[:, None, :], -sine[:, None, :]) * DH ** (-0.5))
        .reshape(tok_rows, HEADS * DH)
        .astype(jnp.bfloat16)
    )
    attn_in_grad = against(query_grad_low, query_back_weight) + against(
        keyval_grad_low, keyval_back_weight
    )
    norm_one_pull = jax.vjp(rms_norm, source, gain_one)[1]
    input_part, gain_one_grad = norm_one_pull(attn_in_grad)
    input_grad = resid_grad + input_part
    shard_count = lax.axis_size("shard")
    context_count = lax.axis_size("context")
    row_parts = (
        lax.all_to_all(
            regroup(attn_in, shard_count, context_count),
            "context",
            split_axis=1,
            concat_axis=0,
            tiled=True,
        ),
        lax.all_to_all(
            regroup(feed_in, shard_count, context_count),
            "context",
            split_axis=1,
            concat_axis=0,
            tiled=True,
        ),
        lax.all_to_all(
            regroup(attn_grad_low, shard_count, context_count),
            "context",
            split_axis=1,
            concat_axis=0,
            tiled=True,
        ),
        lax.all_to_all(
            regroup(cotangent, shard_count, context_count),
            "context",
            split_axis=1,
            concat_axis=0,
            tiled=True,
        ),
    )
    col_parts = (
        lax.all_gather(query_grad_low, "context", axis=0, tiled=True),
        lax.all_gather(keyval_grad_low, "context", axis=0, tiled=True),
        lax.all_gather(gate_up_low, "context", axis=0, tiled=True),
        lax.all_gather(mixed_low, "context", axis=0, tiled=True),
        lax.all_gather(hidden, "context", axis=0, tiled=True),
    )
    group_terms = gradient_terms(row_parts, col_parts)
    summed = lax.psum_scatter(group_terms, "shard", scatter_dimension=0, tiled=True)
    head_cols = HEADS * DH
    query_grad = summed[:, :head_cols]
    keyval_grad = summed[:, head_cols : head_cols + 2 * DH]
    gate_up_grad = summed[:, head_cols + 2 * DH : head_cols + 2 * DH + 2 * FF]
    output_weight_grad = summed[:, head_cols + 2 * DH + 2 * FF : 2 * head_cols + 2 * DH + 2 * FF].T
    down_weight_grad = summed[:, 2 * head_cols + 2 * DH + 2 * FF :].T
    small = (
        lax.psum_scatter(gain_one_grad, ("shard", "context"), scatter_dimension=0, tiled=True),
        lax.psum_scatter(
            jnp.sum(attn_grad_low.astype(jnp.float32), axis=0),
            ("shard", "context"),
            scatter_dimension=0,
            tiled=True,
        ),
        lax.psum_scatter(gain_two_grad, ("shard", "context"), scatter_dimension=0, tiled=True),
        lax.psum_scatter(
            jnp.sum(gate_up_low.astype(jnp.float32), axis=0),
            ("shard", "context"),
            scatter_dimension=0,
            tiled=True,
        ),
        lax.psum_scatter(
            jnp.sum(grad_out, axis=0), ("shard", "context"), scatter_dimension=0, tiled=True
        ),
    )
    return (
        block_out,
        input_grad,
        small[0],
        query_grad,
        keyval_grad,
        output_weight_grad,
        small[1],
        small[2],
        gate_up_grad,
        small[3],
        down_weight_grad,
        small[4],
    )


def solution(mesh):
    placed = (
        P(("shard", "context"), None),
        P("shard"),
        P(("shard", "context"), None),
        P("shard"),
        P("shard", None),
        P("shard", None),
        P("shard", None),
        P("shard"),
        P("shard"),
        P("shard", None),
        P("shard"),
        P("shard", None),
        P("shard"),
    )
    return jax.shard_map(
        body,
        mesh=mesh,
        in_specs=placed,
        out_specs=(
            P(("shard", "context"), None),
            P(("shard", "context"), None),
            P(("shard", "context")),
            P(("shard", "context"), None),
            P(("shard", "context"), None),
            P(None, ("shard", "context")),
            P(("shard", "context")),
            P(("shard", "context")),
            P(("shard", "context"), None),
            P(("shard", "context")),
            P(None, ("shard", "context")),
            P(("shard", "context")),
        ),
        check_vma=False,
    )
```

profile of v0, /device:TPU:0, one launch (start us, length us, event | category | flops | bytes accessed | tf_op | source)
XLA Modules:
  0.0 2890.8 jit_solution(18021450825590017033)
XLA Ops:
  10.8 9.6 all-gather
  20.4 8.2 all-gather.1
  36.0 8.7 all-gather.3
  56.5 124.8 %all-gather.18.cloned.1.call-done = bf16[2560,2560]{1,0:T(8,128)(2,1)} async-done(((bf16[640,2560]{1,0:T(8,128)(2,1)}), bf16[2560,2560]{1,0:T(8,128)(2,1)}) %all-gather.18.cloned.1.call-update) | async-done | bytes 13107216 | tf_op jit(solution)/shard_map/all_gather | solution.py:132
  181.3 8.3 fusion.100
  190.2 44.5 %while.90 = (s32[]{:T(128)}, bf16[128,512]{1,0:T(8,128)(2,1)S(1)}, bf16[8,128,512]{2,1,0:T(8,128)(2,1)}, s32[]{:T(128)}, s32[]{:T(128)}, /*index=5*/s32[]{:T(128)}) while((s32[]{:T(128)}, bf16[128,512]{1,0:T(8,128)(2,1)S(1)}, bf16[8,128,512]{2,1,0:T(8,128)(2,1)}, s32[]{:T(128)}, s32[]{:T(128)}, /*index=5*/s32[]{:T(128)}) %tuple.216), condition=%wide.region_2.3_spmd, body=%wide.region_1.2_spmd.sunk | while | flops 5 | bytes 1048731 | solution.py:158
  234.6 13.9 while.92
  248.6 32.4 %while.93 = (s32[]{:T(128)}, f32[128,10,256]{2,0,1:T(8,128)}, s32[128]{0:T(128)S(1)}, s32[]{:T(128)}, s32[1024]{0:T(1024)S(1)}, /*index=5*/bf16[8,128,512]{2,1,0...) while((s32[]{:T(128)}, f32[128,10,256]{2,0,1:T(8,128)}, ...), condition=%wide.region_8.9_spmd.clone, body=%wide.region_7.8_spmd.clone.sunk | while | flops 169198096 | bytes 3712493 | solution.py:190
  283.4 26.7 all-gather.20.cloned.1.call-done
  318.2 666.6 %all-gather.22.cloned.1.call-done = bf16[2560,15360]{1,0:T(8,128)(2,1)} async-done(((bf16[640,15360]{1,0:T(8,128)(2,1)}), bf16[2560,15360]{1,0:T(8,128)(2,1)}) %all-gather.22.cloned.1.call-update) | async-done | bytes 78643216 | tf_op jit(solution)/shard_map/all_gather | solution.py:195
  984.8 39.2 %convolution_add_fusion.2 = f32[128,15360]{1,0:T(8,128)} fusion(bf16[128,2560]{1,0:T(8,128)(2,1)} %multiply_convert_fusion.1, bf16[2560,15360]{1,0:T(8,128)(2,1)} %all-gather.22.cloned.1.call-done, f32[15360]{0:T(1024)S(1)} %bitcast.281), kind=kOutput, calls=%fused_computation.89 | convolution fusion | flops 10068295680 | bytes 87224320 | tf_op jit(solution)/shard_map/dot_general | solution.py:202
  1024.0 308.5 %all-gather.24.cloned.1.call-done = bf16[7680,2560]{1,0:T(8,128)(2,1)} async-done(((bf16[1920,2560]{1,0:T(8,128)(2,1)}), bf16[7680,2560]{1,0:T(8,128)(2,1)}) %all-gather.24.cloned.1.call-update) | async-done | bytes 39321616 | tf_op jit(solution)/shard_map/all_gather | solution.py:197
  1332.5 21.6 fusion.59
  1358.5 34.3 %multiply_reduce_fusion = (f32[2560]{0:T(1024)}, f32[128]{0:T(128)S(1)}, f32[128,2560]{1,0:T(8,128)}) fusion(f32[128,2560]{1,0:T(8,128)S(1)} %get-tuple-element.1241, f32[128]{0:T(128)S(1)} %fusion.95, f32[2560]{0:T(1024)S(1)} %reshape.556, bf16[128,15360]{1,0:T(8,128)(2,1)} %get-tuple-element.1207, bf16[2560,15360]{1,0:T(8,128)(2,1)} %all-gather.22.cloned.1.call-done), kind=kOutput, calls=%fused_computation.139 | convolution fusion | flops 10068293632 | bytes 85218304 | tf_op jit(solution)/shard_map/dot_general | solution.py:58
  1396.3 9.0 convolution_convert_fusion
  1405.9 15.8 while.94
  1421.7 29.8 %while.95 = (s32[]{:T(128)}, f32[128,10,256]{2,0,1:T(8,128)S(1)}, f32[8,128,512]{2,1,0:T(8,128)}, s32[128]{0:T(128)S(1)}, s32[]{:T(128)}, /*index=5*/s32[1024]{0...) while((s32[]{:T(128)}, f32[128,10,256]{2,0,1:T(8,128)S(1)}, ...), condition=%wide.region_15.16_spmd.clone, body=%wide.region_14.15_spmd.clone.sunk | while | flops 421413376 | bytes 9491461 | solution.py:275
  1452.6 56.0 %while.91 = (s32[]{:T(128)}, f32[128,512]{1,0:T(8,128)S(1)}, f32[8,128,512]{2,1,0:T(8,128)}, s32[]{:T(128)}, s32[]{:T(128)}, /*index=5*/s32[]{:T(128)}, s32[]{:T(128)}) while((s32[]{:T(128)}, f32[128,512]{1,0:T(8,128)S(1)}, f32[8,128,512]{2,1,0:T(8,128)}, s32[]{:T(128)}, s32[]{:T(128)}, /*index=5*/s32[]{:T(128)}, s32[]{:T(128)}) %tuple.231), condition=%wide.region_17.18_spmd, body=%wide.region_16.17_spmd.sunk | while | flops 65542 | bytes 1835175 | solution.py:283
  1514.7 8.2 all-to-all-start
  1526.6 34.9 %all-to-all-done = bf16[128,8,320]{0,2,1:T(8,128)(2,1)S(1)} async-done(((bf16[128,8,320]{0,2,1:T(8,128)(2,1)}), bf16[128,8,320]{0,2,1:T(8,128)(2,1)S(1)}, u32[]{:S(2)}, u32[]{:S(2)}) %all-to-all-start) | async-done | bytes 655392 | tf_op jit(solution)/shard_map/all_to_all | solution.py:301
  1566.2 9.4 fusion.101
  1578.4 19.6 all-to-all-done.1
  1613.0 17.2 all-gather.28.cloned.1.call-done
  1636.4 273.4 %all-gather.30.cloned.1.call-done = bf16[1024,15360]{1,0:T(8,128)(2,1)} async-done(((bf16[128,15360]{1,0:T(8,128)(2,1)}), bf16[1024,15360]{1,0:T(8,128)(2,1)}) %all-gather.30.cloned.1.call-update) | async-done | bytes 31457296 | tf_op jit(solution)/shard_map/all_gather | solution.py:333
  1909.8 20.1 convolution_dynamic-update-slice_fusion
  1929.9 37.1 %all-gather.32.cloned.1.call-done = bf16[1024,2560]{0,1:T(8,128)(2,1)} async-done(((bf16[128,2560]{0,1:T(8,128)(2,1)}), bf16[1024,2560]{0,1:T(8,128)(2,1)}) %all-gather.32.cloned.1.call-update) | async-done | bytes 5242896 | tf_op jit(solution)/shard_map/all_gather | solution.py:334
  1973.3 135.9 %all-gather.34.cloned.1.call-done = bf16[1024,7680]{1,0:T(8,128)(2,1)} async-done(((bf16[128,7680]{1,0:T(8,128)(2,1)}), bf16[1024,7680]{1,0:T(8,128)(2,1)}) %all-gather.34.cloned.1.call-update) | async-done | bytes 15728656 | tf_op jit(solution)/shard_map/all_gather | solution.py:335
  2109.2 13.1 fusion.44
  2124.2 8.1 all-gather.4
  2132.4 16.7 fusion.53
  2149.1 88.2 %all-reduce.15.cloned.1.call-done = (f32[2560]{0:T(1024)}, f32[2560]{0:T(1024)}, f32[2560]{0:T(1024)}, f32[15360]{0:T(1024)}, f32[2560]{0:T(1024)}) async-done(((f32[2560]{0:T(1024)}, f32[2560]{0:T(1024)}, f32[2560]{0:T(1024)}, f32[15360]{0:T(1024)}, f32[2560]{0:T(1024)}), (f32[2560]{0:T(1024)}, f32[2560]{0:T(1024)}, f32[2560]{0:T(1024)}, f32[15360]{0:T(1024)}, ...) | async-done | bytes 102416
  2243.8 625.6 %all-reduce.13.cloned.1.call-done = f32[320,28672]{1,0:T(8,128)} async-done(((f32[320,28672]{1,0:T(8,128)}), f32[320,28672]{1,0:T(8,128)}) %all-reduce.13.cloned.1.call-update) | async-done | bytes 36700176
  (488 shorter events, 300.1 us)
Async XLA Ops:
  7.2 45.4 %all-gather.16.cloned.1.call-start = ((), (), s32[]{:S(2)}) async-start(), calls=%async_computation.4 | async-start | bytes 3276800 | tf_op jit(solution)/shard_map/all_gather | solution.py:133
  7.9 173.4 %all-gather.18.cloned.1.call-start = ((), (), s32[]{:S(2)}) async-start(), calls=%async_computation.5 | async-start | bytes 16384000 | tf_op jit(solution)/shard_map/all_gather | solution.py:132
  8.7 301.4 %all-gather.20.cloned.1.call-start = ((), (), s32[]{:S(2)}) async-start(), calls=%async_computation.6 | async-start | bytes 16384000 | tf_op jit(solution)/shard_map/all_gather | solution.py:134
  9.4 975.4 %all-gather.22.cloned.1.call-start = ((), (), s32[]{:S(2)}) async-start(), calls=%async_computation.7 | async-start | bytes 98304000 | tf_op jit(solution)/shard_map/all_gather | solution.py:195
  10.0 1322.5 %all-gather.24.cloned.1.call-start = ((), (), s32[]{:S(2)}) async-start(), calls=%async_computation.8 | async-start | bytes 49152000 | tf_op jit(solution)/shard_map/all_gather | solution.py:197
  10.6 1595.9 %all-gather.26.cloned.1.call-start = ((), (), s32[]{:S(2)}) async-start(), calls=%async_computation.9 | async-start | bytes 5898240 | tf_op jit(solution)/shard_map/all_gather | solution.py:331
  45.3 136.0 %copy-start.5 = (bf16[128,2560]{1,0:T(8,128)(2,1)}, bf16[128,2560]{1,0:T(8,128)(2,1)S(1)}, u32[]{:S(2)}) copy-start(bf16[128,2560]{1,0:T(8,128)(2,1)S(1)} %fusion.60) | copy-start | bytes 1966084
  190.2 2.7 collective-permute-start
  193.6 5.6 collective-permute-start
  199.9 6.3 collective-permute-start
  206.8 6.3 collective-permute-start
  213.8 6.3 collective-permute-start
  220.7 6.3 collective-permute-start
  227.7 6.3 collective-permute-start
  317.1 1075.8 %copy-start = (f32[128,2560]{1,0:T(8,128)}, f32[128,2560]{1,0:T(8,128)S(1)}, u32[]{:S(2)}) copy-start(f32[128,2560]{1,0:T(8,128)S(1)} %get-tuple-element.1241) | copy-start | bytes 3932164
  1452.6 3.4 collective-permute-start.1
  1457.0 7.1 collective-permute-start.1
  1465.1 7.7 collective-permute-start.1
  1473.8 7.7 collective-permute-start.1
  1482.5 7.7 collective-permute-start.1
  1491.2 7.7 collective-permute-start.1
  1499.9 7.7 collective-permute-start.1
  1510.5 119.7 %all-gather.28.cloned.1.call-start = ((), (), s32[]{:S(2)}) async-start(), calls=%async_computation.10 | async-start | bytes 1179648 | tf_op jit(solution)/shard_map/all_gather | solution.py:332
  1511.4 398.4 %all-gather.30.cloned.1.call-start = ((), (), s32[]{:S(2)}) async-start(), calls=%async_computation.11 | async-start | bytes 35389440 | tf_op jit(solution)/shard_map/all_gather | solution.py:333
  1512.1 454.8 %all-gather.32.cloned.1.call-start = ((), (), s32[]{:S(2)}) async-start(), calls=%async_computation.12 | async-start | bytes 5898240 | tf_op jit(solution)/shard_map/all_gather | solution.py:334
  1512.9 596.3 %all-gather.34.cloned.1.call-start = ((), (), s32[]{:S(2)}) async-start(), calls=%async_computation.13 | async-start | bytes 17694720 | tf_op jit(solution)/shard_map/all_gather | solution.py:335
  1514.7 46.8 %all-to-all-start = ((bf16[128,8,320]{0,2,1:T(8,128)(2,1)}), bf16[128,8,320]{0,2,1:T(8,128)(2,1)S(1)}, u32[]{:S(2)}, u32[]{:S(2)}) async-start(bf16[128,8,320]{0,2,1:T(8,128)(2,1)} %bitcast.13), calls=%async_computation | async-start | bytes 1310720 | tf_op jit(solution)/shard_map/all_to_all | solution.py:301
  1561.5 36.4 %all-to-all-start.1 = ((bf16[128,8,320]{0,2,1:T(8,128)(2,1)}), bf16[128,8,320]{0,2,1:T(8,128)(2,1)}, u32[]{:S(2)}, u32[]{:S(2)}) async-start(bf16[128,8,320]{0,2,1:T(8,128)(2,1)} %bitcast.17), calls=%async_computation.1 | async-start | bytes 1310720 | tf_op jit(solution)/shard_map/all_to_all | solution.py:308
  1598.0 34.8 %all-to-all-start.2 = ((bf16[128,8,320]{0,2,1:T(8,128)(2,1)}), bf16[128,8,320]{0,2,1:T(8,128)(2,1)}, u32[]{:S(2)}, u32[]{:S(2)}) async-start(bf16[128,8,320]{0,2,1:T(8,128)(2,1)} %bitcast.273), calls=%async_computation.2 | async-start | bytes 1310720 | tf_op jit(solution)/shard_map/all_to_all | solution.py:315
  1602.2 635.1 %all-reduce.15.cloned.1.call-start = ((), (), s32[]{:S(2)}) async-start(), calls=%async_computation.15 | async-start | bytes 221184
  1632.8 340.5 %all-to-all-start.3 = ((bf16[128,8,320]{0,2,1:T(8,128)(2,1)}), bf16[128,8,320]{0,2,1:T(8,128)(2,1)S(1)}, u32[]{:S(2)}, u32[]{:S(2)}) async-start(bf16[128,8,320]{0,2,1:T(8,128)(2,1)} %bitcast.25), calls=%async_computation.3 | async-start | bytes 1310720 | tf_op jit(solution)/shard_map/all_to_all | solution.py:322
  1636.3 1233.0 %all-reduce.13.cloned.1.call-start = ((), (), s32[]{:S(2)}) async-start(), calls=%async_computation.14 | async-start | bytes 73400320
  (21 other events, 298.9 us)
Sparse Core Ops, SparseCore 0:
  9.9 42.6 all-gather.15
  54.4 126.8 all-gather.17
  183.1 126.8 all-gather.19
  311.8 672.9 all-gather.21
  986.5 345.9 all-gather.23
  1510.6 89.2 all-gather.25
  1602.1 28.0 all-gather.27
  1631.8 277.9 all-gather.29
  1912.0 54.9 all-gather.31
  1968.4 140.6 all-gather.33
  2116.2 121.0 all-reduce.14
  2240.7 628.6 all-reduce.12
where the time goes:
time: 2900 us; the launch traced here: 2890 us
  waiting for transfers between devices  2420 us (83%)
  matrix products  246 us (8%)
  local copies, waits for them, and re-layouts  69.7 us (2%)
  starting transfers between devices  62.9 us (2%)
  blocking collectives  41.7 us (1%)
  other arithmetic  35.2 us (1%)
    unnamed x14, waiting for transfers between devices  719 us
    all_gather x1, waiting for transfers between devices, body(): lax.all_gather(gate_up_weight, 'shard', axis=0, tiled=True)  667 us
    all_gather x1, waiting for transfers between devices, body(): lax.all_gather(down_weight, 'shard', axis=0, tiled=True)  308 us
    all_gather x1, waiting for transfers between devices, body(): lax.all_gather(gate_up_low, 'context', axis=0, tiled=True)  273 us
    all_gather x1, waiting for transfers between devices, body(): lax.all_gather(hidden, 'context', axis=0, tiled=True)  136 us
    all_gather x1, waiting for transfers between devices, body(): lax.all_gather(query_weight, 'shard', axis=0, tiled=True)  125 us
    dot_general x5, matrix products, against(): lax.dot_general(left, weight, (((1,), (1,)), ((), ())), preferred_element...  76.9 us
  transfers between devices with their start and end apart: 30, of which 27 were waited for; matrix products, arithmetic and copies ran while one was open for 7% of the time, Pallas kernels for 0%

commit v1 on v0

v1 whole, which is shorter than its diff:
```python
import math

import jax
import jax.numpy as jnp
from jax import lax
from jax.experimental import pallas as pl
from jax.experimental.pallas import tpu as pltpu
from jax.sharding import PartitionSpec as P

HEADS = 10
DH = 256
FF = 7680
WINDOW = 2048


EPS = 1e-06
NEG = -1e30
ROPE_LOG = math.log(10000.0)


def frequencies(head_dim):
    quarter = head_dim // 4
    steps = jnp.arange(quarter).astype(jnp.float32)
    return jnp.exp(-ROPE_LOG * (2.0 * steps) / (head_dim // 2))


def rotate(field, cosine, sine):
    width = field.shape[-1] // 2
    quarter = width // 2
    first = field[..., :quarter]
    second = field[..., quarter:width]
    return jnp.concatenate(
        [first * cosine - second * sine, second * cosine + first * sine, field[..., width:]],
        axis=-1,
    )


def rms_norm(field, gain):
    return field * lax.rsqrt(jnp.mean(field * field, axis=-1, keepdims=True) + EPS) * gain


def geglu(gate_up):
    half = gate_up.shape[-1] // 2
    return jax.nn.gelu(gate_up[:, :half], approximate=True) * gate_up[:, half:]


def over_rows(left, right):
    return lax.dot_general(
        left, right, (((0,), (0,)), ((), ())), preferred_element_type=jnp.float32
    )


def against(left, weight):
    return lax.dot_general(
        left, weight, (((1,), (1,)), ((), ())), preferred_element_type=jnp.float32
    )


def regroup(field, shard_count, context_count):
    rows_now, width = field.shape
    owned = width // (shard_count * context_count)
    return (
        field.reshape(rows_now, shard_count, context_count, owned)
        .transpose(0, 2, 1, 3)
        .reshape(rows_now, width)
    )


VMEM_LIMIT = 56 * 1024 * 1024
LANES = 128


def gather(value, axis):
    return lax.all_gather(value, axis, axis=0, tiled=True)


def sibling(value):
    count = lax.axis_size("context")
    return lax.ppermute(value, "context", [(i, i ^ 1) for i in range(count)])


def pair_rows(own, core):
    other = sibling(own)
    return jnp.where(
        core == 0, jnp.concatenate([own, other], axis=0), jnp.concatenate([other, own], axis=0)
    )


def halves(value, core, axis):
    low, high = jnp.split(value, 2, axis=axis)
    return jnp.where(core == 0, low, high), jnp.where(core == 0, high, low)


def swap_rows(value, core):
    mine, theirs = halves(value, core, 0)
    other = sibling(theirs)
    return jnp.where(
        core == 0, jnp.concatenate([mine, other], axis=1), jnp.concatenate([other, mine], axis=1)
    )


def swap_columns(own, core):
    mine, theirs = halves(own, core, 1)
    other = sibling(theirs)
    return jnp.where(
        core == 0, jnp.concatenate([mine, other], axis=0), jnp.concatenate([other, mine], axis=0)
    )


def summed_half(value, core, axis):
    mine, theirs = halves(value, core, axis)
    return mine + sibling(theirs)


def unit_tiles(ff, shards, contexts):
    per_shard = ff // shards // LANES
    return -(-per_shard // contexts), per_shard


def take_units_kernel(start_ref, weight_ref, out_ref):
    out_ref[...] = weight_ref[...]


def take_units(weight, start_tile, shards, width, per_shard):
    rows = weight.shape[0]

    def source(i, start):
        part, rest = i // (shards * width), i % (shards * width)
        return 0, part * shards * per_shard + (rest // width) * per_shard + start[0] + rest % width

    return pl.pallas_call(
        take_units_kernel,
        grid_spec=pltpu.PrefetchScalarGridSpec(
            num_scalar_prefetch=1,
            grid=(2 * shards * width,),
            in_specs=[pl.BlockSpec((rows, LANES), source)],
            out_specs=pl.BlockSpec((rows, LANES), lambda i, start: (0, i)),
        ),
        out_shape=jax.ShapeDtypeStruct((rows, 2 * shards * width * LANES), weight.dtype),
    )(start_tile.reshape(1), weight)


def join_units(pieces, parts, shards, width, per_shard):
    contexts, inner = pieces.shape[0], pieces.shape[1:-1]
    field = pieces.reshape(contexts, *inner, parts, shards, width * LANES)
    kept = []
    for at in range(contexts):
        first = at * width
        if first >= per_shard:
            continue
        start = min(first, per_shard - width)
        stop = min(first + width, per_shard)
        kept.append(field[at, ..., (first - start) * LANES : (stop - start) * LANES])
    return jnp.concatenate(kept, axis=-1).reshape(*inner, parts * shards * per_shard * LANES)


def masked_weights(q, k, mask):
    scores = lax.dot_general(q, k, (((1,), (1,)), ((), ())), preferred_element_type=jnp.float32)
    scores = jnp.where(mask > 0.0, scores, NEG)
    raised = jnp.exp(scores - jnp.max(scores, axis=1, keepdims=True))
    return raised / jnp.sum(raised, axis=1, keepdims=True)


def mix_kernel(mask_ref, q_ref, k_ref, v_ref, out_ref):
    weights = masked_weights(q_ref[...], k_ref[...], mask_ref[...])
    out_ref[...] = jnp.dot(
        weights.astype(jnp.bfloat16), v_ref[...], preferred_element_type=jnp.float32
    ).astype(jnp.bfloat16)


def mix(mask, queries, keys, values):
    rows, width = queries.shape
    slots = keys.shape[0]
    whole = lambda h: (0, 0)
    part = lambda h: (0, h)
    return pl.pallas_call(
        mix_kernel,
        grid=(width // DH,),
        in_specs=[
            pl.BlockSpec((rows, slots), whole),
            pl.BlockSpec((rows, DH), part),
            pl.BlockSpec((slots, DH), whole),
            pl.BlockSpec((slots, DH), whole),
        ],
        out_specs=pl.BlockSpec((rows, DH), part),
        out_shape=jax.ShapeDtypeStruct((rows, width), jnp.bfloat16),
        compiler_params=pltpu.CompilerParams(vmem_limit_bytes=VMEM_LIMIT),
    )(mask, queries, keys, values)


def mix_back_kernel(mask_ref, q_ref, k_ref, v_ref, g_ref, dq_ref, dk_ref, dv_ref):
    q, k, g = q_ref[...], k_ref[...], g_ref[...]
    weights = masked_weights(q, k, mask_ref[...])
    value_score = against(g, v_ref[...])
    delta = jnp.sum(weights * value_score, axis=1, keepdims=True)
    score_back = (weights * (value_score - delta)).astype(jnp.bfloat16)
    dq_ref[...] = jnp.dot(score_back, k, preferred_element_type=jnp.float32)
    key_piece = over_rows(score_back, q)
    value_piece = over_rows(weights.astype(jnp.bfloat16), g)

    @pl.when(pl.program_id(0) == 0)
    def _():
        dk_ref[...] = key_piece
        dv_ref[...] = value_piece

    @pl.when(pl.program_id(0) > 0)
    def _():
        dk_ref[...] += key_piece
        dv_ref[...] += value_piece


def mix_back(mask, queries, keys, values, grad):
    rows, width = queries.shape
    slots = keys.shape[0]
    whole = lambda h: (0, 0)
    part = lambda h: (0, h)
    return pl.pallas_call(
        mix_back_kernel,
        grid=(width // DH,),
        in_specs=[
            pl.BlockSpec((rows, slots), whole),
            pl.BlockSpec((rows, DH), part),
            pl.BlockSpec((slots, DH), whole),
            pl.BlockSpec((slots, DH), whole),
            pl.BlockSpec((rows, DH), part),
        ],
        out_specs=[
            pl.BlockSpec((rows, DH), part),
            pl.BlockSpec((slots, DH), whole),
            pl.BlockSpec((slots, DH), whole),
        ],
        out_shape=[
            jax.ShapeDtypeStruct((rows, width), jnp.float32),
            jax.ShapeDtypeStruct((slots, DH), jnp.float32),
            jax.ShapeDtypeStruct((slots, DH), jnp.float32),
        ],
        compiler_params=pltpu.CompilerParams(vmem_limit_bytes=VMEM_LIMIT),
    )(mask, queries, keys, values, grad)


def body(
    inputs,
    doc_ids,
    cotangent,
    attn_gain,
    query_weight,
    keyval_weight,
    output_weight,
    output_bias,
    feed_gain,
    gate_up_weight,
    gate_up_bias,
    down_weight,
    down_bias,
):
    tok, model = inputs.shape
    shards, contexts = lax.axis_size("shard"), lax.axis_size("context")
    shard, place = lax.axis_index("shard"), lax.axis_index("context")
    core, chip = place % 2, place // 2
    group = tok * contexts
    owned = model // (shards * contexts)
    ff = gate_up_weight.shape[1] // 2
    width, per_shard = unit_tiles(ff, shards, contexts)
    unit_start = jnp.minimum(place * width, per_shard - width)
    units = shards * width * LANES

    vectors = jnp.concatenate([attn_gain, output_bias, feed_gain, down_bias, gate_up_bias])
    vectors = gather(vectors[None], "shard").astype(jnp.float32)
    gain_one, bias_out, gain_two, bias_down = (
        vectors[:, i * (model // shards) : (i + 1) * (model // shards)].reshape(1, model)
        for i in range(4)
    )
    bias_gate_up = vectors[:, 4 * (model // shards) :].reshape(2 * shards, per_shard * LANES)
    bias_gate_up = lax.dynamic_slice_in_dim(
        bias_gate_up, unit_start * LANES, width * LANES, 1
    ).reshape(1, 2 * units)
    keyval_half = gather(halves(keyval_weight, core, 1)[0], "shard")
    query_half = gather(halves(query_weight, core, 1)[0], "shard")
    output_half = gather(halves(output_weight, core, 1)[0], "shard")
    gate_up_part = gather(
        take_units(gate_up_weight, unit_start, shards, width, per_shard), "shard"
    )
    down_part = gather(
        lax.dynamic_slice_in_dim(down_weight, unit_start * LANES, width * LANES, 0), "shard"
    )
    unit_at = unit_start * LANES + jnp.arange(width * LANES, dtype=jnp.int32)
    unit_live = jnp.tile(unit_at >= place * width * LANES, shards)[None, :]

    source = inputs.astype(jnp.float32)
    attn_in = rms_norm(source, gain_one).astype(jnp.bfloat16)
    attn_pair = pair_rows(attn_in, core)
    slots = jnp.arange(group, dtype=jnp.int32)
    pair_slots = chip * (2 * tok) + jnp.arange(2 * tok, dtype=jnp.int32)
    pair_docs = lax.dynamic_slice_in_dim(doc_ids, chip * (2 * tok), 2 * tok)
    distance = pair_slots[:, None] - slots[None, :]
    mask = (
        (pair_docs[:, None] == doc_ids[None, :]) & (distance >= 0) & (distance < WINDOW)
    ).astype(jnp.float32)
    angles = pair_slots.astype(jnp.float32)[:, None] * frequencies(DH)[None, :]
    cosine, sine = jnp.cos(angles), jnp.sin(angles)
    keyval_raw = jnp.dot(attn_pair, keyval_half, preferred_element_type=jnp.float32)
    keyval = jnp.where(core == 0, rotate(keyval_raw, cosine, sine), keyval_raw).astype(jnp.bfloat16)
    keyval = gather(keyval, "context").reshape(contexts // 2, 2, 2 * tok, DH)
    keys, values = keyval[:, 0].reshape(group, DH), keyval[:, 1].reshape(group, DH)
    query_raw = jnp.dot(attn_pair, query_half, preferred_element_type=jnp.float32)
    heads = query_raw.shape[1] // DH
    queries = (
        (
            rotate(query_raw.reshape(2 * tok, heads, DH), cosine[:, None, :], sine[:, None, :])
            * DH ** (-0.5)
        )
        .astype(jnp.bfloat16)
        .reshape(2 * tok, heads * DH)
    )
    mixed_half = mix(mask, queries, keys, values)
    mixed_own = swap_rows(mixed_half, core)
    mixed_pair = pair_rows(mixed_own, core)
    attn_out = swap_rows(
        jnp.dot(mixed_pair, output_half, preferred_element_type=jnp.float32), core
    )
    resid = source + attn_out + bias_out

    feed_in = rms_norm(resid, gain_two).astype(jnp.bfloat16)
    grad_group = gather(cotangent, "context")
    feed_group = gather(feed_in, "context")
    gate_up = jnp.dot(feed_group, gate_up_part, preferred_element_type=jnp.float32) + bias_gate_up
    hidden_grad = against(grad_group, down_part)

    def live_geglu(field):
        return jnp.where(unit_live, geglu(field), 0.0)

    hidden, geglu_pull = jax.vjp(live_geglu, gate_up)
    hidden = hidden.astype(jnp.bfloat16)
    gate_up_low = geglu_pull(hidden_grad)[0].astype(jnp.bfloat16)
    feed_part = against(gate_up_low, gate_up_part).astype(jnp.bfloat16)
    feed_in_grad = lax.psum_scatter(
        feed_part, "context", scatter_dimension=0, tiled=True
    ).astype(jnp.float32)
    down_out = lax.psum_scatter(
        jnp.dot(hidden, down_part, preferred_element_type=jnp.float32).astype(jnp.bfloat16),
        "context",
        scatter_dimension=0,
        tiled=True,
    ).astype(jnp.float32)
    block_out = (resid + down_out + bias_down).astype(jnp.bfloat16)

    grad_out = cotangent.astype(jnp.float32)
    resid_part, gain_two_grad = jax.vjp(rms_norm, resid, gain_two)[1](feed_in_grad)
    resid_grad = grad_out + resid_part
    attn_grad_low = resid_grad.astype(jnp.bfloat16)
    mixed_back = summed_half(
        against(swap_columns(attn_grad_low, core), output_half), core, 1
    ).astype(jnp.bfloat16)
    query_acc, key_acc, value_acc = mix_back(mask, queries, keys, values, mixed_back)
    keyval_acc = jnp.stack(
        [key_acc.reshape(contexts // 2, 2 * tok, DH), value_acc.reshape(contexts // 2, 2 * tok, DH)],
        axis=1,
    ).reshape(2 * group, DH)
    keyval_acc = lax.psum_scatter(keyval_acc, "context", scatter_dimension=0, tiled=True)
    keyval_back = jnp.where(core == 0, rotate(keyval_acc, cosine, -sine), keyval_acc).astype(
        jnp.bfloat16
    )
    query_back = (
        rotate(query_acc.reshape(2 * tok, heads, DH), cosine[:, None, :], -sine[:, None, :])
        * DH ** (-0.5)
    ).reshape(2 * tok, heads * DH).astype(jnp.bfloat16)
    attn_in_grad = summed_half(
        against(query_back, query_half) + against(keyval_back, keyval_half), core, 0
    )
    input_part, gain_one_grad = jax.vjp(rms_norm, source, gain_one)[1](attn_in_grad)
    input_grad = resid_grad + input_part

    gate_up_sum = lax.psum_scatter(
        over_rows(feed_group, gate_up_low).astype(jnp.bfloat16),
        "shard",
        scatter_dimension=0,
        tiled=True,
    )
    down_sum = lax.psum_scatter(
        over_rows(grad_group, hidden).astype(jnp.bfloat16),
        "shard",
        scatter_dimension=0,
        tiled=True,
    )

    def to_owners(field):
        return lax.all_to_all(
            field.reshape(contexts, owned, field.shape[1]), "context", split_axis=0, concat_axis=0
        ).astype(jnp.float32)

    gate_up_grad = join_units(to_owners(gate_up_sum), 2, shards, width, per_shard)
    down_weight_grad = join_units(to_owners(down_sum), 1, shards, width, per_shard).T

    def token_rows(field):
        return lax.all_to_all(
            regroup(field, shards, contexts), "context", split_axis=1, concat_axis=0, tiled=True
        )

    back_own = jnp.concatenate(
        [swap_rows(query_back, core), swap_rows(keyval_back, core)], axis=1
    )
    back_group = gather(back_own, "context")
    mixed_group = gather(mixed_own, "context")
    attn_sum = lax.psum_scatter(
        jnp.concatenate(
            [
                over_rows(token_rows(attn_in), back_group),
                over_rows(token_rows(attn_grad_low), mixed_group),
            ],
            axis=1,
        ).astype(jnp.bfloat16),
        "shard",
        scatter_dimension=0,
        tiled=True,
    ).astype(jnp.float32)
    head_cols = HEADS * DH
    query_grad = attn_sum[:, :head_cols]
    keyval_grad = attn_sum[:, head_cols : head_cols + 2 * DH]
    output_weight_grad = attn_sum[:, head_cols + 2 * DH :].T

    sums = jnp.concatenate(
        [
            gain_one_grad.reshape(model),
            jnp.sum(attn_grad_low.astype(jnp.float32), axis=0),
            gain_two_grad.reshape(model),
            jnp.sum(grad_out, axis=0),
            jnp.sum(gate_up_low.astype(jnp.float32), axis=0),
        ]
    )
    sums = lax.all_gather(sums, ("shard", "context"), axis=0, tiled=False)
    device = shard * contexts + place
    own = [
        jnp.sum(
            lax.dynamic_slice_in_dim(sums[:, i * model : (i + 1) * model], device * owned, owned, 1),
            axis=0,
        )
        for i in range(4)
    ]
    unit_sums = jnp.sum(sums[:, 4 * model :].reshape(shards, contexts, 2 * units), axis=0)
    unit_sums = join_units(unit_sums, 2, shards, width, per_shard)
    unit_owned = 2 * ff // (shards * contexts)
    gate_up_bias_grad = lax.dynamic_slice_in_dim(unit_sums, device * unit_owned, unit_owned)
    return (
        block_out,
        input_grad,
        own[0],
        query_grad,
        keyval_grad,
        output_weight_grad,
        own[1],
        own[2],
        gate_up_grad,
        gate_up_bias_grad,
        down_weight_grad,
        own[3],
    )


def solution(mesh):
    placed = (
        P(("shard", "context"), None),
        P("shard"),
        P(("shard", "context"), None),
        P("shard"),
        P("shard", None),
        P("shard", None),
        P("shard", None),
        P("shard"),
        P("shard"),
        P("shard", None),
        P("shard"),
        P("shard", None),
        P("shard"),
    )
    return jax.shard_map(
        body,
        mesh=mesh,
        in_specs=placed,
        out_specs=(
            P(("shard", "context"), None),
            P(("shard", "context"), None),
            P(("shard", "context")),
            P(("shard", "context"), None),
            P(("shard", "context"), None),
            P(None, ("shard", "context")),
            P(("shard", "context")),
            P(("shard", "context")),
            P(("shard", "context"), None),
            P(("shard", "context")),
            P(None, ("shard", "context")),
            P(("shard", "context")),
        ),
        check_vma=False,
    )
```

time: 2900 us -> 1250 us (0.43)
  waiting for transfers between devices: 2420 us -> 807 us
  matrix products: 246 us -> 119 us
  local copies, waits for them, and re-layouts: 69.7 us -> 157 us
  starting transfers between devices: 62.9 us -> 23.2 us
  other arithmetic: 35.2 us -> 73.4 us
  blocking collectives: 41.7 us -> 9.9 us
    all_gather x10 -> x11, waiting for transfers between devices: 1600 us -> 566 us  [the longest x10 520 us: gather(): return lax.all_gather(value, axis, axis=0, tiled=True)]
    unnamed x14 -> x17, waiting for transfers between devices: 719 us -> 1.46 us
    reduce_scatter x0 -> x6, waiting for transfers between devices: none -> 227 us  [the longest x1 97.1 us: body(): lax.psum_scatter(over_rows(feed_group, gate_up_low).astype(jnp.bfloat16),...]
    dot_general x77 -> x5, matrix products: 121 us -> 37.8 us  [the longest x1 15.2 us: body(): jnp.dot(feed_group, gate_up_part, preferred_element_type=jnp.float32)]
    all_to_all x4, waiting for transfers between devices: 54.5 us -> 2.3 us  [the longest x2 2.29 us: token_rows(): lax.all_to_all(regroup(field, shards, contexts), 'context', split_axis=1,...]
    ppermute x14 -> x9, starting transfers between devices: 41.9 us -> 2.24 us  [sibling(): return lax.ppermute(value, 'context', [(i, i ^ 1) for i in range(count)])]
    ppermute x14 -> x9, waiting for transfers between devices: 46.5 us -> 10.1 us  [sibling(): return lax.ppermute(value, 'context', [(i, i ^ 1) for i in range(count)])]
    dot_general x5, matrix products: 76.9 us -> 43.3 us  [against(): lax.dot_general(left, weight, (((1,), (1,)), ((), ())), preferred_element...]
  transfers between devices with their start and end apart: 30 -> 30, of which waited for: 27 -> 22; matrix products, arithmetic and copies ran while one was open for 7% -> 20% of each run, Pallas kernels for 0% -> 1%
where the time goes in v1:
time: 1250 us; the launch traced here: 1230 us
  waiting for transfers between devices  807 us (65%)
  local copies, waits for them, and re-layouts  157 us (13%)
  matrix products  119 us (10%)
  other arithmetic  73.4 us (6%)
  Pallas kernels  28.5 us (2%)
  starting transfers between devices  23.2 us (2%)
  between operations  15.4 us (1%)
    all_gather x10, waiting for transfers between devices, gather(): return lax.all_gather(value, axis, axis=0, tiled=True)  520 us
    reduce_scatter x1, waiting for transfers between devices, body(): lax.psum_scatter(over_rows(feed_group, gate_up_low).astype(jnp.bfloat16),...  97.1 us
    reduce_scatter x1, waiting for transfers between devices, body(): lax.psum_scatter(feed_part, 'context', scatter_dimension=0, tiled=True)  58.8 us
    reduce_scatter x1, waiting for transfers between devices, body(): lax.psum_scatter(over_rows(grad_group, hidden).astype(jnp.bfloat16), 'sha...  58.5 us
    all_gather x1, waiting for transfers between devices, body(): sums = lax.all_gather(sums, ('shard', 'context'), axis=0, tiled=False)  46 us
    dot_general x5, matrix products, against(): lax.dot_general(left, weight, (((1,), (1,)), ((), ())), preferred_element...  43.3 us
    unnamed x112, local copies, waits for them, and re-layouts  38.3 us
    dot_general x4, matrix products, over_rows(): lax.dot_general(left, right, (((0,), (0,)), ((), ())), preferred_element_...  38.1 us
  transfers between devices with their start and end apart: 30, of which 22 were waited for; matrix products, arithmetic and copies ran while one was open for 20% of the time, Pallas kernels for 1%

profile of v1, /device:TPU:0, one launch (start us, length us, event | category | flops | bytes accessed | tf_op | source)
XLA Modules:
  0.0 1234.0 jit_solution(372755954092483633)
XLA Ops:
  13.5 9.9 all-gather.2
  28.5 13.7 %all-gather.17.cloned.1.call-done = bf16[2560,256]{1,0:T(8,128)(2,1)} async-done(((bf16[640,256]{1,0:T(8,128)(2,1)}), bf16[2560,256]{1,0:T(8,128)(2,1)}) %all-gather.17.cloned.1.call-update) | async-done | bytes 1310736 | tf_op jit(solution)/shard_map/all_gather | solution.py:74
  52.2 9.7 shard_map.221
  70.0 72.2 %all-gather.15.cloned.1.call-done = bf16[2560,1280]{1,0:T(8,128)(2,1)} async-done(((bf16[640,1280]{1,0:T(8,128)(2,1)}), bf16[2560,1280]{1,0:T(8,128)(2,1)}) %all-gather.15.cloned.1.call-update) | async-done | bytes 6553616 | tf_op jit(solution)/shard_map/all_gather | solution.py:74
  142.2 5.6 fusion.47
  149.1 7.9 shard_map.220
  160.1 56.1 %all-gather.21.cloned.1.call-done = bf16[2560,1280]{1,0:T(8,128)(2,1)} async-done(((bf16[640,1280]{1,0:T(8,128)(2,1)}), bf16[2560,1280]{1,0:T(8,128)(2,1)}) %all-gather.21.cloned.1.call-update) | async-done | bytes 6553616 | tf_op jit(solution)/shard_map/all_gather | solution.py:74
  228.6 95.0 %all-gather.25.cloned.1.call-done = bf16[2560,2048]{1,0:T(8,128)(2,1)} async-done(((bf16[640,2048]{1,0:T(8,128)(2,1)}), bf16[2560,2048]{1,0:T(8,128)(2,1)}) %all-gather.25.cloned.1.call-update) | async-done | bytes 10485776 | tf_op jit(solution)/shard_map/all_gather | solution.py:74
  323.6 58.1 %all-gather.23.cloned.1.call-done = bf16[1024,2560]{1,0:T(8,128)(2,1)} async-done(((bf16[128,2560]{1,0:T(8,128)(2,1)}), bf16[1024,2560]{1,0:T(8,128)(2,1)}) %all-gather.23.cloned.1.call-update) | async-done | bytes 5242896 | tf_op jit(solution)/shard_map/all_gather | solution.py:74
  381.7 15.2 %broadcast_add_fusion = f32[1024,2048]{1,0:T(8,128)S(1)} fusion(f32[2048]{0:T(1024)S(1)} %bitcast.124, bf16[1024,2560]{1,0:T(8,128)(2,1)} %all-gather.23.cloned.1.call-done, bf16[2560,2048]{1,0:T(8,128)(2,1)} %all-gather.25.cloned.1.call-done), kind=kOutput, calls=%fused_computation.20 | convolution fusion | flops 10739515392 | bytes 24125440 | tf_op jit(solution)/shard_map/dot_general | solution.py:326
  408.1 7.3 multiply_multiply_fusion.3
  426.1 18.2 %all-gather.27.cloned.1.call-done = bf16[1024,2560]{1,0:T(8,128)(2,1)} async-done(((bf16[256,2560]{1,0:T(8,128)(2,1)}), bf16[1024,2560]{1,0:T(8,128)(2,1)}) %all-gather.27.cloned.1.call-update) | async-done | bytes 5242896 | tf_op jit(solution)/shard_map/all_gather | solution.py:74
  444.4 57.7 %all-gather.29.cloned.1.call-done = bf16[1024,2560]{1,0:T(8,128)(2,1)} async-done(((bf16[128,2560]{1,0:T(8,128)(2,1)}), bf16[1024,2560]{1,0:T(8,128)(2,1)}) %all-gather.29.cloned.1.call-update) | async-done | bytes 5242896 | tf_op jit(solution)/shard_map/all_gather | solution.py:74
  502.1 16.5 %multiply_multiply_fusion.2 = (f32[1024,1024]{1,0:T(8,128)}, f32[1024,1024]{1,0:T(8,128)}, f32[1024,1024]{1,0:T(8,128)}, f32[1024,1024]{1,0:T(8,128)}) fusion(f32[1024,1024]{1,0:T(8,128)} %copy.163, f32[1024,2048]{1,0:T(8,128)} %copy-done.5, pred[1024]{0:T(1024)(128)(4,1)S(1)} %broadcast_in_dim.25, f32[1024,1024]{1,0:T(8,128)} %copy.159, ...), kind=kOutput, calls=%fused_computation.18 | convolution fusion | flops 5375000576 | bytes 44041216 | tf_op jit(solution)/shard_map/dot_general | solution.py:54
  534.8 9.0 multiply_add_fusion.1
  549.1 5.8 copy.165
  554.9 8.8 multiply_add_fusion
  563.7 16.6 %convolution_convert_fusion.2 = bf16[1024,2560]{1,0:T(8,128)(2,1)} fusion(bf16[2560,2048]{1,0:T(8,128)(2,1)} %all-gather.25.cloned.1.call-done, f32[1024,1024]{1,0:T(8,128)} %multiply_add_fusion, f32[1024,1024]{1,0:T(8,128)S(1)} %copy-done.1), kind=kOutput, calls=%fused_computation.6 | convolution fusion | flops 10744233984 | bytes 24117248 | tf_op jit(solution)/shard_map/dot_general | solution.py:54
  580.4 58.8 %reduce-scatter.11.cloned.1.call-done = bf16[128,2560]{1,0:T(8,128)(2,1)} async-done(((bf16[1024,2560]{1,0:T(8,128)(2,1)}), bf16[128,2560]{1,0:T(8,128)(2,1)}) %reduce-scatter.11.cloned.1.call-update) | async-done | bytes 655376 | tf_op jit(solution)/shard_map/reduce_scatter | solution.py:336
  653.2 11.0 shard_map.222
  667.3 10.4 convolution_convert_fusion.3
  678.3 10.2 fusion
  688.5 8.0 copy.184
  713.3 18.2 %convolution_convert_fusion = bf16[2560,2048]{1,0:T(8,128)(2,1)} fusion(bf16[1024,2560]{1,0:T(8,128)(2,1)} %all-gather.23.cloned.1.call-done, f32[1024,1024]{1,0:T(8,128)} %multiply_add_fusion, f32[1024,1024]{1,0:T(8,128)} %get-tuple-element.37), kind=kOutput, calls=%fused_computation | convolution fusion | flops 10746855424 | bytes 24117248 | tf_op jit(solution)/shard_map/dot_general | solution.py:48
  756.0 10.0 reduce-scatter.9.cloned.1.call-done
  775.0 6.6 all-to-all-start
  781.6 60.9 %all-gather.33.cloned.1.call-done = bf16[1024,2560]{1,0:T(8,128)(2,1)} async-done(((bf16[128,2560]{1,0:T(8,128)(2,1)}), bf16[1024,2560]{1,0:T(8,128)(2,1)}) %all-gather.33.cloned.1.call-update) | async-done | bytes 5242896 | tf_op jit(solution)/shard_map/all_gather | solution.py:74
  847.0 58.5 %reduce-scatter.19.cloned.1.call-done = bf16[640,1024]{1,0:T(8,128)(2,1)} async-done(((bf16[2560,1024]{1,0:T(8,128)(2,1)}), bf16[640,1024]{1,0:T(8,128)(2,1)}) %reduce-scatter.19.cloned.1.call-update) | async-done | bytes 1310736 | tf_op jit(solution)/shard_map/reduce_scatter | solution.py:379
  910.2 84.4 %all-gather.31.cloned.1.call-done = bf16[1024,3072]{1,0:T(8,128)(2,1)} async-done(((bf16[128,3072]{1,0:T(8,128)(2,1)}), bf16[1024,3072]{1,0:T(8,128)(2,1)}) %all-gather.31.cloned.1.call-update) | async-done | bytes 6291472 | tf_op jit(solution)/shard_map/all_gather | solution.py:74
  1001.8 97.1 %reduce-scatter.17.cloned.1.call-done = bf16[640,2048]{1,0:T(8,128)(2,1)} async-done(((bf16[2560,2048]{1,0:T(8,128)(2,1)}), bf16[640,2048]{1,0:T(8,128)(2,1)}) %reduce-scatter.17.cloned.1.call-update) | async-done | bytes 2621456 | tf_op jit(solution)/shard_map/reduce_scatter | solution.py:373
  1127.2 46.0 %all-gather.35.cloned.1.call-done = f32[393216]{0:T(1024)} async-done(((f32[12288]{0:T(1024)}), f32[393216]{0:T(1024)}) %all-gather.35.cloned.1.call-update) | async-done | bytes 1572880 | tf_op jit(solution)/shard_map/all_gather | solution.py:430
  1213.7 6.5 reshape.287
  (303 shorter events, 248.9 us)
Async XLA Ops:
  7.2 35.0 %all-gather.17.cloned.1.call-start = ((), (), s32[]{:S(2)}) async-start(), calls=%async_computation.11 | async-start | bytes 1638400 | tf_op jit(solution)/shard_map/all_gather | solution.py:74
  9.2 58.6 %all-gather.19.cloned.1.call-start = ((), (), s32[]{:S(2)}) async-start(), calls=%async_computation.12 | async-start | bytes 1179648 | tf_op jit(solution)/shard_map/all_gather | solution.py:74
  26.3 115.9 %copy-start.9 = (bf16[128,2560]{1,0:T(8,128)(2,1)}, bf16[128,2560]{1,0:T(8,128)(2,1)S(1)}, u32[]{:S(2)}) copy-start(bf16[128,2560]{1,0:T(8,128)(2,1)S(1)} %fusion.9) | copy-start | bytes 1966084
  26.3 2.2 collective-permute-start
  45.5 96.7 %all-gather.15.cloned.1.call-start = ((), (), s32[]{:S(2)}) async-start(), calls=%async_computation.10 | async-start | bytes 8192000 | tf_op jit(solution)/shard_map/all_gather | solution.py:74
  48.8 167.4 %all-gather.21.cloned.1.call-start = ((), (), s32[]{:S(2)}) async-start(), calls=%async_computation.13 | async-start | bytes 8192000 | tf_op jit(solution)/shard_map/all_gather | solution.py:74
  52.2 271.4 %all-gather.25.cloned.1.call-start = ((), (), s32[]{:S(2)}) async-start(), calls=%async_computation.15 | async-start | bytes 13107200 | tf_op jit(solution)/shard_map/all_gather | solution.py:74
  61.9 319.8 %all-gather.23.cloned.1.call-start = ((), (), s32[]{:S(2)}) async-start(), calls=%async_computation.14 | async-start | bytes 5898240 | tf_op jit(solution)/shard_map/all_gather | solution.py:74
  158.1 1.7 collective-permute-start.1
  159.9 56.3 %collective-permute-start.2 = (bf16[128,2560]{1,0:T(8,128)(2,1)S(1)}, bf16[128,2560]{1,0:T(8,128)(2,1)S(1)}, u32[]{:S(2)}, u32[]{:S(2)}) collective-permute-start(bf16[128,2560]{1,0:T(8,128)(2,1)S(1)} %maximum_select_fusion.4), channel_id=1, source_target_pairs={{0,1},{1,0},{2,3},{3,2},{4,5},{5,4},{6,7},{7,6},{8,9},{9,8},{10,11... | collective-permute-start | bytes 1966088 | tf_op jit(solution)/shard_map/ppermute | solution.py:79
  221.1 2.2 collective-permute-start.3
  224.7 219.7 %all-gather.27.cloned.1.call-start = ((), (), s32[]{:S(2)}) async-start(), calls=%async_computation.16 | async-start | bytes 6553600 | tf_op jit(solution)/shard_map/all_gather | solution.py:74
  227.5 274.6 %all-gather.29.cloned.1.call-start = ((), (), s32[]{:S(2)}) async-start(), calls=%async_computation.18 | async-start | bytes 5898240 | tf_op jit(solution)/shard_map/all_gather | solution.py:74
  228.2 411.0 %reduce-scatter.11.cloned.1.call-start = ((), (), s32[]{:S(2)}) async-start(), calls=%async_computation.19 | async-start | bytes 5898240 | tf_op jit(solution)/shard_map/reduce_scatter | solution.py:336
  580.4 126.4 %reduce-scatter.13.cloned.1.call-start = ((), (), s32[]{:S(2)}) async-start(), calls=%async_computation.20 | async-start | bytes 2359296 | tf_op jit(solution)/shard_map/reduce_scatter | solution.py:359
  642.5 1.7 collective-permute-start.4
  649.1 3.1 collective-permute-start.5
  667.2 98.8 %reduce-scatter.9.cloned.1.call-start = ((), (), s32[]{:S(2)}) async-start(), calls=%async_computation.17 | async-start | bytes 5898240 | tf_op jit(solution)/shard_map/reduce_scatter | solution.py:339
  677.7 164.8 %all-gather.33.cloned.1.call-start = ((), (), s32[]{:S(2)}) async-start(), calls=%async_computation.22 | async-start | bytes 5898240 | tf_op jit(solution)/shard_map/all_gather | solution.py:74
  678.2 227.3 %reduce-scatter.19.cloned.1.call-start = ((), (), s32[]{:S(2)}) async-start(), calls=%async_computation.26 | async-start | bytes 6553600 | tf_op jit(solution)/shard_map/reduce_scatter | solution.py:379
  696.5 298.1 %all-gather.31.cloned.1.call-start = ((), (), s32[]{:S(2)}) async-start(), calls=%async_computation.21 | async-start | bytes 7077888 | tf_op jit(solution)/shard_map/all_gather | solution.py:74
  704.7 6.1 collective-permute-start.7
  709.4 2.8 collective-permute-start.8
  713.3 385.7 %reduce-scatter.17.cloned.1.call-start = ((), (), s32[]{:S(2)}) async-start(), calls=%async_computation.24 | async-start | bytes 13107200 | tf_op jit(solution)/shard_map/reduce_scatter | solution.py:373
  740.9 11.4 collective-permute-start.6
  748.0 27.0 %all-to-all-start.1 = ((bf16[128,8,320]{0,2,1:T(8,128)(2,1)}), bf16[128,8,320]{0,2,1:T(8,128)(2,1)}, u32[]{:S(2)}, u32[]{:S(2)}) async-start(bf16[128,8,320]{0,2,1:T(8,128)(2,1)} %bitcast.22), calls=%async_computation.4 | async-start | bytes 1310720 | tf_op jit(solution)/shard_map/all_to_all | solution.py:395
  752.3 420.9 %all-gather.35.cloned.1.call-start = ((), (), s32[]{:S(2)}) async-start(), calls=%async_computation.25 | async-start | bytes 1622016 | tf_op jit(solution)/shard_map/all_gather | solution.py:430
  775.0 72.0 %all-to-all-start = ((bf16[128,8,320]{0,2,1:T(8,128)(2,1)}), bf16[128,8,320]{0,2,1:T(8,128)(2,1)S(1)}, u32[]{:S(2)}, u32[]{:S(2)}) async-start(bf16[128,8,320]{0,2,1:T(8,128)(2,1)} %bitcast.16), calls=%async_computation.3 | async-start | bytes 1310720 | tf_op jit(solution)/shard_map/all_to_all | solution.py:395
  905.5 96.3 %all-to-all-start.3 = ((bf16[8,80,1024]{2,1,0:T(8,128)(2,1)}), bf16[8,80,1024]{2,1,0:T(8,128)(2,1)S(1)}, u32[]{:S(2)}, u32[]{:S(2)}) async-start(bf16[8,80,1024]{2,1,0:T(8,128)(2,1)} %bitcast.112), calls=%async_computation.8 | async-start | bytes 2621440 | tf_op jit(solution)/shard_map/all_to_all | solution.py:387
  910.1 312.9 %reduce-scatter.15.cloned.1.call-start = ((), (), s32[]{:S(2)}) async-start(), calls=%async_computation.23 | async-start | bytes 4505600 | tf_op jit(solution)/shard_map/reduce_scatter | solution.py:404
  1001.8 97.2 %copy-start.2 = (bf16[8,80,1024]{2,1,0:T(8,128)(2,1)}, bf16[8,80,1024]{2,1,0:T(8,128)(2,1)S(1)}, u32[]{:S(2)}) copy-start(bf16[8,80,1024]{2,1,0:T(8,128)(2,1)S(1)} %all-to-all-done.3) | copy-start | bytes 3932164
  1099.0 81.5 %all-to-all-start.2 = ((bf16[8,80,2048]{2,1,0:T(8,128)(2,1)}), bf16[8,80,2048]{2,1,0:T(8,128)(2,1)S(1)}, u32[]{:S(2)}, u32[]{:S(2)}) async-start(bf16[8,80,2048]{2,1,0:T(8,128)(2,1)} %bitcast.106), calls=%async_computation.7 | async-start | bytes 5242880 | tf_op jit(solution)/shard_map/all_to_all | solution.py:387
  (36 other events, 421.1 us)
Sparse Core Ops, SparseCore 0:
  10.4 31.7 all-gather.16
  45.6 22.1 all-gather.18
  70.2 71.9 all-gather.14
  143.8 72.3 all-gather.20
  218.5 105.0 all-gather.24
  325.7 56.0 all-gather.22
  384.1 60.1 all-gather.26
  446.0 56.0 all-gather.28
  580.5 58.6 reduce-scatter.10
  667.4 34.1 reduce-scatter.12
  703.9 62.1 reduce-scatter.8
  768.1 74.3 all-gather.32
  845.4 60.0 reduce-scatter.18
  907.6 86.9 all-gather.30
  997.5 101.4 reduce-scatter.16
  1102.4 70.7 all-gather.34
  1176.1 46.9 reduce-scatter.14

commit v2 on v1

--- a/solution.py
+++ b/solution.py
@@ -1,3 +1,4 @@
+import functools
 import math
 
 import jax
@@ -68,10 +69,70 @@
 
 VMEM_LIMIT = 56 * 1024 * 1024
 LANES = 128
+MESH = pl.DeviceIdType.MESH
+GELU = 0.7978845608028654
+CUBE = 0.044715
 
 
 def gather(value, axis):
     return lax.all_gather(value, axis, axis=0, tiled=True)
+
+
+def across(value, bit):
+    count = lax.axis_size("shard")
+    return lax.ppermute(value, "shard", [(i, i ^ bit) for i in range(count)])
+
+
+def shard_gather(block, shard):
+    rows = block.shape[0]
+    near, next_near = across(block, 1), across(block, 2)
+    far = jnp.concatenate(
+        [across(next_near[: rows // 2], 1), across(near[rows // 2 :], 2)], axis=0
+    )
+    whole = jnp.zeros((4 * rows, block.shape[1]), block.dtype)
+    for bits, part in enumerate((block, near, next_near, far)):
+        whole = lax.dynamic_update_slice_in_dim(whole, part, (shard ^ bits) * rows, 0)
+    return whole
+
+
+def vector_gather(own, shard):
+    near, next_near = across(own, 1), across(own, 2)
+    far = across(near, 2)
+    found = jnp.stack([own, near, next_near, far])
+    return jnp.stack([lax.dynamic_index_in_dim(found, shard ^ j, 0, False) for j in range(4)])
+
+
+def shard_sum(parts):
+    half = parts[0].shape[1] // 2
+
+    def two_hops(pieces, first, second):
+        own, passed = pieces[0], pieces[second]
+        got = across(jnp.concatenate([pieces[first], pieces[3]], axis=0), first).astype(jnp.float32)
+        rows = own.shape[0]
+        passed = (passed.astype(jnp.float32) + got[rows:]).astype(jnp.bfloat16)
+        return own.astype(jnp.float32) + got[:rows] + across(passed, second).astype(jnp.float32)
+
+    return jnp.concatenate(
+        [
+            two_hops([p[:, :half] for p in parts], 1, 2),
+            two_hops([p[:, half:] for p in parts], 2, 1),
+        ],
+        axis=1,
+    )
+
+
+def over_shard_rows(left, right, shard):
+    rows = left.shape[1] // 4
+    return [
+        over_rows(lax.dynamic_slice_in_dim(left, (shard ^ bits) * rows, rows, 1), right).astype(
+            jnp.bfloat16
+        )
+        for bits in range(4)
+    ]
+
+
+def after(value, *earlier):
+    return lax.optimization_barrier((value, *earlier))[0]
 
 
 def sibling(value):
@@ -115,29 +176,6 @@
 def unit_tiles(ff, shards, contexts):
     per_shard = ff // shards // LANES
     return -(-per_shard // contexts), per_shard
-
-
-def take_units_kernel(start_ref, weight_ref, out_ref):
-    out_ref[...] = weight_ref[...]
-
-
-def take_units(weight, start_tile, shards, width, per_shard):
-    rows = weight.shape[0]
-
-    def source(i, start):
-        part, rest = i // (shards * width), i % (shards * width)
-        return 0, part * shards * per_shard + (rest // width) * per_shard + start[0] + rest % width
-
-    return pl.pallas_call(
-        take_units_kernel,
-        grid_spec=pltpu.PrefetchScalarGridSpec(
-            num_scalar_prefetch=1,
-            grid=(2 * shards * width,),
-            in_specs=[pl.BlockSpec((rows, LANES), source)],
-            out_specs=pl.BlockSpec((rows, LANES), lambda i, start: (0, i)),
-        ),
-        out_shape=jax.ShapeDtypeStruct((rows, 2 * shards * width * LANES), weight.dtype),
-    )(start_tile.reshape(1), weight)
 
 
 def join_units(pieces, parts, shards, width, per_shard):
@@ -152,6 +190,162 @@
         stop = min(first + width, per_shard)
         kept.append(field[at, ..., (first - start) * LANES : (stop - start) * LANES])
     return jnp.concatenate(kept, axis=-1).reshape(*inner, parts * shards * per_shard * LANES)
+
+
+def shard_places():
+    here = lax.axis_index("shard")
+    return here, here + 1 - 2 * lax.rem(here, 2), lax.rem(here + 2, 4), 3 - here
+
+
+def greet(*places):
+    barrier = pltpu.get_barrier_semaphore()
+    for place in places:
+        pl.semaphore_signal(barrier, 1, device_id={"shard": place}, device_id_type=MESH)
+    pl.semaphore_wait(barrier, len(places))
+
+
+def to_shard(source, target, send, receive, place):
+    return pltpu.make_async_remote_copy(
+        src_ref=source,
+        dst_ref=target,
+        send_sem=send,
+        recv_sem=receive,
+        device_id={"shard": place},
+        device_id_type=MESH,
+    )
+
+
+def gather_kernel(cuts, *refs):
+    count = len(cuts)
+    sources, wholes = refs[:count], refs[count : 2 * count]
+    send, receive, local, send_on, receive_on = refs[2 * count :]
+    here, along_x, along_y, far = shard_places()
+    greet(along_x, along_y)
+
+    def block(i, place, start, rows):
+        return pl.ds(pl.multiple_of(place * cuts[i][0] + start, 16), rows)
+
+    kept, sent = [], []
+    for i, (rows, pieces) in enumerate(cuts):
+        for j, (row, column, wide, into) in enumerate(pieces()):
+            piece = sources[i].at[pl.ds(row, rows), pl.ds(column, wide)]
+            target = wholes[i].at[block(i, here, 0, rows), pl.ds(into, wide)]
+            kept.append(pltpu.make_async_copy(piece, target, local.at[i, j]))
+            kept[-1].start()
+            for hop, place in enumerate((along_x, along_y)):
+                sent.append(to_shard(piece, target, send.at[i, j, hop], receive.at[i, j, hop], place))
+                sent[-1].start()
+    for i, (rows, pieces) in enumerate(cuts):
+        half = rows // 2
+        for j, (row, column, wide, into) in enumerate(pieces()):
+            for hop, place in enumerate((along_x, along_y)):
+                came = wholes[i].at[block(i, place, 0, rows), pl.ds(into, wide)]
+                to_shard(came, came, send.at[i, j, hop], receive.at[i, j, hop], place).wait_recv()
+        for hop, (place, owner, start) in enumerate(((along_x, along_y, 0), (along_y, along_x, half))):
+            part = wholes[i].at[block(i, owner, start, half)]
+            sent.append(to_shard(part, part, send_on.at[i, hop], receive_on.at[i, hop], place))
+            sent[-1].start()
+    for i, (rows, pieces) in enumerate(cuts):
+        half = rows // 2
+        for hop, (place, start) in enumerate(((along_x, 0), (along_y, half))):
+            came = wholes[i].at[block(i, far, start, half)]
+            to_shard(came, came, send_on.at[i, hop], receive_on.at[i, hop], place).wait_recv()
+    for copy in kept:
+        copy.wait()
+    for copy in sent:
+        copy.wait_send()
+
+
+def gather_cuts(arrays, cuts, shapes, number):
+    count = len(arrays)
+    most = 8
+    return pl.pallas_call(
+        functools.partial(gather_kernel, cuts),
+        in_specs=[pl.BlockSpec(memory_space=pl.ANY)] * count,
+        out_specs=[pl.BlockSpec(memory_space=pl.ANY)] * count,
+        out_shape=[jax.ShapeDtypeStruct(shape, jnp.bfloat16) for shape in shapes],
+        scratch_shapes=[
+            pltpu.SemaphoreType.DMA((count, most, 2)),
+            pltpu.SemaphoreType.DMA((count, most, 2)),
+            pltpu.SemaphoreType.DMA((count, most)),
+            pltpu.SemaphoreType.DMA((count, 2)),
+            pltpu.SemaphoreType.DMA((count, 2)),
+        ],
+        cost_estimate=pl.CostEstimate(
+            flops=0, transcendentals=0, bytes_accessed=20 * sum(a * b for a, b in shapes)
+        ),
+        compiler_params=pltpu.CompilerParams(collective_id=number, has_side_effects=True),
+    )(*arrays)
+
+
+def product_sum_kernel(left_ref, right_ref, out_ref, own, made, first, passed, last, send, receive):
+    here, along_x, along_y, far = shard_places()
+    rows, wide = out_ref.shape
+    half = wide // 2
+    sides = (pl.ds(0, half), pl.ds(half, half))
+    ways = ((along_x, along_y), (along_y, along_x))
+
+    def product(place, side):
+        columns = pl.ds(pl.multiple_of(place * rows, LANES), rows)
+        return over_rows(left_ref[:, columns], right_ref[:, sides[side]])
+
+    greet(along_x, along_y)
+    copies = []
+
+    def push(source, target, slot, place):
+        copies.append(to_shard(source, target, send.at[slot], receive.at[slot], place))
+        copies[-1].start()
+
+    for side in range(2):
+        made[0, side] = product(far, side).astype(jnp.bfloat16)
+        push(made.at[0, side], passed.at[side], side, ways[side][0])
+    for side in range(2):
+        made[1, side] = product(ways[side][0], side).astype(jnp.bfloat16)
+        push(made.at[1, side], first.at[side], 2 + side, ways[side][0])
+    for side in range(2):
+        kept = product(ways[side][1], side)
+        copies[side].wait_recv()
+        made[2, side] = (kept + passed[side].astype(jnp.float32)).astype(jnp.bfloat16)
+        push(made.at[2, side], last.at[side], 4 + side, ways[side][1])
+    for side in range(2):
+        own[:, sides[side]] = product(here, side)
+    for side in range(2):
+        copies[2 + side].wait_recv()
+        own[:, sides[side]] += first[side].astype(jnp.float32)
+    for side in range(2):
+        copies[4 + side].wait_recv()
+        out_ref[:, sides[side]] = (own[:, sides[side]] + last[side].astype(jnp.float32)).astype(
+            jnp.bfloat16
+        )
+    for copy in copies:
+        copy.wait_send()
+
+
+def product_sum(left, right, number):
+    rows, wide = left.shape[1] // 4, right.shape[1]
+    return pl.pallas_call(
+        product_sum_kernel,
+        in_specs=[pl.BlockSpec(memory_space=pltpu.VMEM)] * 2,
+        out_specs=pl.BlockSpec(memory_space=pltpu.VMEM),
+        out_shape=jax.ShapeDtypeStruct((rows, wide), jnp.bfloat16),
+        scratch_shapes=[
+            pltpu.VMEM((rows, wide), jnp.float32),
+            pltpu.VMEM((3, 2, rows, wide // 2), jnp.bfloat16),
+            pltpu.VMEM((2, rows, wide // 2), jnp.bfloat16),
+            pltpu.VMEM((2, rows, wide // 2), jnp.bfloat16),
+            pltpu.VMEM((2, rows, wide // 2), jnp.bfloat16),
+            pltpu.SemaphoreType.DMA((6,)),
+            pltpu.SemaphoreType.DMA((6,)),
+        ],
+        cost_estimate=pl.CostEstimate(
+            flops=2 * left.shape[0] * left.shape[1] * wide,
+            transcendentals=0,
+            bytes_accessed=200 * rows * wide,
+        ),
+        compiler_params=pltpu.CompilerParams(
+            collective_id=number, has_side_effects=True, vmem_limit_bytes=VMEM_LIMIT
+        ),
+    )(left, right)
 
 
 def masked_weights(q, k, mask):
@@ -236,6 +430,82 @@
         ],
         compiler_params=pltpu.CompilerParams(vmem_limit_bytes=VMEM_LIMIT),
     )(mask, queries, keys, values, grad)
+
+
+def feed_kernel(feed_ref, grad_ref, gate_ref, up_ref, down_ref, bias_gate_ref, bias_up_ref, live_ref,
+                hidden_ref, gate_back_ref, up_back_ref, gate_sum_ref, up_sum_ref):
+    rows = feed_ref.shape[0]
+    step = min(rows, 256)
+
+    @pl.when(pl.program_id(1) == 0)
+    def _():
+        gate_sum_ref[...] = jnp.zeros_like(gate_sum_ref)
+        up_sum_ref[...] = jnp.zeros_like(up_sum_ref)
+
+    def part(i, carry):
+        at = pl.ds(pl.multiple_of(i * step, step), step)
+        feed = feed_ref[at, :]
+        gate = jnp.dot(feed, gate_ref[...], preferred_element_type=jnp.float32) + bias_gate_ref[...]
+        up = jnp.dot(feed, up_ref[...], preferred_element_type=jnp.float32) + bias_up_ref[...]
+        back = against(grad_ref[at, :], down_ref[...])
+        live = live_ref[...]
+        square = gate * gate
+        bend = jnp.tanh(GELU * gate * (1.0 + CUBE * square))
+        half = 0.5 * (1.0 + bend)
+        gelu = gate * half * live
+        slope = half + 0.5 * gate * (1.0 - bend * bend) * (GELU * (1.0 + 3.0 * CUBE * square))
+        hidden_ref[at, :] = (gelu * up).astype(jnp.bfloat16)
+        gate_back = (back * up * slope * live).astype(jnp.bfloat16)
+        up_back = (back * gelu).astype(jnp.bfloat16)
+        gate_back_ref[at, :] = gate_back
+        up_back_ref[at, :] = up_back
+        gate_sum_ref[...] += jnp.sum(gate_back.astype(jnp.float32), axis=0, keepdims=True)
+        up_sum_ref[...] += jnp.sum(up_back.astype(jnp.float32), axis=0, keepdims=True)
+        return carry
+
+    lax.fori_loop(0, rows // step, part, 0)
+
+
+def feed(feed_group, grad_group, gate_up, down, bias, live):
+    rows, model = feed_group.shape
+    units = down.shape[0]
+    wide = min(units, 256)
+    blocks = units // wide
+    tall = min(rows, 1024)
+    buffers = {"pipeline_mode": pl.Buffered(1)} if tall == rows else {}
+    tokens = lambda j, i: (i, 0)
+    column = lambda j, i: (0, j)
+    later = lambda j, i: (0, j + blocks)
+    made = lambda j, i: (i, j)
+    return pl.pallas_call(
+        feed_kernel,
+        grid=(blocks, rows // tall),
+        in_specs=[
+            pl.BlockSpec((tall, model), tokens, **buffers),
+            pl.BlockSpec((tall, model), tokens, **buffers),
+            pl.BlockSpec((model, wide), column),
+            pl.BlockSpec((model, wide), later),
+            pl.BlockSpec((wide, model), lambda j, i: (j, 0)),
+            pl.BlockSpec((1, wide), column),
+            pl.BlockSpec((1, wide), later),
+            pl.BlockSpec((1, wide), column),
+        ],
+        out_specs=[
+            pl.BlockSpec((tall, wide), made),
+            pl.BlockSpec((tall, wide), made),
+            pl.BlockSpec((tall, wide), made),
+            pl.BlockSpec((1, wide), column),
+            pl.BlockSpec((1, wide), column),
+        ],
+        out_shape=[
+            jax.ShapeDtypeStruct((rows, units), jnp.bfloat16),
+            jax.ShapeDtypeStruct((rows, units), jnp.bfloat16),
+            jax.ShapeDtypeStruct((rows, units), jnp.bfloat16),
+            jax.ShapeDtypeStruct((1, units), jnp.float32),
+            jax.ShapeDtypeStruct((1, units), jnp.float32),
+        ],
+        compiler_params=pltpu.CompilerParams(vmem_limit_bytes=VMEM_LIMIT),
+    )(feed_group, grad_group, gate_up, gate_up, down, bias, bias, live)
 
 
 def body(
@@ -265,7 +535,7 @@
     units = shards * width * LANES
 
     vectors = jnp.concatenate([attn_gain, output_bias, feed_gain, down_bias, gate_up_bias])
-    vectors = gather(vectors[None], "shard").astype(jnp.float32)
+    vectors = vector_gather(vectors, shard).astype(jnp.float32)
     gain_one, bias_out, gain_two, bias_down = (
         vectors[:, i * (model // shards) : (i + 1) * (model // shards)].reshape(1, model)
         for i in range(4)
@@ -274,17 +544,41 @@
     bias_gate_up = lax.dynamic_slice_in_dim(
         bias_gate_up, unit_start * LANES, width * LANES, 1
     ).reshape(1, 2 * units)
-    keyval_half = gather(halves(keyval_weight, core, 1)[0], "shard")
-    query_half = gather(halves(query_weight, core, 1)[0], "shard")
-    output_half = gather(halves(output_weight, core, 1)[0], "shard")
-    gate_up_part = gather(
-        take_units(gate_up_weight, unit_start, shards, width, per_shard), "shard"
-    )
-    down_part = gather(
-        lax.dynamic_slice_in_dim(down_weight, unit_start * LANES, width * LANES, 0), "shard"
+    shard_rows = model // shards
+    core_cols, core_heads = keyval_weight.shape[1] // 2, query_weight.shape[1] // 2
+
+    def cut_of(wide):
+        def pieces():
+            column = lax.rem(lax.axis_index("context"), 2) * wide
+            return [(0, pl.multiple_of(column, LANES), wide, 0)]
+
+        return shard_rows, pieces
+
+    block = width * LANES
+
+    def first_unit():
+        return jnp.minimum(lax.axis_index("context") * width, per_shard - width) * LANES
+
+    def gate_up_pieces():
+        return [
+            (0, pl.multiple_of(j * per_shard * LANES + first_unit(), LANES), block, j * block)
+            for j in range(2 * shards)
+        ]
+
+    def down_pieces():
+        return [(pl.multiple_of(first_unit(), LANES), 0, model, 0)]
+
+    keyval_half, query_half = gather_cuts(
+        (after(keyval_weight, vectors), query_weight),
+        (cut_of(core_cols), cut_of(core_heads)),
+        ((model, core_cols), (model, core_heads)),
+        0,
+    )
+    output_half = shard_gather(
+        after(halves(output_weight, core, 1)[0], keyval_half, query_half), shard
     )
     unit_at = unit_start * LANES + jnp.arange(width * LANES, dtype=jnp.int32)
-    unit_live = jnp.tile(unit_at >= place * width * LANES, shards)[None, :]
+    unit_live = jnp.tile(unit_at >= place * width * LANES, shards)[None, :].astype(jnp.float32)
 
     source = inputs.astype(jnp.float32)
     attn_in = rms_norm(source, gain_one).astype(jnp.bfloat16)
@@ -300,7 +594,8 @@
     cosine, sine = jnp.cos(angles), jnp.sin(angles)
     keyval_raw = jnp.dot(attn_pair, keyval_half, preferred_element_type=jnp.float32)
     keyval = jnp.where(core == 0, rotate(keyval_raw, cosine, sine), keyval_raw).astype(jnp.bfloat16)
-    keyval = gather(keyval, "context").reshape(contexts // 2, 2, 2 * tok, DH)
+    grad_group = gather(cotangent, "context")
+    keyval = gather(after(keyval, grad_group), "context").reshape(contexts // 2, 2, 2 * tok, DH)
     keys, values = keyval[:, 0].reshape(group, DH), keyval[:, 1].reshape(group, DH)
     query_raw = jnp.dot(attn_pair, query_half, preferred_element_type=jnp.float32)
     heads = query_raw.shape[1] // DH
@@ -321,28 +616,22 @@
     resid = source + attn_out + bias_out
 
     feed_in = rms_norm(resid, gain_two).astype(jnp.bfloat16)
-    grad_group = gather(cotangent, "context")
+    mixed_group = gather(mixed_own, "context")
     feed_group = gather(feed_in, "context")
-    gate_up = jnp.dot(feed_group, gate_up_part, preferred_element_type=jnp.float32) + bias_gate_up
-    hidden_grad = against(grad_group, down_part)
-
-    def live_geglu(field):
-        return jnp.where(unit_live, geglu(field), 0.0)
-
-    hidden, geglu_pull = jax.vjp(live_geglu, gate_up)
-    hidden = hidden.astype(jnp.bfloat16)
-    gate_up_low = geglu_pull(hidden_grad)[0].astype(jnp.bfloat16)
+    gate_up_part, down_part = gather_cuts(
+        (gate_up_weight, after(down_weight, feed_in)),
+        ((shard_rows, gate_up_pieces), (block, down_pieces)),
+        ((model, 2 * units), (units, model)),
+        1,
+    )
+    hidden, gate_back, up_back, gate_sums, up_sums = feed(
+        feed_group, grad_group, gate_up_part, down_part, bias_gate_up, unit_live
+    )
+    gate_up_low = jnp.concatenate([gate_back, up_back], axis=1)
     feed_part = against(gate_up_low, gate_up_part).astype(jnp.bfloat16)
-    feed_in_grad = lax.psum_scatter(
-        feed_part, "context", scatter_dimension=0, tiled=True
-    ).astype(jnp.float32)
-    down_out = lax.psum_scatter(
-        jnp.dot(hidden, down_part, preferred_element_type=jnp.float32).astype(jnp.bfloat16),
-        "context",
-        scatter_dimension=0,
-        tiled=True,
-    ).astype(jnp.float32)
-    block_out = (resid + down_out + bias_down).astype(jnp.bfloat16)
+    feed_in_grad = lax.psum_scatter(feed_part, "context", scatter_dimension=0, tiled=True)
+    down_sum = product_sum(grad_group, after(hidden, feed_part), 2)
+    feed_in_grad = after(feed_in_grad, down_sum).astype(jnp.float32)
 
     grad_out = cotangent.astype(jnp.float32)
     resid_part, gain_two_grad = jax.vjp(rms_norm, resid, gain_two)[1](feed_in_grad)
@@ -356,7 +645,16 @@
         [key_acc.reshape(contexts // 2, 2 * tok, DH), value_acc.reshape(contexts // 2, 2 * tok, DH)],
         axis=1,
     ).reshape(2 * group, DH)
+    down_part_out = jnp.dot(
+        after(hidden, keyval_acc), down_part, preferred_element_type=jnp.float32
+    ).astype(jnp.bfloat16)
+    gate_sum = product_sum(feed_group, after(gate_back, keyval_acc), 2)
     keyval_acc = lax.psum_scatter(keyval_acc, "context", scatter_dimension=0, tiled=True)
+    keyval_acc = after(keyval_acc, gate_sum, down_part_out)
+    down_out = lax.psum_scatter(
+        after(down_part_out, keyval_acc), "context", scatter_dimension=0, tiled=True
+    ).astype(jnp.float32)
+    block_out = (resid + down_out + bias_down).astype(jnp.bfloat16)
     keyval_back = jnp.where(core == 0, rotate(keyval_acc, cosine, -sine), keyval_acc).astype(
         jnp.bfloat16
     )
@@ -370,26 +668,15 @@
     input_part, gain_one_grad = jax.vjp(rms_norm, source, gain_one)[1](attn_in_grad)
     input_grad = resid_grad + input_part
 
-    gate_up_sum = lax.psum_scatter(
-        over_rows(feed_group, gate_up_low).astype(jnp.bfloat16),
-        "shard",
-        scatter_dimension=0,
-        tiled=True,
-    )
-    down_sum = lax.psum_scatter(
-        over_rows(grad_group, hidden).astype(jnp.bfloat16),
-        "shard",
-        scatter_dimension=0,
-        tiled=True,
-    )
-
     def to_owners(field):
         return lax.all_to_all(
             field.reshape(contexts, owned, field.shape[1]), "context", split_axis=0, concat_axis=0
         ).astype(jnp.float32)
 
-    gate_up_grad = join_units(to_owners(gate_up_sum), 2, shards, width, per_shard)
-    down_weight_grad = join_units(to_owners(down_sum), 1, shards, width, per_shard).T
+    def whole_units(field):
+        return join_units(to_owners(field), 1, shards, width, per_shard)
+
+    down_weight_grad = whole_units(down_sum).T
 
     def token_rows(field):
         return lax.all_to_all(
@@ -400,19 +687,17 @@
         [swap_rows(query_back, core), swap_rows(keyval_back, core)], axis=1
     )
     back_group = gather(back_own, "context")
-    mixed_group = gather(mixed_own, "context")
-    attn_sum = lax.psum_scatter(
-        jnp.concatenate(
-            [
-                over_rows(token_rows(attn_in), back_group),
-                over_rows(token_rows(attn_grad_low), mixed_group),
-            ],
-            axis=1,
-        ).astype(jnp.bfloat16),
-        "shard",
-        scatter_dimension=0,
-        tiled=True,
-    ).astype(jnp.float32)
+    up_sum = product_sum(feed_group, after(up_back, back_own), 2)
+    back_group = after(back_group, up_sum)
+    gate_up_grad = jnp.concatenate([whole_units(gate_sum), whole_units(up_sum)], axis=1)
+    attn_rows, attn_grad_rows = token_rows(attn_in), token_rows(attn_grad_low)
+    attn_sum = jnp.concatenate(
+        [
+            shard_sum(over_shard_rows(attn_rows, back_group, shard)),
+            shard_sum(over_shard_rows(attn_grad_rows, mixed_group, shard)),
+        ],
+        axis=1,
+    )
     head_cols = HEADS * DH
     query_grad = attn_sum[:, :head_cols]
     keyval_grad = attn_sum[:, head_cols : head_cols + 2 * DH]
@@ -424,10 +709,13 @@
             jnp.sum(attn_grad_low.astype(jnp.float32), axis=0),
             gain_two_grad.reshape(model),
             jnp.sum(grad_out, axis=0),
-            jnp.sum(gate_up_low.astype(jnp.float32), axis=0),
+            gate_sums.reshape(units),
+            up_sums.reshape(units),
         ]
     )
-    sums = lax.all_gather(sums, ("shard", "context"), axis=0, tiled=False)
+    sums = sums + across(sums, 1)
+    sums = sums + across(sums, 2)
+    sums = gather(sums[None], "context")
     device = shard * contexts + place
     own = [
         jnp.sum(
@@ -436,8 +724,7 @@
         )
         for i in range(4)
     ]
-    unit_sums = jnp.sum(sums[:, 4 * model :].reshape(shards, contexts, 2 * units), axis=0)
-    unit_sums = join_units(unit_sums, 2, shards, width, per_shard)
+    unit_sums = join_units(sums[:, 4 * model :], 2, shards, width, per_shard)
     unit_owned = 2 * ff // (shards * contexts)
     gate_up_bias_grad = lax.dynamic_slice_in_dim(unit_sums, device * unit_owned, unit_owned)
     return (

time: 1250 us -> 848 us (0.68)
  waiting for transfers between devices: 807 us -> 103 us
  Pallas kernels: 28.5 us -> 398 us
  matrix products: 119 us -> 69.1 us
  local copies, waits for them, and re-layouts: 157 us -> 122 us
  starting transfers between devices: 23.2 us -> 57.1 us
  other arithmetic: 73.4 us -> 54.1 us
    all_gather x10 -> x5, waiting for transfers between devices: 520 us -> 8.55 us  [gather(): return lax.all_gather(value, axis, axis=0, tiled=True)]
    pallas_call x1 -> x6, Pallas kernels: 9.69 us -> 379 us  [the longest x2 198 us: gather_cuts(): pl.pallas_call(functools.partial(gather_kernel, cuts), in_specs=[pl.Block...]
    reduce_scatter x4 -> x1, waiting for transfers between devices: 169 us -> 0.01 us  [body(): lax.psum_scatter(after(down_part_out, keyval_acc), 'context', scatter_dim...]
    reduce_scatter x1, waiting for transfers between devices: 58.8 us -> 9.53 us  [body(): lax.psum_scatter(feed_part, 'context', scatter_dimension=0, tiled=True)]
    all_gather x1 -> x0, waiting for transfers between devices: 46 us -> none  [body(): sums = lax.all_gather(sums, ('shard', 'context'), axis=0, tiled=False)]
    all_to_all x2 -> x3, waiting for transfers between devices: 0.01 us -> 38.6 us  [to_owners(): lax.all_to_all(field.reshape(contexts, owned, field.shape[1]), 'context',...]
    ppermute x0 -> x17, waiting for transfers between devices: none -> 31.4 us  [across(): return lax.ppermute(value, 'shard', [(i, i ^ bit) for i in range(count)])]
    mul x5 -> x0, local copies, waits for them, and re-layouts: 27.3 us -> none  [geglu(): return jax.nn.gelu(gate_up[:, :half], approximate=True) * gate_up[:, half:]]
  transfers between devices with their start and end apart: 30 -> 39, of which waited for: 22 -> 16; matrix products, arithmetic and copies ran while one was open for 20% -> 23% of each run, Pallas kernels for 1% -> 43%
where the time goes in v2:
time: 848 us; the launch traced here: 834 us
  Pallas kernels  398 us (47%)
  local copies, waits for them, and re-layouts  122 us (14%)
  waiting for transfers between devices  103 us (12%)
  matrix products  69.1 us (8%)
  starting transfers between devices  57.1 us (7%)
  other arithmetic  54.1 us (6%)
  between operations  15.9 us (2%)
  blocking collectives  14.8 us (2%)
    pallas_call x2, Pallas kernels, gather_cuts(): pl.pallas_call(functools.partial(gather_kernel, cuts), in_specs=[pl.Block...  198 us
    pallas_call x3, Pallas kernels, product_sum(): pl.pallas_call(product_sum_kernel, in_specs=[pl.BlockSpec(memory_space=pl...  154 us
    all_to_all x3, waiting for transfers between devices, to_owners(): lax.all_to_all(field.reshape(contexts, owned, field.shape[1]), 'context',...  38.6 us
    squeeze x28, local copies, waits for them, and re-layouts, join_units(): kept.append(field[at, ..., (first - start) * LANES:(stop - start) * LANES])  35 us
    ppermute x17, waiting for transfers between devices, across(): return lax.ppermute(value, 'shard', [(i, i ^ bit) for i in range(count)])  31.4 us
    unnamed x168, local copies, waits for them, and re-layouts  30.4 us
    dot_general x4, matrix products, against(): lax.dot_general(left, weight, (((1,), (1,)), ((), ())), preferred_element...  28.5 us
    pallas_call x1, Pallas kernels, feed(): pl.pallas_call(feed_kernel, grid=(blocks, rows // tall), in_specs=[pl.Blo...  27.1 us
  transfers between devices with their start and end apart: 39, of which 16 were waited for; matrix products, arithmetic and copies ran while one was open for 23% of the time, Pallas kernels for 43%

profile of v2, /device:TPU:0, one launch (start us, length us, event | category | flops | bytes accessed | tf_op | source)
XLA Modules:
  0.0 833.7 jit_solution(15968511584403760209)
XLA Ops:
  24.4 67.5 %shard_map.220 = (bf16[2560,256]{1,0:T(8,128)(2,1)}, bf16[2560,1280]{1,0:T(8,128)(2,1)}) custom-call(bf16[640,512]{1,0:T(8,128)(2,1)} %refs_0_.1, bf16[640,2560]{1,0:T(8,128)(2,1)} %refs_1_.1), custom_call_target="tpu_custom_call" | custom-call | bytes 78643200 | tf_op jit(solution)/shard_map/pallas_call | solution.py:262
  102.2 5.7 fusion.47
  109.2 8.5 %all-gather.9.cloned.1.call-done = bf16[2048,256]{1,0:T(8,128)(2,1)} async-done(((bf16[256,256]{1,0:T(8,128)(2,1)}), bf16[2048,256]{1,0:T(8,128)(2,1)}) %all-gather.9.cloned.1.call-update) | async-done | bytes 1048592 | tf_op jit(solution)/shard_map/all_gather | solution.py:78
  120.0 7.6 shard_map.221
  151.7 6.8 collective-permute-done.8
  164.3 4.8 fusion.16
  177.5 130.3 %shard_map.222 = (bf16[2560,2048]{1,0:T(8,128)(2,1)}, bf16[1024,2560]{1,0:T(8,128)(2,1)}) custom-call(bf16[640,15360]{1,0:T(8,128)(2,1)} %refs_0_.2, bf16[1920,2560]{1,0:T(8,128)(2,1)} %refs_1_.2), custom_call_target="tpu_custom_call" | custom-call | bytes 157286400 | tf_op jit(solution)/shard_map/pallas_call | solution.py:262
  307.9 27.1 %shard_map.223 = (bf16[1024,1024]{1,0:T(8,128)(2,1)}, bf16[1024,1024]{1,0:T(8,128)(2,1)}, bf16[1024,1024]{1,0:T(8,128)(2,1)}, f32[1,1024]{1,0:T(1,128)}, f32[1,1024]{1,0:T(1,128)}) custom-call(bf16[1024,2560]{1,0:T(8,128)(2,1)} %all-gather.11.cloned.1.call-done.feed_ref.left_ref, bf16[1024,2560]{1,0:T(8,128)(2,1)} %all-gather.7.cloned.1.call-done.grad_ref.left_ref, ...), custom_call_target="tpu_custom_call" | custom-call | tf_op jit(solution)/shard_map/pallas_call | solution.py:480
  335.0 16.5 %convolution_convert_fusion.1 = bf16[1024,2560]{1,0:T(8,128)(2,1)} fusion(bf16[2560,2048]{1,0:T(8,128)(2,1)} %get-tuple-element.42.gate_ref.up_ref, bf16[1024,1024]{1,0:T(8,128)(2,1)} %get-tuple-element.58.right_ref, bf16[1024,1024]{1,0:T(8,128)(2,1)} %get-tuple-element.52.right_ref), kind=kOutput, calls=%fused_computation.1 | convolution fusion | flops 10748428288 | bytes 19922944 | tf_op jit(solution)/shard_map/dot_general | solution.py:55
  351.9 50.4 %shard_map.224 = bf16[640,1024]{1,0:T(8,128)(2,1)} custom-call(bf16[1024,2560]{1,0:T(8,128)(2,1)} %all-gather.7.cloned.1.call-done.grad_ref.left_ref, bf16[1024,1024]{1,0:T(8,128)(2,1)} %get-tuple-element.51.right_ref), custom_call_target="tpu_custom_call" | custom-call | flops 5368709120 | bytes 131072000 | tf_op jit(solution)/shard_map/pallas_call | solution.py:326
  402.4 9.5 %reduce-scatter.4.cloned.1.call-done = bf16[128,2560]{1,0:T(8,128)(2,1)} async-done(((bf16[1024,2560]{1,0:T(8,128)(2,1)}), bf16[128,2560]{1,0:T(8,128)(2,1)}) %reduce-scatter.4.cloned.1.call-update) | async-done | bytes 655376 | tf_op jit(solution)/shard_map/reduce_scatter | solution.py:632
  417.1 4.8 fusion.29
  426.1 10.9 %shard_map.225 = (f32[256,1280]{1,0:T(8,128)}, f32[1024,256]{1,0:T(8,128)}, f32[1024,256]{1,0:T(8,128)}) custom-call(f32[256,1024]{1,0:T(8,128)} %fusion.28.mask_ref, bf16[256,1280]{1,0:T(8,128)(2,1)} %copy.117.q_ref, bf16[1024,256]{1,0:T(8,128)(2,1)} %bitcast.109, bf16[1024,256]{1,0:T(8,128)(2,1)} %bitcast.107, bf16[256,1280]{1,0:T(8,128)(2,1)} %add_convert_fusion.1.g_ref), custom_call_target="tpu_custom_call" | custom-call | tf_op jit(solution)/shard_map/pallas_call | solution.py:411
  445.5 10.7 %reduce-scatter.8.cloned.1.call-start = ((), (), s32[]{:S(2)}) async-start(), calls=%async_computation.13 | async-start | bytes 5898240 | tf_op jit(solution)/shard_map/reduce_scatter | solution.py:654
  456.2 10.2 %convolution_convert_fusion = bf16[1024,2560]{1,0:T(8,128)(2,1)} fusion(bf16[1024,1024]{1,0:T(8,128)(2,1)} %get-tuple-element.51.right_ref, bf16[1024,2560]{1,0:T(8,128)(2,1)} %get-tuple-element.43.down_ref), kind=kOutput, calls=%fused_computation | convolution fusion | flops 5371330560 | bytes 12582912 | tf_op jit(solution)/shard_map/dot_general | solution.py:648
  466.4 52.1 %shard_map.226 = bf16[640,1024]{1,0:T(8,128)(2,1)} custom-call(bf16[1024,2560]{1,0:T(8,128)(2,1)} %all-gather.11.cloned.1.call-done.feed_ref.left_ref, bf16[1024,1024]{1,0:T(8,128)(2,1)} %get-tuple-element.52.right_ref), custom_call_target="tpu_custom_call" | custom-call | flops 5368709120 | bytes 131072000 | tf_op jit(solution)/shard_map/pallas_call | solution.py:326
  519.4 4.8 all-to-all-start.4
  531.8 36.2 %all-to-all-done.4 = bf16[8,80,1024]{2,1,0:T(8,128)(2,1)S(1)} async-done(((bf16[8,80,1024]{2,1,0:T(8,128)(2,1)}), bf16[8,80,1024]{2,1,0:T(8,128)(2,1)S(1)}, u32[]{:S(2)}, u32[]{:S(2)}) %all-to-all-start.4) | async-done | bytes 1310752 | tf_op jit(solution)/shard_map/all_to_all | solution.py:672
  568.0 4.2 all-to-all-start.1
  594.8 6.5 all-to-all-done.1
  602.5 3.7 convolution_convert_fusion.2
  613.7 5.2 collective-permute-done.24
  626.7 3.6 all-to-all-start.2
  643.3 5.1 fusion.101
  652.8 51.7 %shard_map.227 = bf16[640,1024]{1,0:T(8,128)(2,1)} custom-call(bf16[1024,2560]{1,0:T(8,128)(2,1)} %all-gather.11.cloned.1.call-done.feed_ref.left_ref, bf16[1024,1024]{1,0:T(8,128)(2,1)} %get-tuple-element.58.right_ref), custom_call_target="tpu_custom_call" | custom-call | flops 5368709120 | bytes 131072000 | tf_op jit(solution)/shard_map/pallas_call | solution.py:326
  704.5 5.4 all-to-all-start.3
  753.7 3.9 reshape.327
  765.3 3.7 fusion.11
  777.5 14.8 %all-gather = f32[98304]{0:T(1024)S(1)} all-gather(f32[12288]{0:T(1024)S(1)} %add.245), channel_id=2, replica_groups=mesh['shard'=4,'context'=8] {'context'}, dimensions={0}, use_global_device_ids=true | all-gather | bytes 442368 | tf_op jit(solution)/shard_map/all_gather | solution.py:78
  793.5 4.1 convolution_convert_fusion.6
  806.2 7.8 collective-permute-done.20
  818.5 4.0 convolution_convert_fusion.9
  (405 shorter events, 229.8 us)
Async XLA Ops:
  7.2 87.9 %all-gather.7.cloned.1.call-start = ((), (), s32[]{:S(2)}) async-start(), calls=%async_computation.8 | async-start | bytes 5898240 | tf_op jit(solution)/shard_map/all_gather | solution.py:78
  7.9 109.8 %all-gather.9.cloned.1.call-start = ((), (), s32[]{:S(2)}) async-start(), calls=%async_computation.9 | async-start | bytes 1179648 | tf_op jit(solution)/shard_map/all_gather | solution.py:78
  12.3 5.8 collective-permute-start
  23.2 68.7 %collective-permute-start.3 = (bf16[128,2560]{1,0:T(8,128)(2,1)S(1)}, bf16[128,2560]{1,0:T(8,128)(2,1)S(1)}, u32[]{:S(2)}, u32[]{:S(2)}) collective-permute-start(bf16[128,2560]{1,0:T(8,128)(2,1)S(1)} %fusion.7), channel_id=1, source_target_pairs={{0,1},{1,0},{2,3},{3,2},{4,5},{5,4},{6,7},{7,6},{8,9},{9,8},{10,11... | collective-permute-start | bytes 1966088 | tf_op jit(solution)/shard_map/ppermute | solution.py:140
  95.2 212.7 %all-gather.11.cloned.1.call-start = ((), (), s32[]{:S(2)}) async-start(), calls=%async_computation.10 | async-start | bytes 5898240 | tf_op jit(solution)/shard_map/all_gather | solution.py:78
  100.1 41.3 %collective-permute-start.6 = (bf16[640,1280]{1,0:T(8,128)(2,1)}, bf16[640,1280]{1,0:T(8,128)(2,1)}, u32[]{:S(2)}, u32[]{:S(2)}) collective-permute-start(bf16[640,1280]{1,0:T(8,128)(2,1)} %slice_select_fusion), channel_id=1, source_target_pairs={{0,8},{8,0},{16,24},{24,16},{1,9},{9,1},{17,25},{25,17},{2,10},{10... | collective-permute-start | bytes 4915208 | tf_op jit(solution)/shard_map/ppermute | solution.py:83
  100.7 37.2 %collective-permute-start.7 = (bf16[640,1280]{1,0:T(8,128)(2,1)}, bf16[640,1280]{1,0:T(8,128)(2,1)}, u32[]{:S(2)}, u32[]{:S(2)}) collective-permute-start(bf16[640,1280]{1,0:T(8,128)(2,1)} %slice_select_fusion), channel_id=1, source_target_pairs={{0,16},{8,24},{16,0},{24,8},{1,17},{9,25},{17,1},{25,9},{2,18},{10... | collective-permute-start | bytes 4915208 | tf_op jit(solution)/shard_map/ppermute | solution.py:83
  128.7 15.3 %collective-permute-start.4 = (bf16[128,1280]{1,0:T(8,128)(2,1)S(1)}, bf16[128,1280]{1,0:T(8,128)(2,1)S(1)}, u32[]{:S(2)}, u32[]{:S(2)}) collective-permute-start(bf16[128,1280]{1,0:T(8,128)(2,1)S(1)} %get-tuple-element.113), channel_id=1, source_target_pairs={{0,1},{1,0},{2,3},{3,2},{4,5},{5,4},{6,7},{7,6},{8,9},{9,8},{10,11... | collective-permute-start | bytes 983048 | tf_op jit(solution)/shard_map/ppermute | solution.py:140
  139.9 18.6 %collective-permute-start.8 = (bf16[320,1280]{1,0:T(8,128)(2,1)}, bf16[320,1280]{1,0:T(8,128)(2,1)S(1)}, u32[]{:S(2)}, u32[]{:S(2)}) collective-permute-start(bf16[320,1280]{1,0:T(8,128)(2,1)} %slice.382), channel_id=1, source_target_pairs={{0,8},{8,0},{16,24},{24,16},{1,9},{9,1},{17,25},{25,17},{2,10},{10... | collective-permute-start | bytes 2457608 | tf_op jit(solution)/shard_map/ppermute | solution.py:83
  143.5 18.4 %collective-permute-start.9 = (bf16[320,1280]{1,0:T(8,128)(2,1)}, bf16[320,1280]{1,0:T(8,128)(2,1)}, u32[]{:S(2)}, u32[]{:S(2)}) collective-permute-start(bf16[320,1280]{1,0:T(8,128)(2,1)} %slice.383), channel_id=1, source_target_pairs={{0,16},{8,24},{16,0},{24,8},{1,17},{9,25},{17,1},{25,9},{2,18},{10... | collective-permute-start | bytes 2457608 | tf_op jit(solution)/shard_map/ppermute | solution.py:83
  146.0 18.3 %collective-permute-start.5 = (bf16[128,2560]{1,0:T(8,128)(2,1)S(1)}, bf16[128,2560]{1,0:T(8,128)(2,1)S(1)}, u32[]{:S(2)}, u32[]{:S(2)}) collective-permute-start(bf16[128,2560]{1,0:T(8,128)(2,1)S(1)} %maximum_select_fusion.4), channel_id=1, source_target_pairs={{0,1},{1,0},{2,3},{3,2},{4,5},{5,4},{6,7},{7,6},{8,9},{9,8},{10,11... | collective-permute-start | bytes 1966088 | tf_op jit(solution)/shard_map/ppermute | solution.py:140
  176.0 235.9 %reduce-scatter.4.cloned.1.call-start = ((), (), s32[]{:S(2)}) async-start(), calls=%async_computation.11 | async-start | bytes 5898240 | tf_op jit(solution)/shard_map/reduce_scatter | solution.py:632
  351.6 166.9 %reduce-scatter.6.cloned.1.call-start = ((), (), s32[]{:S(2)}) async-start(), calls=%async_computation.12 | async-start | bytes 2359296 | tf_op jit(solution)/shard_map/reduce_scatter | solution.py:652
  440.2 162.3 %all-gather.15.cloned.1.call-start = ((), (), s32[]{:S(2)}) async-start(), calls=%async_computation.15 | async-start | bytes 5898240 | tf_op jit(solution)/shard_map/all_gather | solution.py:78
  442.0 76.6 %all-to-all-start = ((bf16[128,8,320]{0,2,1:T(8,128)(2,1)}), bf16[128,8,320]{0,2,1:T(8,128)(2,1)S(1)}, u32[]{:S(2)}, u32[]{:S(2)}) async-start(bf16[128,8,320]{0,2,1:T(8,128)(2,1)} %bitcast.16), calls=%async_computation.3 | async-start | bytes 1310720 | tf_op jit(solution)/shard_map/all_to_all | solution.py:682
  445.5 319.7 %reduce-scatter.8.cloned.1.call-start = ((), (), s32[]{:S(2)}) async-start(), calls=%async_computation.13 | async-start | bytes 5898240 | tf_op jit(solution)/shard_map/reduce_scatter | solution.py:654
  519.4 48.6 %all-to-all-start.4 = ((bf16[8,80,1024]{2,1,0:T(8,128)(2,1)}), bf16[8,80,1024]{2,1,0:T(8,128)(2,1)S(1)}, u32[]{:S(2)}, u32[]{:S(2)}) async-start(bf16[8,80,1024]{2,1,0:T(8,128)(2,1)} %bitcast.122), calls=%async_computation.7 | async-start | bytes 2621440 | tf_op jit(solution)/shard_map/all_to_all | solution.py:672
  568.0 33.3 %all-to-all-start.1 = ((bf16[128,8,320]{0,2,1:T(8,128)(2,1)}), bf16[128,8,320]{0,2,1:T(8,128)(2,1)}, u32[]{:S(2)}, u32[]{:S(2)}) async-start(bf16[128,8,320]{0,2,1:T(8,128)(2,1)} %bitcast.115), calls=%async_computation.4 | async-start | bytes 1310720 | tf_op jit(solution)/shard_map/all_to_all | solution.py:682
  607.8 11.2 %collective-permute-start.24 = (bf16[160,1280]{1,0:T(8,128)(2,1)S(1)}, bf16[160,1280]{1,0:T(8,128)(2,1)S(1)}, u32[]{:S(2)}, u32[]{:S(2)}) collective-permute-start(bf16[160,1280]{1,0:T(8,128)(2,1)S(1)} %pad_maximum_fusion.7), channel_id=1, source_target_pairs={{0,16},{8,24},{16,0},{24,8},{1,17},{9,25},{17,1},{25,9},{2,18},{10... | collective-permute-start | bytes 1228808 | tf_op jit(solution)/shard_map/ppermute | solution.py:83
  610.4 10.9 %collective-permute-start.22 = (bf16[160,1280]{1,0:T(8,128)(2,1)S(1)}, bf16[160,1280]{1,0:T(8,128)(2,1)S(1)}, u32[]{:S(2)}, u32[]{:S(2)}) collective-permute-start(bf16[160,1280]{1,0:T(8,128)(2,1)S(1)} %pad_maximum_fusion.6), channel_id=1, source_target_pairs={{0,8},{8,0},{16,24},{24,16},{1,9},{9,1},{17,25},{25,17},{2,10},{10... | collective-permute-start | bytes 1228808 | tf_op jit(solution)/shard_map/ppermute | solution.py:83
  619.8 28.6 %collective-permute-start.25 = (bf16[80,1280]{1,0:T(8,128)(2,1)}, bf16[80,1280]{1,0:T(8,128)(2,1)}, u32[]{:S(2)}, u32[]{:S(2)}) collective-permute-start(bf16[80,1280]{1,0:T(8,128)(2,1)} %fusion.40), channel_id=1, source_target_pairs={{0,8},{8,0},{16,24},{24,16},{1,9},{9,1},{17,25},{25,17},{2,10},{10... | collective-permute-start | bytes 614408 | tf_op jit(solution)/shard_map/ppermute | solution.py:83
  622.2 26.3 %collective-permute-start.23 = (bf16[80,1280]{1,0:T(8,128)(2,1)}, bf16[80,1280]{1,0:T(8,128)(2,1)}, u32[]{:S(2)}, u32[]{:S(2)}) collective-permute-start(bf16[80,1280]{1,0:T(8,128)(2,1)} %fusion.42), channel_id=1, source_target_pairs={{0,16},{8,24},{16,0},{24,8},{1,17},{9,25},{17,1},{25,9},{2,18},{10... | collective-permute-start | bytes 614408 | tf_op jit(solution)/shard_map/ppermute | solution.py:83
  626.7 77.8 %all-to-all-start.2 = ((bf16[8,80,1024]{2,1,0:T(8,128)(2,1)}), bf16[8,80,1024]{2,1,0:T(8,128)(2,1)S(1)}, u32[]{:S(2)}, u32[]{:S(2)}) async-start(bf16[8,80,1024]{2,1,0:T(8,128)(2,1)} %bitcast.121), calls=%async_computation.5 | async-start | bytes 2621440 | tf_op jit(solution)/shard_map/all_to_all | solution.py:672
  630.3 163.2 %all-gather.13.cloned.1.call-start = ((), (), s32[]{:S(2)}) async-start(), calls=%async_computation.14 | async-start | bytes 7077888 | tf_op jit(solution)/shard_map/all_gather | solution.py:78
  636.5 4.3 collective-permute-start.16
  704.5 37.6 %all-to-all-start.3 = ((bf16[8,80,1024]{2,1,0:T(8,128)(2,1)}), bf16[8,80,1024]{2,1,0:T(8,128)(2,1)}, u32[]{:S(2)}, u32[]{:S(2)}) async-start(bf16[8,80,1024]{2,1,0:T(8,128)(2,1)} %bitcast.123), calls=%async_computation.6 | async-start | bytes 2621440 | tf_op jit(solution)/shard_map/all_to_all | solution.py:672
  712.8 23.2 %collective-permute-start.13 = (f32[128,2560]{1,0:T(8,128)}, f32[128,2560]{1,0:T(8,128)}, u32[]{:S(2)}, u32[]{:S(2)}) collective-permute-start(f32[128,2560]{1,0:T(8,128)} %slice_select_fusion.1), channel_id=1, source_target_pairs={{0,1},{1,0},{2,3},{3,2},{4,5},{5,4},{6,7},{7,6},{8,9},{9,8},{10,11... | collective-permute-start | bytes 3932168 | tf_op jit(solution)/shard_map/ppermute | solution.py:140
  769.0 4.3 collective-permute-start.14
  800.2 13.8 %collective-permute-start.20 = (bf16[160,1536]{1,0:T(8,128)(2,1)}, bf16[160,1536]{1,0:T(8,128)(2,1)}, u32[]{:S(2)}, u32[]{:S(2)}) collective-permute-start(bf16[160,1536]{1,0:T(8,128)(2,1)} %pad_maximum_fusion.5), channel_id=1, source_target_pairs={{0,16},{8,24},{16,0},{24,8},{1,17},{9,25},{17,1},{25,9},{2,18},{10... | collective-permute-start | bytes 1474568 | tf_op jit(solution)/shard_map/ppermute | solution.py:83
  802.8 13.7 %collective-permute-start.18 = (bf16[160,1536]{1,0:T(8,128)(2,1)S(1)}, bf16[160,1536]{1,0:T(8,128)(2,1)}, u32[]{:S(2)}, u32[]{:S(2)}) collective-permute-start(bf16[160,1536]{1,0:T(8,128)(2,1)S(1)} %pad_maximum_fusion.4), channel_id=1, source_target_pairs={{0,8},{8,0},{16,24},{24,16},{1,9},{9,1},{17,25},{25,17},{2,10},{10... | collective-permute-start | bytes 1474568 | tf_op jit(solution)/shard_map/ppermute | solution.py:83
  815.1 7.5 collective-permute-start.21
  817.7 7.2 collective-permute-start.19
  (70 other events, 800.3 us)
Sparse Core Ops, SparseCore 0:
  9.7 58.7 all-gather.6
  95.3 22.3 all-gather.8
  176.1 56.2 all-gather.10
  351.7 60.1 reduce-scatter.3
  440.3 41.6 reduce-scatter.5
  483.5 69.9 all-gather.14
  555.8 74.1 reduce-scatter.7
  643.4 72.9 all-gather.12

commit v3 on v2

--- a/solution.py
+++ b/solution.py
@@ -57,16 +57,6 @@
     )
 
 
-def regroup(field, shard_count, context_count):
-    rows_now, width = field.shape
-    owned = width // (shard_count * context_count)
-    return (
-        field.reshape(rows_now, shard_count, context_count, owned)
-        .transpose(0, 2, 1, 3)
-        .reshape(rows_now, width)
-    )
-
-
 VMEM_LIMIT = 56 * 1024 * 1024
 LANES = 128
 MESH = pl.DeviceIdType.MESH
@@ -100,35 +90,6 @@
     far = across(near, 2)
     found = jnp.stack([own, near, next_near, far])
     return jnp.stack([lax.dynamic_index_in_dim(found, shard ^ j, 0, False) for j in range(4)])
-
-
-def shard_sum(parts):
-    half = parts[0].shape[1] // 2
-
-    def two_hops(pieces, first, second):
-        own, passed = pieces[0], pieces[second]
-        got = across(jnp.concatenate([pieces[first], pieces[3]], axis=0), first).astype(jnp.float32)
-        rows = own.shape[0]
-        passed = (passed.astype(jnp.float32) + got[rows:]).astype(jnp.bfloat16)
-        return own.astype(jnp.float32) + got[:rows] + across(passed, second).astype(jnp.float32)
-
-    return jnp.concatenate(
-        [
-            two_hops([p[:, :half] for p in parts], 1, 2),
-            two_hops([p[:, half:] for p in parts], 2, 1),
-        ],
-        axis=1,
-    )
-
-
-def over_shard_rows(left, right, shard):
-    rows = left.shape[1] // 4
-    return [
-        over_rows(lax.dynamic_slice_in_dim(left, (shard ^ bits) * rows, rows, 1), right).astype(
-            jnp.bfloat16
-        )
-        for bits in range(4)
-    ]
 
 
 def after(value, *earlier):
@@ -192,25 +153,72 @@
     return jnp.concatenate(kept, axis=-1).reshape(*inner, parts * shards * per_shard * LANES)
 
 
+def unit_pieces(contexts, shards, width, per_shard):
+    found = []
+    for at in range(contexts):
+        first = at * width
+        if first >= per_shard:
+            continue
+        start, stop = min(first, per_shard - width), min(first + width, per_shard)
+        for shard in range(shards):
+            found.append(
+                (
+                    at,
+                    (shard * width + first - start) * LANES,
+                    (stop - first) * LANES,
+                    (shard * per_shard + first) * LANES,
+                )
+            )
+    return found
+
+
+def lay_kernel(pieces, *refs):
+    *sources, out_ref = refs
+    units = out_ref.shape[1] // len(sources)
+    for part, source in enumerate(sources):
+        for at, column, wide, first in pieces:
+            out_ref[:, part * units + first : part * units + first + wide] = source[
+                at, :, column : column + wide
+            ].astype(jnp.float32)
+
+
+def lay_kernel_turned(pieces, source, out_ref):
+    for at, column, wide, first in pieces:
+        out_ref[first : first + wide, :] = source[at, :, column : column + wide].astype(jnp.float32).T
+
+
+def lay(fields, pieces, units, turned=False):
+    rows = fields[0].shape[1]
+    shape = (units, rows) if turned else (rows, len(fields) * units)
+    return pl.pallas_call(
+        functools.partial(lay_kernel_turned if turned else lay_kernel, pieces),
+        in_specs=[pl.BlockSpec(memory_space=pltpu.VMEM)] * len(fields),
+        out_specs=pl.BlockSpec(memory_space=pltpu.VMEM),
+        out_shape=jax.ShapeDtypeStruct(shape, jnp.float32),
+        compiler_params=pltpu.CompilerParams(vmem_limit_bytes=VMEM_LIMIT),
+    )(*fields)
+
+
 def shard_places():
     here = lax.axis_index("shard")
     return here, here + 1 - 2 * lax.rem(here, 2), lax.rem(here + 2, 4), 3 - here
 
 
-def greet(*places):
+def greet(shards, contexts=()):
     barrier = pltpu.get_barrier_semaphore()
-    for place in places:
-        pl.semaphore_signal(barrier, 1, device_id={"shard": place}, device_id_type=MESH)
-    pl.semaphore_wait(barrier, len(places))
-
-
-def to_shard(source, target, send, receive, place):
+    for axis, places in (("shard", shards), ("context", contexts)):
+        for place in places:
+            pl.semaphore_signal(barrier, 1, device_id={axis: place}, device_id_type=MESH)
+    pl.semaphore_wait(barrier, len(shards) + len(contexts))
+
+
+def to_device(axis, source, target, send, receive, place):
     return pltpu.make_async_remote_copy(
         src_ref=source,
         dst_ref=target,
         send_sem=send,
         recv_sem=receive,
-        device_id={"shard": place},
+        device_id={axis: place},
         device_id_type=MESH,
     )
 
@@ -220,7 +228,7 @@
     sources, wholes = refs[:count], refs[count : 2 * count]
     send, receive, local, send_on, receive_on = refs[2 * count :]
     here, along_x, along_y, far = shard_places()
-    greet(along_x, along_y)
+    greet((along_x, along_y))
 
     def block(i, place, start, rows):
         return pl.ds(pl.multiple_of(place * cuts[i][0] + start, 16), rows)
@@ -233,23 +241,23 @@
             kept.append(pltpu.make_async_copy(piece, target, local.at[i, j]))
             kept[-1].start()
             for hop, place in enumerate((along_x, along_y)):
-                sent.append(to_shard(piece, target, send.at[i, j, hop], receive.at[i, j, hop], place))
+                sent.append(to_device("shard", piece, target, send.at[i, j, hop], receive.at[i, j, hop], place))
                 sent[-1].start()
     for i, (rows, pieces) in enumerate(cuts):
         half = rows // 2
         for j, (row, column, wide, into) in enumerate(pieces()):
             for hop, place in enumerate((along_x, along_y)):
                 came = wholes[i].at[block(i, place, 0, rows), pl.ds(into, wide)]
-                to_shard(came, came, send.at[i, j, hop], receive.at[i, j, hop], place).wait_recv()
+                to_device("shard", came, came, send.at[i, j, hop], receive.at[i, j, hop], place).wait_recv()
         for hop, (place, owner, start) in enumerate(((along_x, along_y, 0), (along_y, along_x, half))):
             part = wholes[i].at[block(i, owner, start, half)]
-            sent.append(to_shard(part, part, send_on.at[i, hop], receive_on.at[i, hop], place))
+            sent.append(to_device("shard", part, part, send_on.at[i, hop], receive_on.at[i, hop], place))
             sent[-1].start()
     for i, (rows, pieces) in enumerate(cuts):
         half = rows // 2
         for hop, (place, start) in enumerate(((along_x, 0), (along_y, half))):
             came = wholes[i].at[block(i, far, start, half)]
-            to_shard(came, came, send_on.at[i, hop], receive_on.at[i, hop], place).wait_recv()
+            to_device("shard", came, came, send_on.at[i, hop], receive_on.at[i, hop], place).wait_recv()
     for copy in kept:
         copy.wait()
     for copy in sent:
@@ -278,74 +286,169 @@
     )(*arrays)
 
 
-def product_sum_kernel(left_ref, right_ref, out_ref, own, made, first, passed, last, send, receive):
-    here, along_x, along_y, far = shard_places()
-    rows, wide = out_ref.shape
-    half = wide // 2
-    sides = (pl.ds(0, half), pl.ds(half, half))
-    ways = ((along_x, along_y), (along_y, along_x))
-
-    def product(place, side):
-        columns = pl.ds(pl.multiple_of(place * rows, LANES), rows)
-        return over_rows(left_ref[:, columns], right_ref[:, sides[side]])
-
-    greet(along_x, along_y)
-    copies = []
-
-    def push(source, target, slot, place):
-        copies.append(to_shard(source, target, send.at[slot], receive.at[slot], place))
-        copies[-1].start()
-
-    for side in range(2):
-        made[0, side] = product(far, side).astype(jnp.bfloat16)
-        push(made.at[0, side], passed.at[side], side, ways[side][0])
-    for side in range(2):
-        made[1, side] = product(ways[side][0], side).astype(jnp.bfloat16)
-        push(made.at[1, side], first.at[side], 2 + side, ways[side][0])
-    for side in range(2):
-        kept = product(ways[side][1], side)
-        copies[side].wait_recv()
-        made[2, side] = (kept + passed[side].astype(jnp.float32)).astype(jnp.bfloat16)
-        push(made.at[2, side], last.at[side], 4 + side, ways[side][1])
-    for side in range(2):
-        own[:, sides[side]] = product(here, side)
-    for side in range(2):
-        copies[2 + side].wait_recv()
-        own[:, sides[side]] += first[side].astype(jnp.float32)
-    for side in range(2):
-        copies[4 + side].wait_recv()
-        out_ref[:, sides[side]] = (own[:, sides[side]] + last[side].astype(jnp.float32)).astype(
-            jnp.bfloat16
+class Product:
+    def __init__(self, left, right):
+        self.rows, self.wide = left[1] // 4, right[1]
+        half = -(-self.wide // (2 * LANES)) * LANES
+        self.sides = ((0, half), (half, self.wide - half))
+
+    def scratch(self):
+        shapes = [pltpu.VMEM((self.rows, self.wide), jnp.float32)]
+        for _, wide in self.sides:
+            shapes += [pltpu.VMEM((3, self.rows, wide), jnp.bfloat16)] * 2
+        return shapes + [pltpu.SemaphoreType.DMA((6,)), pltpu.SemaphoreType.DMA((6,))]
+
+    def run(self, left, right, out, own, made_a, came_a, made_b, came_b, send, receive):
+        here, along_x, along_y, far = shard_places()
+        ways = ((along_x, along_y), (along_y, along_x))
+        made, came = (made_a, made_b), (came_a, came_b)
+        columns = [pl.ds(start, wide) for start, wide in self.sides]
+        copies = []
+
+        def product(place, side):
+            block = pl.ds(pl.multiple_of(place * self.rows, LANES), self.rows)
+            return over_rows(left[:, block], right[:, columns[side]])
+
+        def push(step, side, place):
+            slot = 2 * step + side
+            copies.append(
+                to_device(
+                    "shard",
+                    made[side].at[step],
+                    came[side].at[step],
+                    send.at[slot],
+                    receive.at[slot],
+                    place,
+                )
+            )
+            copies[-1].start()
+
+        for side in range(2):
+            made[side][0] = product(far, side).astype(jnp.bfloat16)
+            push(0, side, ways[side][0])
+        for side in range(2):
+            made[side][1] = product(ways[side][0], side).astype(jnp.bfloat16)
+            push(1, side, ways[side][0])
+        for side in range(2):
+            kept = product(ways[side][1], side)
+            copies[side].wait_recv()
+            made[side][2] = (kept + came[side][0].astype(jnp.float32)).astype(jnp.bfloat16)
+            push(2, side, ways[side][1])
+        for side in range(2):
+            own[:, columns[side]] = product(here, side)
+        for side in range(2):
+            copies[2 + side].wait_recv()
+            own[:, columns[side]] += came[side][1].astype(jnp.float32)
+        for side in range(2):
+            copies[4 + side].wait_recv()
+            out[:, columns[side]] = (own[:, columns[side]] + came[side][2].astype(jnp.float32)).astype(
+                jnp.bfloat16
+            )
+        return copies
+
+
+class Exchange:
+    def __init__(self, count, stride):
+        self.count, self.stride = count, stride
+
+    def scratch(self):
+        return [pltpu.SemaphoreType.DMA((self.count,))] * 2 + [pltpu.SemaphoreType.DMA]
+
+    def peers(self):
+        me = lax.axis_index("context")
+        slot, rest = me // self.stride, lax.rem(me, self.stride)
+        places = [lax.rem(slot + k, self.count) for k in range(self.count)]
+        return places, [place * self.stride + rest for place in places]
+
+    def start(self, blocks, out, send, receive, local):
+        slots, devices = self.peers()
+        kept = pltpu.make_async_copy(blocks(slots[0]), out.at[slots[0]], local)
+        kept.start()
+        copies = []
+        for k in range(1, self.count):
+            copies.append(
+                to_device(
+                    "context", blocks(slots[k]), out.at[slots[0]], send.at[k], receive.at[k], devices[k]
+                )
+            )
+            copies[-1].start()
+
+        def finish():
+            kept.wait()
+            for k in range(1, self.count):
+                source = slots[self.count - k]
+                to_device(
+                    "context", out.at[source], out.at[source], send.at[k], receive.at[k], devices[k]
+                ).wait_recv()
+            for copy in copies:
+                copy.wait_send()
+
+        return finish
+
+
+def work_kernel(products, exchanges, chained, *refs):
+    refs = list(refs)
+
+    def take(count):
+        taken = refs[:count]
+        del refs[:count]
+        return taken
+
+    operands = [take(2) for _ in products]
+    arrays = take(len(exchanges) - (1 if chained else 0))
+    results = take(len(products))
+    moved = take(len(exchanges))
+    product_scratch = [take(len(p.scratch())) for p in products]
+    exchange_scratch = [take(len(e.scratch())) for e in exchanges]
+    _, along_x, along_y, _ = shard_places()
+    everyone = max(exchanges, key=lambda e: e.count).peers()[1][1:] if exchanges else []
+    greet((along_x, along_y), everyone)
+    finishes, copies = [], []
+    for exchange, array, out, scratch in zip(exchanges, arrays, moved, exchange_scratch):
+        finishes.append(exchange.start(lambda j, array=array: array.at[j], out, *scratch))
+    for product, (left, right), out, scratch in zip(products, operands, results, product_scratch):
+        copies += product.run(left, right, out, *scratch)
+    if chained:
+        rows = products[0].rows // exchanges[-1].count
+        finishes.append(
+            exchanges[-1].start(
+                lambda j: results[0].at[pl.ds(pl.multiple_of(j * rows, 16), rows)],
+                moved[-1],
+                *exchange_scratch[-1],
+            )
         )
     for copy in copies:
         copy.wait_send()
-
-
-def product_sum(left, right, number):
-    rows, wide = left.shape[1] // 4, right.shape[1]
-    return pl.pallas_call(
-        product_sum_kernel,
-        in_specs=[pl.BlockSpec(memory_space=pltpu.VMEM)] * 2,
-        out_specs=pl.BlockSpec(memory_space=pltpu.VMEM),
-        out_shape=jax.ShapeDtypeStruct((rows, wide), jnp.bfloat16),
-        scratch_shapes=[
-            pltpu.VMEM((rows, wide), jnp.float32),
-            pltpu.VMEM((3, 2, rows, wide // 2), jnp.bfloat16),
-            pltpu.VMEM((2, rows, wide // 2), jnp.bfloat16),
-            pltpu.VMEM((2, rows, wide // 2), jnp.bfloat16),
-            pltpu.VMEM((2, rows, wide // 2), jnp.bfloat16),
-            pltpu.SemaphoreType.DMA((6,)),
-            pltpu.SemaphoreType.DMA((6,)),
-        ],
-        cost_estimate=pl.CostEstimate(
-            flops=2 * left.shape[0] * left.shape[1] * wide,
-            transcendentals=0,
-            bytes_accessed=200 * rows * wide,
-        ),
+    for finish in finishes:
+        finish()
+
+
+def work(number, products=(), exchanges=(), chained=False):
+    contexts = lax.axis_size("context")
+    made = [Product(left.shape, right.shape) for left, right in products]
+    swaps = [Exchange(array.shape[0], contexts // array.shape[0]) for array in exchanges]
+    results = [jax.ShapeDtypeStruct((p.rows, p.wide), jnp.bfloat16) for p in made]
+    moved = [jax.ShapeDtypeStruct(array.shape, array.dtype) for array in exchanges]
+    if chained:
+        swaps.append(Exchange(contexts, 1))
+        moved.append(
+            jax.ShapeDtypeStruct((contexts, made[0].rows // contexts, made[0].wide), jnp.bfloat16)
+        )
+    scratch = [shape for part in made + swaps for shape in part.scratch()]
+    vmem = pl.BlockSpec(memory_space=pltpu.VMEM)
+    hbm = pl.BlockSpec(memory_space=pl.ANY)
+    outs = pl.pallas_call(
+        functools.partial(work_kernel, made, swaps, chained),
+        in_specs=[vmem] * (2 * len(made)) + [hbm] * len(exchanges),
+        out_specs=[vmem] * len(made) + [hbm] * len(swaps),
+        out_shape=results + moved,
+        scratch_shapes=scratch,
+        cost_estimate=pl.CostEstimate(flops=0, transcendentals=0, bytes_accessed=150_000_000),
         compiler_params=pltpu.CompilerParams(
             collective_id=number, has_side_effects=True, vmem_limit_bytes=VMEM_LIMIT
         ),
-    )(left, right)
+    )(*[operand for pair in products for operand in pair], *exchanges)
+    return outs[: len(made)], outs[len(made) :]
 
 
 def masked_weights(q, k, mask):
@@ -613,7 +716,8 @@
     attn_out = swap_rows(
         jnp.dot(mixed_pair, output_half, preferred_element_type=jnp.float32), core
     )
-    resid = source + attn_out + bias_out
+    attn_group = gather(after(attn_in, keyval), "context")
+    resid = source + after(attn_out, attn_group) + bias_out
 
     feed_in = rms_norm(resid, gain_two).astype(jnp.bfloat16)
     mixed_group = gather(mixed_own, "context")
@@ -625,13 +729,21 @@
         1,
     )
     hidden, gate_back, up_back, gate_sums, up_sums = feed(
-        feed_group, grad_group, gate_up_part, down_part, bias_gate_up, unit_live
+        feed_group, after(grad_group, mixed_group), gate_up_part, down_part, bias_gate_up, unit_live
     )
     gate_up_low = jnp.concatenate([gate_back, up_back], axis=1)
     feed_part = against(gate_up_low, gate_up_part).astype(jnp.bfloat16)
     feed_in_grad = lax.psum_scatter(feed_part, "context", scatter_dimension=0, tiled=True)
-    down_sum = product_sum(grad_group, after(hidden, feed_part), 2)
-    feed_in_grad = after(feed_in_grad, down_sum).astype(jnp.float32)
+    (down_sum,), _ = work(2, [(grad_group, after(hidden, feed_part))])
+    down_part_out = jnp.dot(
+        after(hidden, down_sum), down_part, preferred_element_type=jnp.float32
+    ).astype(jnp.bfloat16)
+    feed_in_grad = after(feed_in_grad, down_part_out)
+    down_out = lax.psum_scatter(
+        after(down_part_out, feed_in_grad), "context", scatter_dimension=0, tiled=True
+    ).astype(jnp.float32)
+    block_out = (resid + down_out + bias_down).astype(jnp.bfloat16)
+    feed_in_grad = feed_in_grad.astype(jnp.float32)
 
     grad_out = cotangent.astype(jnp.float32)
     resid_part, gain_two_grad = jax.vjp(rms_norm, resid, gain_two)[1](feed_in_grad)
@@ -644,17 +756,17 @@
     keyval_acc = jnp.stack(
         [key_acc.reshape(contexts // 2, 2 * tok, DH), value_acc.reshape(contexts // 2, 2 * tok, DH)],
         axis=1,
-    ).reshape(2 * group, DH)
-    down_part_out = jnp.dot(
-        after(hidden, keyval_acc), down_part, preferred_element_type=jnp.float32
-    ).astype(jnp.bfloat16)
-    gate_sum = product_sum(feed_group, after(gate_back, keyval_acc), 2)
-    keyval_acc = lax.psum_scatter(keyval_acc, "context", scatter_dimension=0, tiled=True)
-    keyval_acc = after(keyval_acc, gate_sum, down_part_out)
-    down_out = lax.psum_scatter(
-        after(down_part_out, keyval_acc), "context", scatter_dimension=0, tiled=True
-    ).astype(jnp.float32)
-    block_out = (resid + down_out + bias_down).astype(jnp.bfloat16)
+    ).reshape(contexts, 2 * tok, DH).astype(jnp.bfloat16)
+    rows_wide = -(-owned // LANES) * LANES
+    attn_grad_rows = jnp.pad(
+        attn_grad_low.reshape(tok, shards, contexts, owned).transpose(2, 0, 1, 3),
+        ((0, 0), (0, 0), (0, 0), (0, rows_wide - owned)),
+    ).reshape(contexts, tok, shards * rows_wide)
+    (gate_sum,), (keyval_acc, attn_grad_rows) = work(
+        3, [(feed_group, gate_back)], [keyval_acc, attn_grad_rows]
+    )
+    attn_grad_rows = attn_grad_rows.reshape(group, shards * rows_wide)
+    keyval_acc = jnp.sum(keyval_acc.astype(jnp.float32), axis=0)
     keyval_back = jnp.where(core == 0, rotate(keyval_acc, cosine, -sine), keyval_acc).astype(
         jnp.bfloat16
     )
@@ -668,40 +780,27 @@
     input_part, gain_one_grad = jax.vjp(rms_norm, source, gain_one)[1](attn_in_grad)
     input_grad = resid_grad + input_part
 
-    def to_owners(field):
-        return lax.all_to_all(
-            field.reshape(contexts, owned, field.shape[1]), "context", split_axis=0, concat_axis=0
-        ).astype(jnp.float32)
-
-    def whole_units(field):
-        return join_units(to_owners(field), 1, shards, width, per_shard)
-
-    down_weight_grad = whole_units(down_sum).T
-
-    def token_rows(field):
-        return lax.all_to_all(
-            regroup(field, shards, contexts), "context", split_axis=1, concat_axis=0, tiled=True
+    chips = contexts // 2
+
+    def by_chips(field):
+        return field.reshape(2 * tok, chips, field.shape[1] // chips).transpose(1, 0, 2)
+
+    def by_owners(field):
+        return field.reshape(contexts, owned, field.shape[1])
+
+    head_part, keyval_part = query_back.shape[1] // chips, keyval_back.shape[1] // chips
+    spare = max(2 * LANES - head_part - keyval_part, 0)
+    back_cols = jnp.concatenate([by_chips(query_back), by_chips(keyval_back)], axis=2)
+    back_cols = jnp.pad(back_cols, ((0, 0), (0, 0), (0, spare)))
+    moving = [back_cols, by_owners(down_sum), by_owners(gate_sum)]
+    if group <= 1024:
+        (up_sum, output_sum), (back_cols, down_rows, gate_rows) = work(
+            4, [(feed_group, up_back), (attn_grad_rows, mixed_group)], moving
         )
-
-    back_own = jnp.concatenate(
-        [swap_rows(query_back, core), swap_rows(keyval_back, core)], axis=1
-    )
-    back_group = gather(back_own, "context")
-    up_sum = product_sum(feed_group, after(up_back, back_own), 2)
-    back_group = after(back_group, up_sum)
-    gate_up_grad = jnp.concatenate([whole_units(gate_sum), whole_units(up_sum)], axis=1)
-    attn_rows, attn_grad_rows = token_rows(attn_in), token_rows(attn_grad_low)
-    attn_sum = jnp.concatenate(
-        [
-            shard_sum(over_shard_rows(attn_rows, back_group, shard)),
-            shard_sum(over_shard_rows(attn_grad_rows, mixed_group, shard)),
-        ],
-        axis=1,
-    )
-    head_cols = HEADS * DH
-    query_grad = attn_sum[:, :head_cols]
-    keyval_grad = attn_sum[:, head_cols : head_cols + 2 * DH]
-    output_weight_grad = attn_sum[:, head_cols + 2 * DH :].T
+    else:
+        (up_sum,), (back_cols, down_rows, gate_rows) = work(4, [(feed_group, up_back)], moving)
+        (output_sum,), _ = work(6, [(attn_grad_rows, mixed_group)])
+    back_cols = back_cols.reshape(group, back_cols.shape[2])
 
     sums = jnp.concatenate(
         [
@@ -715,18 +814,54 @@
     )
     sums = sums + across(sums, 1)
     sums = sums + across(sums, 2)
-    sums = gather(sums[None], "context")
-    device = shard * contexts + place
-    own = [
-        jnp.sum(
-            lax.dynamic_slice_in_dim(sums[:, i * model : (i + 1) * model], device * owned, owned, 1),
-            axis=0,
+    mine = [
+        lax.dynamic_index_in_dim(
+            sums[i * model : (i + 1) * model].reshape(shards, contexts, owned), shard, 0, False
         )
         for i in range(4)
     ]
-    unit_sums = join_units(sums[:, 4 * model :], 2, shards, width, per_shard)
+    wide = 4 * owned + 2 * units
+    tall = -(-wide // (8 * LANES)) * LANES
+    vectors = jnp.concatenate(
+        mine
+        + [
+            jnp.broadcast_to(sums[4 * model :], (contexts, 2 * units)),
+            jnp.zeros((contexts, 8 * tall - wide), jnp.float32),
+        ],
+        axis=1,
+    ).reshape(contexts, 8, tall)
+    if owned % 16 == 0:
+        _, (up_rows, vectors, back_rows) = work(
+            5, [(attn_group, back_cols)], [by_owners(up_sum), vectors], True
+        )
+    else:
+        (back_sum,), (up_rows, vectors) = work(
+            5, [(attn_group, back_cols)], [by_owners(up_sum), vectors]
+        )
+        _, (back_rows,) = work(7, [], [by_owners(back_sum)])
+    vectors = vectors.reshape(contexts, 8 * tall)
+    own = jnp.sum(vectors[:, : 4 * owned], axis=0).reshape(4, owned)
+    unit_sums = join_units(
+        vectors[:, 4 * owned : wide], 2, shards, width, per_shard
+    )
     unit_owned = 2 * ff // (shards * contexts)
-    gate_up_bias_grad = lax.dynamic_slice_in_dim(unit_sums, device * unit_owned, unit_owned)
+    gate_up_bias_grad = lax.dynamic_slice_in_dim(
+        unit_sums, (shard * contexts + place) * unit_owned, unit_owned
+    )
+    pieces = unit_pieces(contexts, shards, width, per_shard)
+    down_weight_grad = lay([down_rows], pieces, ff, True)
+    gate_up_grad = lay([gate_rows, up_rows], pieces, ff)
+    def by_columns(field):
+        return (
+            field.reshape(chips, 2, owned, field.shape[2])
+            .transpose(2, 1, 0, 3)
+            .reshape(owned, contexts * field.shape[2])
+            .astype(jnp.float32)
+        )
+
+    query_grad = by_columns(back_rows[:, :, :head_part])
+    keyval_grad = by_columns(back_rows[:, :, head_part : head_part + keyval_part])
+    output_weight_grad = output_sum[:owned].astype(jnp.float32).T
     return (
         block_out,
         input_grad,

time: 848 us -> 761 us (0.90)
  Pallas kernels: 398 us -> 494 us
  local copies, waits for them, and re-layouts: 122 us -> 57.5 us
  starting transfers between devices: 57.1 us -> 17.2 us
  matrix products: 69.1 us -> 47 us
  waiting for transfers between devices: 103 us -> 83.3 us
  other arithmetic: 54.1 us -> 35.6 us
  blocking collectives: 14.8 us -> 0 us
    pallas_call x3 -> x6, Pallas kernels: 154 us -> 250 us  [the longest x4 242 us: work(): pl.pallas_call(functools.partial(work_kernel, made, swaps, chained), in_s...]
    all_to_all x5 -> x0, waiting for transfers between devices: 45.1 us -> none  [the longest x3 38.6 us: to_owners(): lax.all_to_all(field.reshape(contexts, owned, field.shape[1]), 'context',...]
    squeeze x28 -> x7, local copies, waits for them, and re-layouts: 35 us -> 0.07 us  [join_units(): kept.append(field[at, ..., (first - start) * LANES:(stop - start) * LANES])]
    all_to_all x5 -> x0, starting transfers between devices: 21.5 us -> none  [the longest x3 13.7 us: to_owners(): lax.all_to_all(field.reshape(contexts, owned, field.shape[1]), 'context',...]
    ppermute x17 -> x9, waiting for transfers between devices: 31.4 us -> 52.2 us  [across(): return lax.ppermute(value, 'shard', [(i, i ^ bit) for i in range(count)])]
    dot_general x9 -> x1, matrix products: 28.3 us -> 9.8 us  [body(): jnp.dot(after(hidden, down_sum), down_part, preferred_element_type=jnp.fl...]
    all_gather x5, waiting for transfers between devices: 8.55 us -> 24.4 us  [gather(): return lax.all_gather(value, axis, axis=0, tiled=True)]
    all_gather x1 -> x0, blocking collectives: 14.8 us -> none  [gather(): return lax.all_gather(value, axis, axis=0, tiled=True)]
  transfers between devices with their start and end apart: 39 -> 23, of which waited for: 16 -> 9; matrix products, arithmetic and copies ran while one was open for 23% -> 14% of each run, Pallas kernels for 43% -> 55%
where the time goes in v3:
time: 761 us; the launch traced here: 751 us
  Pallas kernels  494 us (65%)
  waiting for transfers between devices  83.3 us (11%)
  local copies, waits for them, and re-layouts  57.5 us (8%)
  matrix products  47 us (6%)
  other arithmetic  35.6 us (5%)
  starting transfers between devices  17.2 us (2%)
  between operations  15.8 us (2%)
    pallas_call x4, Pallas kernels, work(): pl.pallas_call(functools.partial(work_kernel, made, swaps, chained), in_s...  242 us
    pallas_call x2, Pallas kernels, gather_cuts(): pl.pallas_call(functools.partial(gather_kernel, cuts), in_specs=[pl.Block...  198 us
    ppermute x9, waiting for transfers between devices, across(): return lax.ppermute(value, 'shard', [(i, i ^ bit) for i in range(count)])  52.2 us
    pallas_call x1, Pallas kernels, feed(): pl.pallas_call(feed_kernel, grid=(blocks, rows // tall), in_specs=[pl.Blo...  27.1 us
    dot_general x4, matrix products, against(): lax.dot_general(left, weight, (((1,), (1,)), ((), ())), preferred_element...  26.9 us
    unnamed x113, local copies, waits for them, and re-layouts  26 us
    all_gather x5, waiting for transfers between devices, gather(): return lax.all_gather(value, axis, axis=0, tiled=True)  24.4 us
  transfers between devices with their start and end apart: 23, of which 9 were waited for; matrix products, arithmetic and copies ran while one was open for 14% of the time, Pallas kernels for 55%

profile of v3, /device:TPU:0, one launch (start us, length us, event | category | flops | bytes accessed | tf_op | source)
XLA Modules:
  0.0 750.7 jit_solution(16934098995985116763)
XLA Ops:
  12.3 3.0 collective-permute-start
  19.1 2.8 collective-permute-done.2
  23.3 67.7 %shard_map.220 = (bf16[2560,256]{1,0:T(8,128)(2,1)}, bf16[2560,1280]{1,0:T(8,128)(2,1)}) custom-call(bf16[640,512]{1,0:T(8,128)(2,1)} %refs_0_.1, bf16[640,2560]{1,0:T(8,128)(2,1)} %refs_1_.1), custom_call_target="tpu_custom_call" | custom-call | bytes 78643200 | tf_op jit(solution)/shard_map/pallas_call | solution.py:270
  91.1 2.3 fusion.38
  94.5 24.3 %all-gather.8.cloned.1.call-done = bf16[2048,256]{0,1:T(8,128)(2,1)} async-done(((bf16[256,256]{0,1:T(8,128)(2,1)}), bf16[2048,256]{0,1:T(8,128)(2,1)}) %all-gather.8.cloned.1.call-update) | async-done | bytes 1048592 | tf_op jit(solution)/shard_map/all_gather | solution.py:68
  123.3 6.1 fusion.39
  133.0 3.5 copy.73
  138.5 7.6 %shard_map.221 = bf16[256,1280]{1,0:T(8,128)(2,1)} custom-call(f32[256,1024]{1,0:T(8,128)} %fusion.28.mask_ref, bf16[256,1280]{1,0:T(8,128)(2,1)} %copy.55.q_ref, bf16[1024,256]{1,0:T(8,128)(2,1)} %bitcast.79, bf16[1024,256]{1,0:T(8,128)(2,1)} %bitcast.81), custom_call_target="tpu_custom_call" | custom-call | tf_op jit(solution)/shard_map/pallas_call | solution.py:473
  154.3 36.1 %collective-permute-done.7 = bf16[640,1280]{1,0:T(8,128)(2,1)} collective-permute-done((bf16[640,1280]{1,0:T(8,128)(2,1)S(1)}, bf16[640,1280]{1,0:T(8,128)(2,1)}, u32[]{:S(2)}, u32[]{:S(2)}) %collective-permute-start.7) | collective-permute-done | bytes 1638432 | tf_op jit(solution)/shard_map/ppermute | solution.py:73
  199.8 11.4 %collective-permute-done.8 = bf16[320,1280]{1,0:T(8,128)(2,1)S(1)} collective-permute-done((bf16[320,1280]{1,0:T(8,128)(2,1)S(1)}, bf16[320,1280]{1,0:T(8,128)(2,1)S(1)}, u32[]{:S(2)}, u32[]{:S(2)}) %collective-permute-start.8) | collective-permute-done | bytes 819232 | tf_op jit(solution)/shard_map/ppermute | solution.py:73
  223.3 130.3 %shard_map.222 = (bf16[2560,2048]{1,0:T(8,128)(2,1)}, bf16[1024,2560]{1,0:T(8,128)(2,1)}) custom-call(bf16[640,15360]{1,0:T(8,128)(2,1)} %refs_0_.2, bf16[1920,2560]{1,0:T(8,128)(2,1)} %refs_1_.2), custom_call_target="tpu_custom_call" | custom-call | bytes 157286400 | tf_op jit(solution)/shard_map/pallas_call | solution.py:270
  353.7 27.1 %shard_map.223 = (bf16[1024,1024]{1,0:T(8,128)(2,1)}, bf16[1024,1024]{1,0:T(8,128)(2,1)}, bf16[1024,1024]{1,0:T(8,128)(2,1)}, f32[1,1024]{1,0:T(1,128)}, f32[1,1024]{1,0:T(1,128)}) custom-call(bf16[1024,2560]{1,0:T(8,128)(2,1)} %all-gather.12.cloned.1.call-done.feed_ref.refs_0_, bf16[1024,2560]{1,0:T(8,128)(2,1)} %all-gather.6.cloned.1.call-done.grad_ref.refs_0_, ...), custom_call_target="tpu_custom_call" | custom-call | tf_op jit(solution)/shard_map/pallas_call | solution.py:583
  380.8 16.6 %convolution_convert_fusion.1 = bf16[1024,2560]{1,0:T(8,128)(2,1)} fusion(bf16[2560,2048]{1,0:T(8,128)(2,1)} %get-tuple-element.55.gate_ref.up_ref, bf16[1024,1024]{1,0:T(8,128)(2,1)} %get-tuple-element.59.refs_1_, bf16[1024,1024]{1,0:T(8,128)(2,1)} %get-tuple-element.58.refs_1_), kind=kOutput, calls=%fused_computation.1 | convolution fusion | flops 10748428288 | bytes 19922944 | tf_op jit(solution)/shard_map/dot_general | solution.py:55
  397.9 50.5 %shard_map.224 = bf16[640,1024]{1,0:T(8,128)(2,1)} custom-call(bf16[1024,2560]{1,0:T(8,128)(2,1)} %all-gather.6.cloned.1.call-done.grad_ref.refs_0_, bf16[1024,1024]{1,0:T(8,128)(2,1)} %get-tuple-element.61.refs_1_), custom_call_target="tpu_custom_call" | custom-call | bytes 150000000 | tf_op jit(solution)/shard_map/pallas_call | solution.py:440
  448.4 9.8 %convolution_convert_fusion = bf16[1024,2560]{1,0:T(8,128)(2,1)} fusion(bf16[1024,1024]{1,0:T(8,128)(2,1)S(1)} %copy-done.12, bf16[1024,2560]{1,0:T(8,128)(2,1)} %get-tuple-element.56.down_ref), kind=kOutput, calls=%fused_computation | convolution fusion | flops 5371330560 | bytes 12582912 | tf_op jit(solution)/shard_map/dot_general | solution.py:738
  463.3 4.9 fusion.29
  471.4 2.3 copy.75
  473.8 2.8 pad.4.clone
  476.5 2.3 reshape.298.refs_3_
  478.8 3.1 add_convert_fusion.g_ref
  482.0 11.2 %shard_map.225 = (f32[256,1280]{1,0:T(8,128)}, f32[1024,256]{1,0:T(8,128)}, f32[1024,256]{1,0:T(8,128)}) custom-call(f32[256,1024]{1,0:T(8,128)} %fusion.28.mask_ref, bf16[256,1280]{1,0:T(8,128)(2,1)} %copy.55.q_ref, bf16[1024,256]{1,0:T(8,128)(2,1)} %bitcast.80, bf16[1024,256]{1,0:T(8,128)(2,1)} %bitcast.82, bf16[256,1280]{1,0:T(8,128)(2,1)} %add_convert_fusion.g_ref), custom_call_target="tpu_custom_call" | custom-call | tf_op jit(solution)/shard_map/pallas_call | solution.py:514
  495.8 58.6 %shard_map.226 = (bf16[640,1024]{1,0:T(8,128)(2,1)}, bf16[8,256,256]{2,1,0:T(8,128)(2,1)}, bf16[8,128,512]{2,1,0:T(8,128)(2,1)}) custom-call(bf16[1024,2560]{1,0:T(8,128)(2,1)} %all-gather.12.cloned.1.call-done.feed_ref.refs_0_, bf16[1024,1024]{1,0:T(8,128)(2,1)} %get-tuple-element.58.refs_1_, bf16[8,256,256]{2,1,0:T(8,128)(2,1)} %bitcast.83, ...), custom_call_target="tpu_custom_call" | custom-call | bytes 150000000 | tf_op jit(solution)/shard_map/pallas_call | solution.py:440
  556.6 2.8 copy.57
  562.1 4.9 fusion.66
  569.5 2.6 collective-permute-start.13
  575.1 3.5 fusion.8
  578.7 4.0 fusion.11
  585.4 83.7 %shard_map.227 = (bf16[640,1024]{1,0:T(8,128)(2,1)}, bf16[128,2560]{1,0:T(8,128)(2,1)}, bf16[4,256,384]{2,1,0:T(8,128)(2,1)}, bf16[8,80,1024]{2,1,0:T(8,128)(2,1)}, bf16[8,80,1024]{2,1,0:T(8,128)(2,1)}) custom-call(bf16[1024,2560]{1,0:T(8,128)(2,1)} %all-gather.12.cloned.1.call-done.feed_ref.refs_0_, bf16[1024,1024]{1,0:T(8,128)(2,1)} %get-tuple-element.59.refs_1_, ...), custom_call_target="tpu_custom_call" | custom-call | bytes 150000000 | tf_op jit(solution)/shard_map/pallas_call | solution.py:440
  672.6 3.8 shard_map.230
  676.4 5.1 copy.71
  682.7 49.4 %shard_map.228 = (bf16[640,384]{1,0:T(8,128)(2,1)}, bf16[8,80,1024]{2,1,0:T(8,128)(2,1)}, f32[8,8,384]{2,1,0:T(8,128)}, bf16[8,80,384]{2,1,0:T(8,128)(2,1)}) custom-call(bf16[1024,2560]{1,0:T(8,128)(2,1)} %all-gather.10.cloned.1.call-done.refs_0_, bf16[1024,384]{1,0:T(8,128)(2,1)} %bitcast.100, bf16[8,80,1024]{2,1,0:T(8,128)(2,1)} %bitcast.92, ...), custom_call_target="tpu_custom_call" | custom-call | bytes 150000000 | tf_op jit(solution)/shard_map/pallas_call | solution.py:440
  739.2 4.3 shard_map.229
  (267 shorter events, 86.5 us)
Async XLA Ops:
  7.2 15.7 %copy-start.1 = (bf16[128,2560]{1,0:T(8,128)(2,1)S(1)}, bf16[128,2560]{1,0:T(8,128)(2,1)}, u32[]{:S(2)}) copy-start(bf16[128,2560]{1,0:T(8,128)(2,1)} %param.13) | copy-start | bytes 1966084
  7.2 87.2 %all-gather.6.cloned.1.call-start = ((), (), s32[]{:S(2)}) async-start(), calls=%async_computation.2 | async-start | bytes 5898240 | tf_op jit(solution)/shard_map/all_gather | solution.py:68
  7.9 110.9 %all-gather.8.cloned.1.call-start = ((), (), s32[]{:S(2)}) async-start(), calls=%async_computation.3 | async-start | bytes 1179648 | tf_op jit(solution)/shard_map/all_gather | solution.py:68
  12.3 5.8 collective-permute-start
  15.3 3.8 collective-permute-start.1
  18.1 73.0 %copy-start.40 = (f32[128]{0:T(128)}, f32[128]{0:T(128)S(1)}, u32[]{:S(2)}) copy-start(f32[128]{0:T(128)S(1)} %fusion.12) | copy-start | bytes 1540
  18.1 3.8 collective-permute-start.2
  19.0 72.0 %copy-start.32 = (f32[128]{0:T(128)}, f32[128]{0:T(128)S(1)}, u32[]{:S(2)}) copy-start(f32[128]{0:T(128)S(1)} %fusion.51) | copy-start | bytes 1540
  22.9 68.2 %copy-start.24 = (f32[2560]{0:T(1024)}, f32[2560]{0:T(1024)S(1)}, u32[]{:S(2)}) copy-start(f32[2560]{0:T(1024)S(1)} %mul.275) | copy-start | bytes 30724
  23.1 68.0 %copy-start.9 = (bf16[128,2560]{1,0:T(8,128)(2,1)}, bf16[128,2560]{1,0:T(8,128)(2,1)S(1)}, u32[]{:S(2)}) copy-start(bf16[128,2560]{1,0:T(8,128)(2,1)S(1)} %fusion.7) | copy-start | bytes 1966084
  23.2 67.9 %collective-permute-start.3 = (bf16[128,2560]{1,0:T(8,128)(2,1)S(1)}, bf16[128,2560]{1,0:T(8,128)(2,1)S(1)}, u32[]{:S(2)}, u32[]{:S(2)}) collective-permute-start(bf16[128,2560]{1,0:T(8,128)(2,1)S(1)} %fusion.7), channel_id=1, source_target_pairs={{0,1},{1,0},{2,3},{3,2},{4,5},{5,4},{6,7},{7,6},{8,9},{9,8},{10,11... | collective-permute-start | bytes 1966088 | tf_op jit(solution)/shard_map/ppermute | solution.py:101
  23.3 97.6 %copy-start.34 = (f32[64]{0:T(128)}, f32[64]{0:T(128)S(1)}, u32[]{:S(2)}) copy-start(f32[64]{0:T(128)S(1)} %multiply_exponential_fusion) | copy-start | bytes 772
  94.5 26.3 %copy-start.31 = (s32[1024]{0:T(1024)S(1)}, s32[1024]{0:T(1024)}, u32[]{:S(2)}) copy-start(s32[1024]{0:T(1024)} %param.14) | copy-start | bytes 12292
  94.5 126.1 %all-gather.10.cloned.1.call-start = ((), (), s32[]{:S(2)}) async-start(), calls=%async_computation.4 | async-start | bytes 5898240 | tf_op jit(solution)/shard_map/all_gather | solution.py:68
  120.7 232.9 %all-gather.14.cloned.1.call-start = ((), (), s32[]{:S(2)}) async-start(), calls=%async_computation.6 | async-start | bytes 5898240 | tf_op jit(solution)/shard_map/all_gather | solution.py:68
  147.2 1.7 collective-permute-start.4
  149.9 203.8 %all-gather.12.cloned.1.call-start = ((), (), s32[]{:S(2)}) async-start(), calls=%async_computation.5 | async-start | bytes 5898240 | tf_op jit(solution)/shard_map/all_gather | solution.py:68
  152.3 38.1 %collective-permute-start.7 = (bf16[640,1280]{1,0:T(8,128)(2,1)S(1)}, bf16[640,1280]{1,0:T(8,128)(2,1)}, u32[]{:S(2)}, u32[]{:S(2)}) collective-permute-start(bf16[640,1280]{1,0:T(8,128)(2,1)S(1)} %slice_select_fusion), channel_id=1, source_target_pairs={{0,16},{8,24},{16,0},{24,8},{1,17},{9,25},{17,1},{25,9},{2,18},{10... | collective-permute-start | bytes 4915208 | tf_op jit(solution)/shard_map/ppermute | solution.py:73
  152.9 39.5 %collective-permute-start.6 = (bf16[640,1280]{1,0:T(8,128)(2,1)S(1)}, bf16[640,1280]{1,0:T(8,128)(2,1)}, u32[]{:S(2)}, u32[]{:S(2)}) collective-permute-start(bf16[640,1280]{1,0:T(8,128)(2,1)S(1)} %slice_select_fusion), channel_id=1, source_target_pairs={{0,8},{8,0},{16,24},{24,16},{1,9},{9,1},{17,25},{25,17},{2,10},{10... | collective-permute-start | bytes 4915208 | tf_op jit(solution)/shard_map/ppermute | solution.py:73
  191.6 19.6 %collective-permute-start.8 = (bf16[320,1280]{1,0:T(8,128)(2,1)S(1)}, bf16[320,1280]{1,0:T(8,128)(2,1)S(1)}, u32[]{:S(2)}, u32[]{:S(2)}) collective-permute-start(bf16[320,1280]{1,0:T(8,128)(2,1)S(1)} %slice.199), channel_id=1, source_target_pairs={{0,8},{8,0},{16,24},{24,16},{1,9},{9,1},{17,25},{25,17},{2,10},{10... | collective-permute-start | bytes 2457608 | tf_op jit(solution)/shard_map/ppermute | solution.py:73
  193.6 19.6 %collective-permute-start.9 = (bf16[320,1280]{1,0:T(8,128)(2,1)S(1)}, bf16[320,1280]{1,0:T(8,128)(2,1)S(1)}, u32[]{:S(2)}, u32[]{:S(2)}) collective-permute-start(bf16[320,1280]{1,0:T(8,128)(2,1)S(1)} %slice.200), channel_id=1, source_target_pairs={{0,16},{8,24},{16,0},{24,8},{1,17},{9,25},{17,1},{25,9},{2,18},{10... | collective-permute-start | bytes 2457608 | tf_op jit(solution)/shard_map/ppermute | solution.py:73
  196.6 16.7 %collective-permute-start.5 = (bf16[128,2560]{1,0:T(8,128)(2,1)S(1)}, bf16[128,2560]{1,0:T(8,128)(2,1)S(1)}, u32[]{:S(2)}, u32[]{:S(2)}) collective-permute-start(bf16[128,2560]{1,0:T(8,128)(2,1)S(1)} %copy-done.11), channel_id=1, source_target_pairs={{0,1},{1,0},{2,3},{3,2},{4,5},{5,4},{6,7},{7,6},{8,9},{9,8},{10,11... | collective-permute-start | bytes 1966088 | tf_op jit(solution)/shard_map/ppermute | solution.py:101
  216.1 2.2 collective-permute-start.10
  220.9 239.5 %copy-start.29 = (f32[128]{0:T(128)}, f32[128]{0:T(128)S(1)}, u32[]{:S(2)}) copy-start(f32[128]{0:T(128)S(1)} %fusion.52) | copy-start | bytes 1540
  222.0 236.3 %reduce-scatter.3.cloned.1.call-start = ((), (), s32[]{:S(2)}) async-start(), calls=%async_computation.7 | async-start | bytes 5898240 | tf_op jit(solution)/shard_map/reduce_scatter | solution.py:736
  397.4 181.2 %reduce-scatter.5.cloned.1.call-start = ((), (), s32[]{:S(2)}) async-start(), calls=%async_computation.8 | async-start | bytes 5898240 | tf_op jit(solution)/shard_map/reduce_scatter | solution.py:742
  397.9 50.5 %copy-start.12 = (bf16[1024,1024]{1,0:T(8,128)(2,1)S(1)}, bf16[1024,1024]{1,0:T(8,128)(2,1)}, u32[]{:S(2)}) copy-start(bf16[1024,1024]{1,0:T(8,128)(2,1)} %get-tuple-element.61.refs_1_) | copy-start | bytes 6291460
  461.6 1.7 collective-permute-start.11
  470.2 8.7 %collective-permute-start.12 = (f32[256,1280]{1,0:T(8,128)}, f32[256,1280]{1,0:T(8,128)}, u32[]{:S(2)}, u32[]{:S(2)}) collective-permute-start(f32[256,1280]{1,0:T(8,128)} %slice_select_fusion.2), channel_id=1, source_target_pairs={{0,1},{1,0},{2,3},{3,2},{4,5},{5,4},{6,7},{7,6},{8,9},{9,8},{10,11... | collective-permute-start | bytes 3932168 | tf_op jit(solution)/shard_map/ppermute | solution.py:101
  569.5 5.6 collective-permute-start.13
  582.8 86.3 %collective-permute-start.14 = (f32[12288]{0:T(1024)S(1)}, f32[12288]{0:T(1024)S(1)}, u32[]{:S(2)}, u32[]{:S(2)}) collective-permute-start(f32[12288]{0:T(1024)S(1)} %constant_dynamic-update-slice_fusion.9), channel_id=1, source_target_pairs={{0,8},{8,0},{16,24},{24,16},{1,9},{9,1},{17,25},{25,17},{2,10},{10... | collective-permute-start | bytes 147464 | tf_op jit(solution)/shard_map/ppermute | solution.py:73
  669.1 12.4 %collective-permute-start.15 = (f32[12288]{0:T(1024)S(1)}, f32[12288]{0:T(1024)S(1)}, u32[]{:S(2)}, u32[]{:S(2)}) collective-permute-start(f32[12288]{0:T(1024)S(1)} %add.191), channel_id=1, source_target_pairs={{0,16},{8,24},{16,0},{24,8},{1,17},{9,25},{17,1},{25,9},{2,18},{10... | collective-permute-start | bytes 147464 | tf_op jit(solution)/shard_map/ppermute | solution.py:73
  (34 other events, 116.3 us)
Sparse Core Ops, SparseCore 0:
  9.7 58.7 all-gather.5
  94.6 24.2 all-gather.7
  121.1 54.6 all-gather.9
  177.8 54.8 all-gather.13
  234.7 54.8 all-gather.11
  397.5 59.0 reduce-scatter.2
  458.9 69.7 reduce-scatter.4

commit v4 on v3

--- a/solution.py
+++ b/solution.py
@@ -73,25 +73,6 @@
     return lax.ppermute(value, "shard", [(i, i ^ bit) for i in range(count)])
 
 
-def shard_gather(block, shard):
-    rows = block.shape[0]
-    near, next_near = across(block, 1), across(block, 2)
-    far = jnp.concatenate(
-        [across(next_near[: rows // 2], 1), across(near[rows // 2 :], 2)], axis=0
-    )
-    whole = jnp.zeros((4 * rows, block.shape[1]), block.dtype)
-    for bits, part in enumerate((block, near, next_near, far)):
-        whole = lax.dynamic_update_slice_in_dim(whole, part, (shard ^ bits) * rows, 0)
-    return whole
-
-
-def vector_gather(own, shard):
-    near, next_near = across(own, 1), across(own, 2)
-    far = across(near, 2)
-    found = jnp.stack([own, near, next_near, far])
-    return jnp.stack([lax.dynamic_index_in_dim(found, shard ^ j, 0, False) for j in range(4)])
-
-
 def after(value, *earlier):
     return lax.optimization_barrier((value, *earlier))[0]
 
@@ -99,13 +80,6 @@
 def sibling(value):
     count = lax.axis_size("context")
     return lax.ppermute(value, "context", [(i, i ^ 1) for i in range(count)])
-
-
-def pair_rows(own, core):
-    other = sibling(own)
-    return jnp.where(
-        core == 0, jnp.concatenate([own, other], axis=0), jnp.concatenate([other, own], axis=0)
-    )
 
 
 def halves(value, core, axis):
@@ -223,67 +197,321 @@
     )
 
 
-def gather_kernel(cuts, *refs):
-    count = len(cuts)
-    sources, wholes = refs[:count], refs[count : 2 * count]
-    send, receive, local, send_on, receive_on = refs[2 * count :]
-    here, along_x, along_y, far = shard_places()
-    greet((along_x, along_y))
-
-    def block(i, place, start, rows):
-        return pl.ds(pl.multiple_of(place * cuts[i][0] + start, 16), rows)
-
-    kept, sent = [], []
-    for i, (rows, pieces) in enumerate(cuts):
-        for j, (row, column, wide, into) in enumerate(pieces()):
-            piece = sources[i].at[pl.ds(row, rows), pl.ds(column, wide)]
-            target = wholes[i].at[block(i, here, 0, rows), pl.ds(into, wide)]
-            kept.append(pltpu.make_async_copy(piece, target, local.at[i, j]))
-            kept[-1].start()
-            for hop, place in enumerate((along_x, along_y)):
-                sent.append(to_device("shard", piece, target, send.at[i, j, hop], receive.at[i, j, hop], place))
-                sent[-1].start()
-    for i, (rows, pieces) in enumerate(cuts):
-        half = rows // 2
-        for j, (row, column, wide, into) in enumerate(pieces()):
-            for hop, place in enumerate((along_x, along_y)):
-                came = wholes[i].at[block(i, place, 0, rows), pl.ds(into, wide)]
-                to_device("shard", came, came, send.at[i, j, hop], receive.at[i, j, hop], place).wait_recv()
-        for hop, (place, owner, start) in enumerate(((along_x, along_y, 0), (along_y, along_x, half))):
-            part = wholes[i].at[block(i, owner, start, half)]
-            sent.append(to_device("shard", part, part, send_on.at[i, hop], receive_on.at[i, hop], place))
-            sent[-1].start()
-    for i, (rows, pieces) in enumerate(cuts):
-        half = rows // 2
-        for hop, (place, start) in enumerate(((along_x, 0), (along_y, half))):
-            came = wholes[i].at[block(i, far, start, half)]
-            to_device("shard", came, came, send_on.at[i, hop], receive_on.at[i, hop], place).wait_recv()
-    for copy in kept:
+class Gather:
+    def __init__(self, rows, pieces):
+        self.rows, self.pieces = rows, pieces
+
+    def scratch(self):
+        most = 2 * (len(self.pieces()) // 2) or 1
+        return [
+            pltpu.SemaphoreType.DMA((most, 2)),
+            pltpu.SemaphoreType.DMA((most, 2)),
+            pltpu.SemaphoreType.DMA((most,)),
+            pltpu.SemaphoreType.DMA((2,)),
+            pltpu.SemaphoreType.DMA((2,)),
+        ]
+
+    def bind(self, source, whole, send, receive, local, send_on, receive_on):
+        self.source, self.whole, self.local = source, whole, local
+        self.send, self.receive, self.send_on, self.receive_on = send, receive, send_on, receive_on
+        self.here, along_x, along_y, self.far = shard_places()
+        self.near = (along_x, along_y)
+        self.kept, self.sent = [], []
+
+    def block(self, place, start, rows):
+        return pl.ds(pl.multiple_of(place * self.rows + start, 16), rows)
+
+    def post(self):
+        for j, (row, column, wide, into) in enumerate(self.pieces()):
+            piece = self.source.at[pl.ds(row, self.rows), pl.ds(column, wide)]
+            target = self.whole.at[self.block(self.here, 0, self.rows), pl.ds(into, wide)]
+            self.kept.append(pltpu.make_async_copy(piece, target, self.local.at[j]))
+            self.kept[-1].start()
+            for hop, place in enumerate(self.near):
+                self.push(piece, target, self.send.at[j, hop], self.receive.at[j, hop], place)
+
+    def push(self, source, target, send, receive, place):
+        self.sent.append(to_device("shard", source, target, send, receive, place))
+        self.sent[-1].start()
+
+    def pass_on(self):
+        half = self.rows // 2
+        for j, (_, _, wide, into) in enumerate(self.pieces()):
+            for hop, place in enumerate(self.near):
+                came = self.whole.at[self.block(place, 0, self.rows), pl.ds(into, wide)]
+                to_device(
+                    "shard", came, came, self.send.at[j, hop], self.receive.at[j, hop], place
+                ).wait_recv()
+        for hop in range(2):
+            part = self.whole.at[self.block(self.near[1 - hop], hop * half, half)]
+            self.push(part, part, self.send_on.at[hop], self.receive_on.at[hop], self.near[hop])
+
+    def finish(self):
+        half = self.rows // 2
+        for hop in range(2):
+            came = self.whole.at[self.block(self.far, hop * half, half)]
+            to_device(
+                "shard", came, came, self.send_on.at[hop], self.receive_on.at[hop], self.near[hop]
+            ).wait_recv()
+        for copy in self.kept:
+            copy.wait()
+
+    def close(self):
+        for copy in self.sent:
+            copy.wait_send()
+
+
+class Spread:
+    def __init__(self, chips):
+        self.chips = chips
+
+    def scratch(self):
+        return [pltpu.SemaphoreType.DMA((self.chips,))] * 4 + [pltpu.SemaphoreType.DMA]
+
+    def bind(self, own, group, send, receive, send_on, receive_on, local):
+        self.own, self.group, self.local = own, group, local
+        self.send, self.receive, self.send_on, self.receive_on = send, receive, send_on, receive_on
+        self.me = lax.axis_index("context")
+        self.chip, self.core = self.me // 2, lax.rem(self.me, 2)
+        self.mate = self.me + 1 - 2 * self.core
+        self.sent = []
+
+    def push(self, source, target, send, receive, place):
+        self.sent.append(to_device("context", source, target, send, receive, place))
+        self.sent[-1].start()
+
+    def came(self, k, core):
+        return 2 * lax.rem(self.chip + self.chips - k, self.chips) + core
+
+    def post(self):
+        self.kept = pltpu.make_async_copy(self.own, self.group.at[self.me], self.local)
+        self.kept.start()
+        for k in range(1, self.chips):
+            place = 2 * lax.rem(self.chip + k, self.chips) + self.core
+            self.push(self.own, self.group.at[self.me], self.send.at[k], self.receive.at[k], place)
+        self.push(
+            self.own, self.group.at[self.me], self.send_on.at[0], self.receive_on.at[0], self.mate
+        )
+
+    def pass_on(self):
+        for k in range(1, self.chips):
+            block = self.group.at[self.came(k, self.core)]
+            to_device(
+                "context", block, block, self.send.at[k], self.receive.at[k], self.mate
+            ).wait_recv()
+            self.push(block, block, self.send_on.at[k], self.receive_on.at[k], self.mate)
+
+    def finish(self):
+        self.kept.wait()
+        for k in range(self.chips):
+            block = self.group.at[self.came(k, 1 - self.core)]
+            to_device(
+                "context", block, block, self.send_on.at[k], self.receive_on.at[k], self.mate
+            ).wait_recv()
+        for copy in self.sent:
+            copy.wait_send()
+
+
+def opening_kernel(gathers, spreads, *refs):
+    refs = list(refs)
+
+    def take(count):
+        taken = refs[:count]
+        del refs[:count]
+        return taken
+
+    sources = take(len(gathers))
+    source_ref, mask_ref, cosine_ref, sine_ref = take(4)
+    wholes = take(len(gathers))
+    queries_ref, keyval_ref, resid_ref = take(3)
+    groups = take(2)
+    pair, attn, small, big, keyval, mixed, mixed_own, feed_own, out, out_came, vectors = take(11)
+    swap_send, swap_receive, load, keyval_send, keyval_receive = take(5)
+    for gather_of, source, whole in zip(gathers, sources, wholes):
+        gather_of.bind(source, whole, *take(5))
+    for spread, own, group in zip(spreads, (mixed_own, feed_own), groups):
+        spread.bind(own, group, *take(5))
+    me, contexts = lax.axis_index("context"), lax.axis_size("context")
+    chip, core = me // 2, lax.rem(me, 2)
+    mate = me + 1 - 2 * core
+    tok, model = source_ref.shape
+    rows = 2 * tok
+    half = model // 2
+    others = [lax.rem(me + k, contexts) for k in range(1, contexts)]
+    greet(gathers[0].near, others)
+    vector_of, keyval_of, query_of, output_of, gate_up_of, down_of = gathers
+    swaps = []
+
+    def swap(step, source, target):
+        swaps.append(
+            to_device("context", source, target, swap_send.at[step], swap_receive.at[step], mate)
+        )
+        swaps[-1].start()
+
+    def fetch(step, whole, target):
+        copy = pltpu.make_async_copy(whole, target, load.at[step])
+        copy.start()
         copy.wait()
-    for copy in sent:
+
+    vector_of.post()
+    keyval_of.post()
+    query_of.post()
+    pair[core] = source_ref[...]
+    swap(0, source_ref, pair.at[core])
+
+    vector_of.pass_on()
+    vector_of.finish()
+    fetch(0, vector_of.whole, vectors)
+
+    def vector(row):
+        tall = vector_of.rows
+        return jnp.concatenate(
+            [vectors[j * tall + row : j * tall + row + 1, :] for j in range(4)], axis=1
+        ).astype(jnp.float32)
+
+    swaps[0].wait_recv()
+    attn[...] = rms_norm(
+        pair[...].reshape(rows, model).astype(jnp.float32), vector(0)
+    ).astype(jnp.bfloat16)
+
+    keyval_of.pass_on()
+    keyval_of.finish()
+    fetch(1, keyval_of.whole, small)
+    cosine, sine = cosine_ref[...], sine_ref[...]
+
+    def turned(field):
+        return field * cosine + pltpu.roll(field, DH // 4, 1) * sine
+
+    raw = jnp.dot(attn[...], small[...], preferred_element_type=jnp.float32)
+    at = pl.ds(pl.multiple_of(chip * rows, rows), rows)
+    keyval[core, at, : DH // 2] = jnp.where(
+        core == 0, turned(raw[:, : DH // 2]), raw[:, : DH // 2]
+    ).astype(jnp.bfloat16)
+    keyval[core, at, DH // 2 :] = raw[:, DH // 2 :].astype(jnp.bfloat16)
+    keyval_sent = []
+    for k in range(1, contexts):
+        block = keyval.at[core, at]
+        keyval_sent.append(
+            to_device(
+                "context", block, block, keyval_send.at[k], keyval_receive.at[k], others[k - 1]
+            )
+        )
+        keyval_sent[-1].start()
+
+    query_of.pass_on()
+    query_of.finish()
+    output_of.post()
+    fetch(2, query_of.whole, big)
+    heads = half // DH
+    for h in range(heads):
+        raw = jnp.dot(
+            attn[...], big[:, h * DH : (h + 1) * DH], preferred_element_type=jnp.float32
+        ) * DH ** (-0.5)
+        queries_ref[:, h * DH : h * DH + DH // 2] = turned(raw[:, : DH // 2]).astype(jnp.bfloat16)
+        queries_ref[:, h * DH + DH // 2 : (h + 1) * DH] = raw[:, DH // 2 :].astype(jnp.bfloat16)
+    for k in range(1, contexts):
+        place = lax.rem(me + contexts - k, contexts)
+        block = keyval.at[
+            lax.rem(place, 2), pl.ds(pl.multiple_of((place // 2) * rows, rows), rows)
+        ]
+        to_device(
+            "context", block, block, keyval_send.at[k], keyval_receive.at[k], others[k - 1]
+        ).wait_recv()
+    for h in range(heads):
+        weights = masked_weights(queries_ref[:, h * DH : (h + 1) * DH], keyval[0], mask_ref[...])
+        mixed[core, :, h * DH : (h + 1) * DH] = jnp.dot(
+            weights.astype(jnp.bfloat16), keyval[1], preferred_element_type=jnp.float32
+        ).astype(jnp.bfloat16)
+    swap(1, mixed.at[core], mixed.at[core])
+
+    output_of.pass_on()
+    output_of.finish()
+    gate_up_of.post()
+    down_of.post()
+    fetch(3, output_of.whole, big)
+    swaps[1].wait_recv()
+    out[...] = jnp.dot(mixed[0], big[:half], preferred_element_type=jnp.float32) + jnp.dot(
+        mixed[1], big[half:], preferred_element_type=jnp.float32
+    )
+    mine = pl.ds(pl.multiple_of(core * tok, tok), tok)
+    theirs = pl.ds(pl.multiple_of((1 - core) * tok, tok), tok)
+    swap(2, out.at[theirs], out_came)
+    mixed_own[:, :half] = mixed[0, mine]
+    mixed_own[:, half:] = mixed[1, mine]
+    swaps[2].wait_recv()
+    low = jnp.where(core == 0, out[mine], out_came[...])
+    high = jnp.where(core == 0, out_came[...], out[mine])
+    resid = (
+        source_ref[...].astype(jnp.float32) + jnp.concatenate([low, high], axis=1) + vector(1)
+    )
+    resid_ref[...] = resid
+    feed_own[...] = rms_norm(resid, vector(2)).astype(jnp.bfloat16)
+    spreads[1].post()
+    spreads[0].post()
+    keyval_ref[...] = keyval[...]
+    gate_up_of.pass_on()
+    down_of.pass_on()
+    spreads[1].pass_on()
+    spreads[0].pass_on()
+    for part in spreads:
+        part.finish()
+    gate_up_of.finish()
+    down_of.finish()
+    for gather_of in gathers:
+        gather_of.close()
+    for copy in swaps + keyval_sent:
         copy.wait_send()
 
 
-def gather_cuts(arrays, cuts, shapes, number):
-    count = len(arrays)
-    most = 8
-    return pl.pallas_call(
-        functools.partial(gather_kernel, cuts),
-        in_specs=[pl.BlockSpec(memory_space=pl.ANY)] * count,
-        out_specs=[pl.BlockSpec(memory_space=pl.ANY)] * count,
-        out_shape=[jax.ShapeDtypeStruct(shape, jnp.bfloat16) for shape in shapes],
+def opening(number, cuts, source, mask, cosine, sine):
+    contexts = lax.axis_size("context")
+    tok, model = source.shape
+    slots = mask.shape[1]
+    half = model // 2
+    gathers = [Gather(rows, pieces) for _, rows, pieces, _ in cuts]
+    spreads = [Spread(contexts // 2), Spread(contexts // 2)]
+    low, full = jnp.bfloat16, jnp.float32
+    dma = pltpu.SemaphoreType.DMA
+    tall, wide = cuts[0][1], cuts[0][3]
+    outs = pl.pallas_call(
+        functools.partial(opening_kernel, gathers, spreads),
+        in_specs=[pl.BlockSpec(memory_space=pl.ANY)] * len(cuts)
+        + [pl.BlockSpec(memory_space=pltpu.VMEM)] * 4,
+        out_specs=[pl.BlockSpec(memory_space=pl.ANY)] * len(cuts)
+        + [pl.BlockSpec(memory_space=pltpu.VMEM)] * 3
+        + [pl.BlockSpec(memory_space=pl.ANY)] * 2,
+        out_shape=[jax.ShapeDtypeStruct((4 * rows, columns), low) for _, rows, _, columns in cuts]
+        + [
+            jax.ShapeDtypeStruct((2 * tok, half), low),
+            jax.ShapeDtypeStruct((2, slots, DH), low),
+            jax.ShapeDtypeStruct((tok, model), full),
+        ]
+        + [jax.ShapeDtypeStruct((contexts, tok, model), low)] * 2,
         scratch_shapes=[
-            pltpu.SemaphoreType.DMA((count, most, 2)),
-            pltpu.SemaphoreType.DMA((count, most, 2)),
-            pltpu.SemaphoreType.DMA((count, most)),
-            pltpu.SemaphoreType.DMA((count, 2)),
-            pltpu.SemaphoreType.DMA((count, 2)),
-        ],
-        cost_estimate=pl.CostEstimate(
-            flops=0, transcendentals=0, bytes_accessed=20 * sum(a * b for a, b in shapes)
+            pltpu.VMEM((2, tok, model), low),
+            pltpu.VMEM((2 * tok, model), low),
+            pltpu.VMEM((model, cuts[1][3]), low),
+            pltpu.VMEM((model, half), low),
+            pltpu.VMEM((2, slots, DH), low),
+            pltpu.VMEM((2, 2 * tok, half), low),
+            pltpu.VMEM((tok, model), low),
+            pltpu.VMEM((tok, model), low),
+            pltpu.VMEM((2 * tok, half), full),
+            pltpu.VMEM((tok, half), full),
+            pltpu.VMEM((4 * tall, wide), low),
+            dma((3,)),
+            dma((3,)),
+            dma((4,)),
+            dma((contexts,)),
+            dma((contexts,)),
+        ]
+        + [shape for part in gathers + spreads for shape in part.scratch()],
+        cost_estimate=pl.CostEstimate(flops=0, transcendentals=0, bytes_accessed=700_000_000),
+        compiler_params=pltpu.CompilerParams(
+            collective_id=number, has_side_effects=True, vmem_limit_bytes=VMEM_LIMIT
         ),
-        compiler_params=pltpu.CompilerParams(collective_id=number, has_side_effects=True),
-    )(*arrays)
+    )(*[array for array, _, _, _ in cuts], source, mask, cosine, sine)
+    return outs[: len(cuts)], outs[len(cuts) :]
 
 
 class Product:
@@ -456,33 +684,6 @@
     scores = jnp.where(mask > 0.0, scores, NEG)
     raised = jnp.exp(scores - jnp.max(scores, axis=1, keepdims=True))
     return raised / jnp.sum(raised, axis=1, keepdims=True)
-
-
-def mix_kernel(mask_ref, q_ref, k_ref, v_ref, out_ref):
-    weights = masked_weights(q_ref[...], k_ref[...], mask_ref[...])
-    out_ref[...] = jnp.dot(
-        weights.astype(jnp.bfloat16), v_ref[...], preferred_element_type=jnp.float32
-    ).astype(jnp.bfloat16)
-
-
-def mix(mask, queries, keys, values):
-    rows, width = queries.shape
-    slots = keys.shape[0]
-    whole = lambda h: (0, 0)
-    part = lambda h: (0, h)
-    return pl.pallas_call(
-        mix_kernel,
-        grid=(width // DH,),
-        in_specs=[
-            pl.BlockSpec((rows, slots), whole),
-            pl.BlockSpec((rows, DH), part),
-            pl.BlockSpec((slots, DH), whole),
-            pl.BlockSpec((slots, DH), whole),
-        ],
-        out_specs=pl.BlockSpec((rows, DH), part),
-        out_shape=jax.ShapeDtypeStruct((rows, width), jnp.bfloat16),
-        compiler_params=pltpu.CompilerParams(vmem_limit_bytes=VMEM_LIMIT),
-    )(mask, queries, keys, values)
 
 
 def mix_back_kernel(mask_ref, q_ref, k_ref, v_ref, g_ref, dq_ref, dk_ref, dv_ref):
@@ -637,27 +838,15 @@
     unit_start = jnp.minimum(place * width, per_shard - width)
     units = shards * width * LANES
 
-    vectors = jnp.concatenate([attn_gain, output_bias, feed_gain, down_bias, gate_up_bias])
-    vectors = vector_gather(vectors, shard).astype(jnp.float32)
-    gain_one, bias_out, gain_two, bias_down = (
-        vectors[:, i * (model // shards) : (i + 1) * (model // shards)].reshape(1, model)
-        for i in range(4)
-    )
-    bias_gate_up = vectors[:, 4 * (model // shards) :].reshape(2 * shards, per_shard * LANES)
-    bias_gate_up = lax.dynamic_slice_in_dim(
-        bias_gate_up, unit_start * LANES, width * LANES, 1
-    ).reshape(1, 2 * units)
     shard_rows = model // shards
-    core_cols, core_heads = keyval_weight.shape[1] // 2, query_weight.shape[1] // 2
-
-    def cut_of(wide):
+    block = width * LANES
+
+    def half_of(wide):
         def pieces():
             column = lax.rem(lax.axis_index("context"), 2) * wide
             return [(0, pl.multiple_of(column, LANES), wide, 0)]
 
-        return shard_rows, pieces
-
-    block = width * LANES
+        return pieces
 
     def first_unit():
         return jnp.minimum(lax.axis_index("context") * width, per_shard - width) * LANES
@@ -671,21 +860,8 @@
     def down_pieces():
         return [(pl.multiple_of(first_unit(), LANES), 0, model, 0)]
 
-    keyval_half, query_half = gather_cuts(
-        (after(keyval_weight, vectors), query_weight),
-        (cut_of(core_cols), cut_of(core_heads)),
-        ((model, core_cols), (model, core_heads)),
-        0,
-    )
-    output_half = shard_gather(
-        after(halves(output_weight, core, 1)[0], keyval_half, query_half), shard
-    )
-    unit_at = unit_start * LANES + jnp.arange(width * LANES, dtype=jnp.int32)
-    unit_live = jnp.tile(unit_at >= place * width * LANES, shards)[None, :].astype(jnp.float32)
-
-    source = inputs.astype(jnp.float32)
-    attn_in = rms_norm(source, gain_one).astype(jnp.bfloat16)
-    attn_pair = pair_rows(attn_in, core)
+    unit_at = unit_start * LANES + jnp.arange(block, dtype=jnp.int32)
+    unit_live = jnp.tile(unit_at >= place * block, shards)[None, :].astype(jnp.float32)
     slots = jnp.arange(group, dtype=jnp.int32)
     pair_slots = chip * (2 * tok) + jnp.arange(2 * tok, dtype=jnp.int32)
     pair_docs = lax.dynamic_slice_in_dim(doc_ids, chip * (2 * tok), 2 * tok)
@@ -695,41 +871,45 @@
     ).astype(jnp.float32)
     angles = pair_slots.astype(jnp.float32)[:, None] * frequencies(DH)[None, :]
     cosine, sine = jnp.cos(angles), jnp.sin(angles)
-    keyval_raw = jnp.dot(attn_pair, keyval_half, preferred_element_type=jnp.float32)
-    keyval = jnp.where(core == 0, rotate(keyval_raw, cosine, sine), keyval_raw).astype(jnp.bfloat16)
+    vectors = jnp.concatenate([attn_gain, output_bias, feed_gain, down_bias, gate_up_bias])
+    vector_rows = vectors.shape[0] // shard_rows
+    vector_tall = -(-vector_rows // 32) * 32
+    vectors = jnp.pad(
+        vectors.reshape(vector_rows, shard_rows), ((0, vector_tall - vector_rows), (0, 0))
+    )
+    core_cols, core_heads = keyval_weight.shape[1] // 2, query_weight.shape[1] // 2
+    (vectors, keyval_half, query_half, output_half, gate_up_part, down_part), (
+        queries, keyval, resid, mixed_group, feed_group
+    ) = opening(
+        0,
+        (
+            (vectors, vector_tall, lambda: [(0, 0, shard_rows, 0)], shard_rows),
+            (keyval_weight, shard_rows, half_of(core_cols), core_cols),
+            (query_weight, shard_rows, half_of(core_heads), core_heads),
+            (output_weight, shard_rows, half_of(model // 2), model // 2),
+            (gate_up_weight, shard_rows, gate_up_pieces, 2 * units),
+            (down_weight, block, down_pieces, model),
+        ),
+        inputs,
+        mask,
+        jnp.concatenate([cosine, cosine], axis=1),
+        jnp.concatenate([-sine, sine], axis=1),
+    )
     grad_group = gather(cotangent, "context")
-    keyval = gather(after(keyval, grad_group), "context").reshape(contexts // 2, 2, 2 * tok, DH)
-    keys, values = keyval[:, 0].reshape(group, DH), keyval[:, 1].reshape(group, DH)
-    query_raw = jnp.dot(attn_pair, query_half, preferred_element_type=jnp.float32)
-    heads = query_raw.shape[1] // DH
-    queries = (
-        (
-            rotate(query_raw.reshape(2 * tok, heads, DH), cosine[:, None, :], sine[:, None, :])
-            * DH ** (-0.5)
-        )
-        .astype(jnp.bfloat16)
-        .reshape(2 * tok, heads * DH)
-    )
-    mixed_half = mix(mask, queries, keys, values)
-    mixed_own = swap_rows(mixed_half, core)
-    mixed_pair = pair_rows(mixed_own, core)
-    attn_out = swap_rows(
-        jnp.dot(mixed_pair, output_half, preferred_element_type=jnp.float32), core
-    )
-    attn_group = gather(after(attn_in, keyval), "context")
-    resid = source + after(attn_out, attn_group) + bias_out
-
-    feed_in = rms_norm(resid, gain_two).astype(jnp.bfloat16)
-    mixed_group = gather(mixed_own, "context")
-    feed_group = gather(feed_in, "context")
-    gate_up_part, down_part = gather_cuts(
-        (gate_up_weight, after(down_weight, feed_in)),
-        ((shard_rows, gate_up_pieces), (block, down_pieces)),
-        ((model, 2 * units), (units, model)),
-        1,
-    )
+    source_group = gather(inputs, "context")
+    vectors = vectors.reshape(shards, vector_tall, shard_rows).astype(jnp.float32)
+    gain_one, gain_two, bias_down = (vectors[:, i].reshape(1, model) for i in (0, 2, 3))
+    bias_gate_up = vectors[:, 4:vector_rows].reshape(2 * shards, per_shard * LANES)
+    bias_gate_up = lax.dynamic_slice_in_dim(
+        bias_gate_up, unit_start * LANES, block, 1
+    ).reshape(1, 2 * units)
+    source = inputs.astype(jnp.float32)
+    keys, values = keyval[0], keyval[1]
+    heads = core_heads // DH
+    mixed_group, feed_group = mixed_group.reshape(group, model), feed_group.reshape(group, model)
+
     hidden, gate_back, up_back, gate_sums, up_sums = feed(
-        feed_group, after(grad_group, mixed_group), gate_up_part, down_part, bias_gate_up, unit_live
+        feed_group, after(grad_group, source_group), gate_up_part, down_part, bias_gate_up, unit_live
     )
     gate_up_low = jnp.concatenate([gate_back, up_back], axis=1)
     feed_part = against(gate_up_low, gate_up_part).astype(jnp.bfloat16)
@@ -788,6 +968,7 @@
     def by_owners(field):
         return field.reshape(contexts, owned, field.shape[1])
 
+    attn_group = rms_norm(source_group.astype(jnp.float32), gain_one).astype(jnp.bfloat16)
     head_part, keyval_part = query_back.shape[1] // chips, keyval_back.shape[1] // chips
     spare = max(2 * LANES - head_part - keyval_part, 0)
     back_cols = jnp.concatenate([by_chips(query_back), by_chips(keyval_back)], axis=2)

time: 761 us -> 691 us (0.908)
  waiting for transfers between devices: 83.3 us -> 7.94 us
  Pallas kernels: 494 us -> 545 us
  local copies, waits for them, and re-layouts: 57.5 us -> 41.3 us
  starting transfers between devices: 17.2 us -> 5.05 us
  matrix products: 47 us -> 35 us
    pallas_call x3 -> x1, Pallas kernels: 206 us -> 264 us  [opening(): pl.pallas_call(functools.partial(opening_kernel, gathers, spreads), in_sp...]
    ppermute x9 -> x2, waiting for transfers between devices: 52.2 us -> 0.01 us  [across(): return lax.ppermute(value, 'shard', [(i, i ^ bit) for i in range(count)])]
    all_gather x5 -> x2, waiting for transfers between devices: 24.4 us -> 0.01 us  [gather(): return lax.all_gather(value, axis, axis=0, tiled=True)]
    unnamed x113 -> x103, local copies, waits for them, and re-layouts: 26 us -> 14.9 us
    dot_general x3 -> x0, matrix products: 10.3 us -> none  [the longest x1 6.11 us: body(): jnp.dot(attn_pair, query_half, preferred_element_type=jnp.float32)]
    ppermute x9 -> x2, starting transfers between devices: 12.8 us -> 3.12 us  [across(): return lax.ppermute(value, 'shard', [(i, i ^ bit) for i in range(count)])]
  transfers between devices with their start and end apart: 23 -> 9, of which waited for: 9 -> 2; matrix products, arithmetic and copies ran while one was open for 14% -> 11% of each run, Pallas kernels for 55% -> 68%
where the time goes in v4:
time: 691 us; the launch traced here: 681 us
  Pallas kernels  545 us (79%)
  local copies, waits for them, and re-layouts  41.3 us (6%)
  matrix products  35 us (5%)
  other arithmetic  31.2 us (5%)
  between operations  15.1 us (2%)
  waiting for transfers between devices  7.94 us (1%)
    pallas_call x1, Pallas kernels, opening(): pl.pallas_call(functools.partial(opening_kernel, gathers, spreads), in_sp...  264 us
    pallas_call x4, Pallas kernels, work(): pl.pallas_call(functools.partial(work_kernel, made, swaps, chained), in_s...  235 us
    dot_general x4, matrix products, against(): lax.dot_general(left, weight, (((1,), (1,)), ((), ())), preferred_element...  27.3 us
    pallas_call x1, Pallas kernels, feed(): pl.pallas_call(feed_kernel, grid=(blocks, rows // tall), in_specs=[pl.Blo...  27.1 us
    unnamed x103, local copies, waits for them, and re-layouts  14.9 us
  transfers between devices with their start and end apart: 9, of which 2 were waited for; matrix products, arithmetic and copies ran while one was open for 11% of the time, Pallas kernels for 68%

profile of v4, /device:TPU:0, one launch (start us, length us, event | category | flops | bytes accessed | tf_op | source)
XLA Modules:
  0.0 680.6 jit_solution(2804707064596213706)
XLA Ops:
  14.8 263.8 %shard_map.220 = (bf16[128,640]{1,0:T(8,128)(2,1)}, bf16[2560,256]{1,0:T(8,128)(2,1)}, bf16[2560,1280]{1,0:T(8,128)(2,1)}, bf16[2560,1280]{1,0:T(8,128)(2,1)}, b...) custom-call(bf16[32,640]{1,0:T(8,128)(2,1)} %pad.8.refs_0_, ...), custom_call_target="tpu_custom_call" | custom-call | bytes 700000000 | tf_op jit(solution)/shard_map/pallas_call | solution.py:476
  281.0 27.1 %shard_map.221 = (bf16[1024,1024]{1,0:T(8,128)(2,1)}, bf16[1024,1024]{1,0:T(8,128)(2,1)}, bf16[1024,1024]{1,0:T(8,128)(2,1)}, f32[1,1024]{1,0:T(1,128)}, f32[1,1024]{1,0:T(1,128)}) custom-call(bf16[1024,2560]{1,0:T(8,128)(2,1)} %bitcast.76, bf16[1024,2560]{1,0:T(8,128)(2,1)} %all-gather.3.cloned.1.call-done.grad_ref.refs_0_, ...), custom_call_target="tpu_custom_call" | custom-call | tf_op jit(solution)/shard_map/pallas_call | solution.py:784
  308.1 16.8 %convolution_convert_fusion.1 = bf16[1024,2560]{1,0:T(8,128)(2,1)} fusion(bf16[2560,2048]{1,0:T(8,128)(2,1)} %get-tuple-element.50.gate_ref.up_ref, bf16[1024,1024]{1,0:T(8,128)(2,1)} %get-tuple-element.55.refs_1_, bf16[1024,1024]{1,0:T(8,128)(2,1)} %get-tuple-element.54.refs_1_), kind=kOutput, calls=%fused_computation.6 | convolution fusion | flops 10748428288 | bytes 19922944 | tf_op jit(solution)/shard_map/dot_general | solution.py:55
  325.0 48.4 %shard_map.222 = bf16[640,1024]{1,0:T(8,128)(2,1)} custom-call(bf16[1024,2560]{1,0:T(8,128)(2,1)} %all-gather.3.cloned.1.call-done.grad_ref.refs_0_, bf16[1024,1024]{1,0:T(8,128)(2,1)} %get-tuple-element.57.refs_1_), custom_call_target="tpu_custom_call" | custom-call | bytes 150000000 | tf_op jit(solution)/shard_map/pallas_call | solution.py:668
  373.4 7.8 %convolution_convert_fusion = bf16[1024,2560]{1,0:T(8,128)(2,1)} fusion(bf16[1024,1024]{1,0:T(8,128)(2,1)S(1)} %copy-done.7, bf16[1024,2560]{1,0:T(8,128)(2,1)S(1)} %bitcast.82), kind=kOutput, calls=%fused_computation.5 | convolution fusion | flops 5371330560 | bytes 12582912 | tf_op jit(solution)/shard_map/dot_general | solution.py:918
  381.1 4.9 reduce-scatter.3.cloned.1.call-done
  386.0 1.7 slice_reduce_fusion.1
  390.3 1.6 collective-permute-done
  391.9 5.0 fusion.21
  402.0 2.3 slice_bitcast_fusion
  404.2 2.2 copy.51
  406.4 2.3 copy.60
  408.7 2.8 pad.9.clone
  411.5 2.2 reshape.280.refs_3_
  413.8 2.3 add_convert_fusion.g_ref
  416.1 11.2 %shard_map.223 = (f32[256,1280]{1,0:T(8,128)}, f32[1024,256]{1,0:T(8,128)}, f32[1024,256]{1,0:T(8,128)}) custom-call(f32[256,1024]{1,0:T(8,128)} %fusion.20.refs_7_.mask_ref, bf16[256,1280]{1,0:T(8,128)(2,1)} %get-tuple-element.60.q_ref, bf16[1024,256]{1,0:T(8,128)(2,1)} %get-tuple-element.140.k_ref, bf16[1024,256]{1,0:T(8,128)(2,1)} %get-tuple-element.139.v_ref, ...), custom_call_target="tpu_custom_call" | custom-call | tf_op jit(solution)/shard_map/pallas_call | solution.py:715
  427.3 1.8 copy.46
  431.5 52.9 %shard_map.224 = (bf16[640,1024]{1,0:T(8,128)(2,1)}, bf16[8,256,256]{2,1,0:T(8,128)(2,1)}, bf16[8,128,512]{2,1,0:T(8,128)(2,1)}) custom-call(bf16[1024,2560]{1,0:T(8,128)(2,1)} %bitcast.77, bf16[1024,1024]{1,0:T(8,128)(2,1)} %get-tuple-element.54.refs_1_, bf16[8,256,256]{2,1,0:T(8,128)(2,1)} %bitcast.87, bf16[8,128,512]{2,1,0:T(8,128)(2,1)} %reshape.280.refs_3_), custom_call_target="tpu_custom_call" | custom-call | bytes 150000000 | tf_op jit(solution)/shard_map/pallas_call | solution.py:668
  487.3 4.9 fusion.39
  496.7 3.8 fusion.2.refs_0_
  502.3 2.2 copy.53
  504.6 2.8 fusion.14
  508.1 4.6 fusion.10
  512.8 1.5 collective-permute-start.3
  515.4 84.2 %shard_map.225 = (bf16[640,1024]{1,0:T(8,128)(2,1)}, bf16[128,2560]{1,0:T(8,128)(2,1)}, bf16[4,256,384]{2,1,0:T(8,128)(2,1)}, bf16[8,80,1024]{2,1,0:T(8,128)(2,1)}, bf16[8,80,1024]{2,1,0:T(8,128)(2,1)}) custom-call(bf16[1024,2560]{1,0:T(8,128)(2,1)} %bitcast.78, bf16[1024,1024]{1,0:T(8,128)(2,1)} %get-tuple-element.55.refs_1_, bf16[1024,512]{1,0:T(8,128)(2,1)} %bitcast.96, ...), custom_call_target="tpu_custom_call" | custom-call | bytes 150000000 | tf_op jit(solution)/shard_map/pallas_call | solution.py:668
  599.6 1.6 collective-permute-start.4
  601.1 2.0 convert_bitcast_fusion.1
  603.1 3.8 shard_map.228
  606.9 4.9 copy.59
  613.0 49.4 %shard_map.226 = (bf16[640,384]{1,0:T(8,128)(2,1)}, bf16[8,80,1024]{2,1,0:T(8,128)(2,1)}, f32[8,8,384]{2,1,0:T(8,128)}, bf16[8,80,384]{2,1,0:T(8,128)(2,1)}) custom-call(bf16[1024,2560]{1,0:T(8,128)(2,1)} %fusion.2.refs_0_, bf16[1024,384]{1,0:T(8,128)(2,1)} %bitcast.100, bf16[8,80,1024]{2,1,0:T(8,128)(2,1)} %bitcast.95, f32[8,8,384]{2,1,0:T(8,128)} %bitcast.106), custom_call_target="tpu_custom_call" | custom-call | bytes 150000000 | tf_op jit(solution)/shard_map/pallas_call | solution.py:668
  667.2 1.5 reshape.298
  669.3 4.3 shard_map.227
  (204 shorter events, 36.9 us)
Async XLA Ops:
  7.2 2.8 copy-start.32
  7.2 3.0 copy-start.20
  7.2 3.3 copy-start.21
  7.2 273.7 %all-gather.3.cloned.1.call-start = ((), (), s32[]{:S(2)}) async-start(), calls=%async_computation.2 | async-start | bytes 5898240 | tf_op jit(solution)/shard_map/all_gather | solution.py:68
  8.0 273.0 %all-gather.5.cloned.1.call-start = ((), (), s32[]{:S(2)}) async-start(), calls=%async_computation.3 | async-start | bytes 5898240 | tf_op jit(solution)/shard_map/all_gather | solution.py:68
  8.7 377.3 %reduce-scatter.3.cloned.1.call-start = ((), (), s32[]{:S(2)}) async-start(), calls=%async_computation.4 | async-start | bytes 5898240 | tf_op jit(solution)/shard_map/reduce_scatter | solution.py:916
  324.9 48.5 %slice-start.2 = ((s8[5242880]{0:T(1024)(128)(4,1)}), s8[1048576]{0:T(1024)(128)(4,1)S(1)}, s32[]{:S(2)}) async-start(s8[5242880]{0:T(1024)(128)(4,1)} %bitcast.81), calls=%async_computation.8 | async-start | bytes 2097152
  324.9 183.2 %reduce-scatter.5.cloned.1.call-start = ((), (), s32[]{:S(2)}) async-start(), calls=%async_computation.5 | async-start | bytes 5898240 | tf_op jit(solution)/shard_map/reduce_scatter | solution.py:922
  324.9 48.4 %slice-start.3 = ((s8[5242880]{0:T(1024)(128)(4,1)}), s8[4194304]{0:T(1024)(128)(4,1)S(1)}, s32[]{:S(2)}) async-start(s8[5242880]{0:T(1024)(128)(4,1)} %bitcast.81), calls=%async_computation.9 | async-start | bytes 8388608
  325.0 48.4 %copy-start.7 = (bf16[1024,1024]{1,0:T(8,128)(2,1)S(1)}, bf16[1024,1024]{1,0:T(8,128)(2,1)}, u32[]{:S(2)}) copy-start(bf16[1024,1024]{1,0:T(8,128)(2,1)} %get-tuple-element.57.refs_1_) | copy-start | bytes 6291460
  381.1 6.7 copy-start
  390.2 1.7 collective-permute-start
  396.9 4.3 copy-start.1
  398.2 15.6 %collective-permute-start.1 = (f32[256,1280]{1,0:T(8,128)}, f32[256,1280]{1,0:T(8,128)}, u32[]{:S(2)}, u32[]{:S(2)}) collective-permute-start(f32[256,1280]{1,0:T(8,128)} %slice_select_fusion.1), channel_id=1, source_target_pairs={{0,1},{1,0},{2,3},{3,2},{4,5},{5,4},{6,7},{7,6},{8,9},{9,8},{10,11... | collective-permute-start | bytes 3932168 | tf_op jit(solution)/shard_map/ppermute | solution.py:82
  399.9 96.7 %copy-start.14 = (f32[2560]{0:T(1024)}, f32[2560]{0:T(1024)S(1)}, u32[]{:S(2)}) copy-start(f32[2560]{0:T(1024)S(1)} %mul.241) | copy-start | bytes 30724
  401.4 5.0 copy-start.33
  486.6 5.6 copy-start.6
  487.3 4.9 copy-start.8
  492.3 3.3 slice-start
  492.3 3.3 slice-start.1
  494.1 10.5 %collective-permute-start.2 = (f32[128,2560]{1,0:T(8,128)}, f32[128,2560]{1,0:T(8,128)}, u32[]{:S(2)}, u32[]{:S(2)}) collective-permute-start(f32[128,2560]{1,0:T(8,128)} %slice_select_fusion), channel_id=1, source_target_pairs={{0,1},{1,0},{2,3},{3,2},{4,5},{5,4},{6,7},{7,6},{8,9},{9,8},{10,11... | collective-permute-start | bytes 3932168 | tf_op jit(solution)/shard_map/ppermute | solution.py:82
  504.6 2.8 copy-start.16
  504.6 2.8 copy-start.15
  504.6 3.5 copy-start.34
  504.6 3.5 copy-start.23
  508.1 4.7 copy-start.19
  508.1 4.7 copy-start.25
  508.1 4.7 copy-start.24
  508.1 6.2 copy-start.5
  512.8 86.7 %collective-permute-start.3 = (f32[12288]{0:T(1024)S(1)}, f32[12288]{0:T(1024)S(1)}, u32[]{:S(2)}, u32[]{:S(2)}) collective-permute-start(f32[12288]{0:T(1024)S(1)} %constant_dynamic-update-slice_fusion.9), channel_id=1, source_target_pairs={{0,8},{8,0},{16,24},{24,16},{1,9},{9,1},{17,25},{25,17},{2,10},{10... | collective-permute-start | bytes 147464 | tf_op jit(solution)/shard_map/ppermute | solution.py:73
  599.6 12.3 %collective-permute-start.4 = (f32[12288]{0:T(1024)S(1)}, f32[12288]{0:T(1024)S(1)}, u32[]{:S(2)}, u32[]{:S(2)}) collective-permute-start(f32[12288]{0:T(1024)S(1)} %add.148), channel_id=1, source_target_pairs={{0,16},{8,24},{16,0},{24,8},{1,17},{9,25},{17,1},{25,9},{2,18},{10... | collective-permute-start | bytes 147464 | tf_op jit(solution)/shard_map/ppermute | solution.py:73
  662.4 4.1 copy-start.11
  (16 other events, 26.9 us)
Sparse Core Ops, SparseCore 0:
  9.7 58.7 all-gather.2
  70.1 73.2 all-gather.4
  325.0 60.9 reduce-scatter.2
  388.2 63.5 reduce-scatter.4

commit v5 on v4

--- a/solution.py
+++ b/solution.py
@@ -58,6 +58,7 @@
 
 
 VMEM_LIMIT = 56 * 1024 * 1024
+BACK_LIMIT = 60 * 1024 * 1024
 LANES = 128
 MESH = pl.DeviceIdType.MESH
 GELU = 0.7978845608028654
@@ -111,20 +112,6 @@
 def unit_tiles(ff, shards, contexts):
     per_shard = ff // shards // LANES
     return -(-per_shard // contexts), per_shard
-
-
-def join_units(pieces, parts, shards, width, per_shard):
-    contexts, inner = pieces.shape[0], pieces.shape[1:-1]
-    field = pieces.reshape(contexts, *inner, parts, shards, width * LANES)
-    kept = []
-    for at in range(contexts):
-        first = at * width
-        if first >= per_shard:
-            continue
-        start = min(first, per_shard - width)
-        stop = min(first + width, per_shard)
-        kept.append(field[at, ..., (first - start) * LANES : (stop - start) * LANES])
-    return jnp.concatenate(kept, axis=-1).reshape(*inner, parts * shards * per_shard * LANES)
 
 
 def unit_pieces(contexts, shards, width, per_shard):
@@ -146,29 +133,36 @@
     return found
 
 
-def lay_kernel(pieces, *refs):
-    *sources, out_ref = refs
-    units = out_ref.shape[1] // len(sources)
-    for part, source in enumerate(sources):
+def lay_kernel(pieces, down_ref, gate_ref, up_ref, back_ref, output_ref, *outs):
+    down_out, gate_up_out, query_out, keyval_out, output_out = outs
+    units, owned = down_out.shape[1], down_out.shape[0]
+    contexts = back_ref.shape[0]
+    head_part, keyval_part = query_out.shape[1] // contexts, keyval_out.shape[1] // contexts
+    for source, out, offset in (
+        (down_ref, down_out, 0),
+        (gate_ref, gate_up_out, 0),
+        (up_ref, gate_up_out, units),
+    ):
         for at, column, wide, first in pieces:
-            out_ref[:, part * units + first : part * units + first + wide] = source[
+            out[:, offset + first : offset + first + wide] = source[
                 at, :, column : column + wide
             ].astype(jnp.float32)
-
-
-def lay_kernel_turned(pieces, source, out_ref):
-    for at, column, wide, first in pieces:
-        out_ref[first : first + wide, :] = source[at, :, column : column + wide].astype(jnp.float32).T
-
-
-def lay(fields, pieces, units, turned=False):
-    rows = fields[0].shape[1]
-    shape = (units, rows) if turned else (rows, len(fields) * units)
+    for at in range(contexts):
+        slot = (at % 2) * (contexts // 2) + at // 2
+        part = back_ref[at].astype(jnp.float32)
+        query_out[:, slot * head_part : (slot + 1) * head_part] = part[:, :head_part]
+        keyval_out[:, slot * keyval_part : (slot + 1) * keyval_part] = part[
+            :, head_part : head_part + keyval_part
+        ]
+    output_out[...] = output_ref[:owned].astype(jnp.float32)
+
+
+def lay(pieces, owned, widths, *fields):
     return pl.pallas_call(
-        functools.partial(lay_kernel_turned if turned else lay_kernel, pieces),
+        functools.partial(lay_kernel, pieces),
         in_specs=[pl.BlockSpec(memory_space=pltpu.VMEM)] * len(fields),
-        out_specs=pl.BlockSpec(memory_space=pltpu.VMEM),
-        out_shape=jax.ShapeDtypeStruct(shape, jnp.float32),
+        out_specs=[pl.BlockSpec(memory_space=pltpu.VMEM)] * len(widths),
+        out_shape=[jax.ShapeDtypeStruct((owned, wide), jnp.float32) for wide in widths],
         compiler_params=pltpu.CompilerParams(vmem_limit_bytes=VMEM_LIMIT),
     )(*fields)
 
@@ -320,24 +314,33 @@
         del refs[:count]
         return taken
 
-    sources = take(len(gathers))
+    sources = take(len(gathers) - 1)
+    vector_refs = take(5)
     source_ref, mask_ref, cosine_ref, sine_ref = take(4)
     wholes = take(len(gathers))
     queries_ref, keyval_ref, resid_ref = take(3)
-    groups = take(2)
-    pair, attn, small, big, keyval, mixed, mixed_own, feed_own, out, out_came, vectors = take(11)
+    groups = take(3)
+    pair, attn, small, big, keyval, mixed, mixed_own, feed_own, out, out_came = take(10)
+    vectors, vectors_own = take(2)
     swap_send, swap_receive, load, keyval_send, keyval_receive = take(5)
-    for gather_of, source, whole in zip(gathers, sources, wholes):
+    for gather_of, source, whole in zip(gathers, [vectors_own] + sources, wholes):
         gather_of.bind(source, whole, *take(5))
-    for spread, own, group in zip(spreads, (mixed_own, feed_own), groups):
-        spread.bind(own, group, *take(5))
     me, contexts = lax.axis_index("context"), lax.axis_size("context")
     chip, core = me // 2, lax.rem(me, 2)
     mate = me + 1 - 2 * core
     tok, model = source_ref.shape
     rows = 2 * tok
+    attn_own = attn.at[pl.ds(pl.multiple_of(core * tok, tok), tok)]
+    for spread, own, group in zip(spreads, (mixed_own, feed_own, attn_own), groups):
+        spread.bind(own, group, *take(5))
     half = model // 2
     others = [lax.rem(me + k, contexts) for k in range(1, contexts)]
+    vectors_own[...] = jnp.zeros_like(vectors_own)
+    row, across_row = 0, vectors_own.shape[1]
+    for ref in vector_refs:
+        for start in range(0, ref.shape[1], across_row):
+            vectors_own[row : row + 1, :] = ref[:, start : start + across_row]
+            row += 1
     greet(gathers[0].near, others)
     vector_of, keyval_of, query_of, output_of, gate_up_of, down_of = gathers
     swaps = []
@@ -353,8 +356,8 @@
         copy.start()
         copy.wait()
 
+    keyval_of.post()
     vector_of.post()
-    keyval_of.post()
     query_of.post()
     pair[core] = source_ref[...]
     swap(0, source_ref, pair.at[core])
@@ -417,6 +420,7 @@
         to_device(
             "context", block, block, keyval_send.at[k], keyval_receive.at[k], others[k - 1]
         ).wait_recv()
+    spreads[2].post()
     for h in range(heads):
         weights = masked_weights(queries_ref[:, h * DH : (h + 1) * DH], keyval[0], mask_ref[...])
         mixed[core, :, h * DH : (h + 1) * DH] = jnp.dot(
@@ -448,6 +452,7 @@
     feed_own[...] = rms_norm(resid, vector(2)).astype(jnp.bfloat16)
     spreads[1].post()
     spreads[0].post()
+    spreads[2].pass_on()
     keyval_ref[...] = keyval[...]
     gate_up_of.pass_on()
     down_of.pass_on()
@@ -463,30 +468,30 @@
         copy.wait_send()
 
 
-def opening(number, cuts, source, mask, cosine, sine):
+def opening(number, cuts, vectors, source, mask, cosine, sine):
     contexts = lax.axis_size("context")
     tok, model = source.shape
     slots = mask.shape[1]
     half = model // 2
     gathers = [Gather(rows, pieces) for _, rows, pieces, _ in cuts]
-    spreads = [Spread(contexts // 2), Spread(contexts // 2)]
+    spreads = [Spread(contexts // 2) for _ in range(3)]
     low, full = jnp.bfloat16, jnp.float32
     dma = pltpu.SemaphoreType.DMA
     tall, wide = cuts[0][1], cuts[0][3]
     outs = pl.pallas_call(
         functools.partial(opening_kernel, gathers, spreads),
-        in_specs=[pl.BlockSpec(memory_space=pl.ANY)] * len(cuts)
-        + [pl.BlockSpec(memory_space=pltpu.VMEM)] * 4,
+        in_specs=[pl.BlockSpec(memory_space=pl.ANY)] * (len(cuts) - 1)
+        + [pl.BlockSpec(memory_space=pltpu.VMEM)] * 9,
         out_specs=[pl.BlockSpec(memory_space=pl.ANY)] * len(cuts)
         + [pl.BlockSpec(memory_space=pltpu.VMEM)] * 3
-        + [pl.BlockSpec(memory_space=pl.ANY)] * 2,
+        + [pl.BlockSpec(memory_space=pl.ANY)] * 3,
         out_shape=[jax.ShapeDtypeStruct((4 * rows, columns), low) for _, rows, _, columns in cuts]
         + [
             jax.ShapeDtypeStruct((2 * tok, half), low),
             jax.ShapeDtypeStruct((2, slots, DH), low),
             jax.ShapeDtypeStruct((tok, model), full),
         ]
-        + [jax.ShapeDtypeStruct((contexts, tok, model), low)] * 2,
+        + [jax.ShapeDtypeStruct((contexts, tok, model), low)] * 3,
         scratch_shapes=[
             pltpu.VMEM((2, tok, model), low),
             pltpu.VMEM((2 * tok, model), low),
@@ -499,6 +504,7 @@
             pltpu.VMEM((2 * tok, half), full),
             pltpu.VMEM((tok, half), full),
             pltpu.VMEM((4 * tall, wide), low),
+            pltpu.VMEM((tall, wide), low),
             dma((3,)),
             dma((3,)),
             dma((4,)),
@@ -510,7 +516,7 @@
         compiler_params=pltpu.CompilerParams(
             collective_id=number, has_side_effects=True, vmem_limit_bytes=VMEM_LIMIT
         ),
-    )(*[array for array, _, _, _ in cuts], source, mask, cosine, sine)
+    )(*[array for array, _, _, _ in cuts[1:]], *vectors, source, mask, cosine, sine)
     return outs[: len(cuts)], outs[len(cuts) :]
 
 
@@ -520,59 +526,68 @@
         half = -(-self.wide // (2 * LANES)) * LANES
         self.sides = ((0, half), (half, self.wide - half))
 
+    def buffers(self):
+        return [pltpu.VMEM((3, self.rows, wide), jnp.bfloat16) for _, wide in self.sides]
+
     def scratch(self):
-        shapes = [pltpu.VMEM((self.rows, self.wide), jnp.float32)]
-        for _, wide in self.sides:
-            shapes += [pltpu.VMEM((3, self.rows, wide), jnp.bfloat16)] * 2
-        return shapes + [pltpu.SemaphoreType.DMA((6,)), pltpu.SemaphoreType.DMA((6,))]
-
-    def run(self, left, right, out, own, made_a, came_a, made_b, came_b, send, receive):
-        here, along_x, along_y, far = shard_places()
-        ways = ((along_x, along_y), (along_y, along_x))
-        made, came = (made_a, made_b), (came_a, came_b)
-        columns = [pl.ds(start, wide) for start, wide in self.sides]
-        copies = []
-
-        def product(place, side):
-            block = pl.ds(pl.multiple_of(place * self.rows, LANES), self.rows)
-            return over_rows(left[:, block], right[:, columns[side]])
-
-        def push(step, side, place):
-            slot = 2 * step + side
-            copies.append(
-                to_device(
-                    "shard",
-                    made[side].at[step],
-                    came[side].at[step],
-                    send.at[slot],
-                    receive.at[slot],
-                    place,
-                )
+        return self.buffers() + self.buffers() + [pltpu.SemaphoreType.DMA((6,))] * 2
+
+    def bind(self, left, right, made_a, made_b, came_a, came_b, send, receive):
+        self.left, self.right, self.send, self.receive = left, right, send, receive
+        self.made, self.came = (made_a, made_b), (came_a, came_b)
+        self.here, along_x, along_y, self.far = shard_places()
+        self.ways = ((along_x, along_y), (along_y, along_x))
+        self.columns = [pl.ds(start, wide) for start, wide in self.sides]
+        self.copies = []
+
+    def product(self, place, side):
+        block = pl.ds(pl.multiple_of(place * self.rows, LANES), self.rows)
+        return over_rows(self.left[:, block], self.right[:, self.columns[side]])
+
+    def push(self, step, side, place):
+        slot = 2 * step + side
+        self.copies.append(
+            to_device(
+                "shard",
+                self.made[side].at[step],
+                self.came[side].at[step],
+                self.send.at[slot],
+                self.receive.at[slot],
+                place,
             )
-            copies[-1].start()
-
+        )
+        self.copies[-1].start()
+
+    def begin(self):
         for side in range(2):
-            made[side][0] = product(far, side).astype(jnp.bfloat16)
-            push(0, side, ways[side][0])
+            self.made[side][0] = self.product(self.far, side).astype(jnp.bfloat16)
+            self.push(0, side, self.ways[side][0])
         for side in range(2):
-            made[side][1] = product(ways[side][0], side).astype(jnp.bfloat16)
-            push(1, side, ways[side][0])
+            self.made[side][1] = self.product(self.ways[side][0], side).astype(jnp.bfloat16)
+            self.push(1, side, self.ways[side][0])
+
+    def middle(self):
         for side in range(2):
-            kept = product(ways[side][1], side)
-            copies[side].wait_recv()
-            made[side][2] = (kept + came[side][0].astype(jnp.float32)).astype(jnp.bfloat16)
-            push(2, side, ways[side][1])
-        for side in range(2):
-            own[:, columns[side]] = product(here, side)
-        for side in range(2):
-            copies[2 + side].wait_recv()
-            own[:, columns[side]] += came[side][1].astype(jnp.float32)
-        for side in range(2):
-            copies[4 + side].wait_recv()
-            out[:, columns[side]] = (own[:, columns[side]] + came[side][2].astype(jnp.float32)).astype(
+            kept = self.product(self.ways[side][1], side)
+            self.copies[side].wait_recv()
+            self.made[side][2] = (kept + self.came[side][0].astype(jnp.float32)).astype(
                 jnp.bfloat16
             )
-        return copies
+            self.push(2, side, self.ways[side][1])
+
+    def finish(self, out):
+        for side in range(2):
+            total = self.product(self.here, side)
+            self.copies[2 + side].wait_recv()
+            total = total + self.came[side][1].astype(jnp.float32)
+            self.copies[4 + side].wait_recv()
+            out[:, self.columns[side]] = (
+                total + self.came[side][2].astype(jnp.float32)
+            ).astype(jnp.bfloat16)
+
+    def drain(self, first, last):
+        for copy in self.copies[first:last]:
+            copy.wait_send()
 
 
 class Exchange:
@@ -614,7 +629,7 @@
         return finish
 
 
-def work_kernel(products, exchanges, chained, *refs):
+def work_kernel(products, exchanges, chained, summed, *refs):
     refs = list(refs)
 
     def take(count):
@@ -626,32 +641,69 @@
     arrays = take(len(exchanges) - (1 if chained else 0))
     results = take(len(products))
     moved = take(len(exchanges))
+    total_ref = take(1)[0] if summed else None
     product_scratch = [take(len(p.scratch())) for p in products]
     exchange_scratch = [take(len(e.scratch())) for e in exchanges]
     _, along_x, along_y, _ = shard_places()
+    if summed:
+        arrived, stage, stage_came, stage_send, stage_receive = take(5)
     everyone = max(exchanges, key=lambda e: e.count).peers()[1][1:] if exchanges else []
     greet((along_x, along_y), everyone)
-    finishes, copies = [], []
+    finishes, steps = [], []
+    if summed:
+        moved = [arrived] + moved[1:]
+
+    def hop(step, place):
+        steps.append(
+            to_device(
+                "shard",
+                stage.at[step],
+                stage_came.at[step],
+                stage_send.at[step],
+                stage_receive.at[step],
+                place,
+            )
+        )
+        steps[-1].start()
+
     for exchange, array, out, scratch in zip(exchanges, arrays, moved, exchange_scratch):
         finishes.append(exchange.start(lambda j, array=array: array.at[j], out, *scratch))
-    for product, (left, right), out, scratch in zip(products, operands, results, product_scratch):
-        copies += product.run(left, right, out, *scratch)
-    if chained:
-        rows = products[0].rows // exchanges[-1].count
-        finishes.append(
-            exchanges[-1].start(
-                lambda j: results[0].at[pl.ds(pl.multiple_of(j * rows, 16), rows)],
-                moved[-1],
-                *exchange_scratch[-1],
+    for product, (left, right), scratch in zip(products, operands, product_scratch):
+        product.bind(left, right, *scratch)
+        product.begin()
+    if summed:
+        finishes.pop(0)()
+        stage[0] = jnp.sum(arrived[...], axis=0)
+        hop(0, along_x)
+    for product in products:
+        product.middle()
+    if summed:
+        steps[0].wait_recv()
+        stage[1] = stage[0] + stage_came[0]
+        hop(1, along_y)
+    for i, product in enumerate(products):
+        product.finish(results[i])
+        if chained and i == 0:
+            rows = product.rows // exchanges[-1].count
+            finishes.append(
+                exchanges[-1].start(
+                    lambda j: results[0].at[pl.ds(pl.multiple_of(j * rows, 16), rows)],
+                    moved[-1],
+                    *exchange_scratch[-1],
+                )
             )
-        )
-    for copy in copies:
-        copy.wait_send()
+    if summed:
+        steps[1].wait_recv()
+        total_ref[...] = stage[1] + stage_came[1]
+    for product in products:
+        product.drain(0, 6)
+    for step in steps:
+        step.wait_send()
     for finish in finishes:
         finish()
 
 
-def work(number, products=(), exchanges=(), chained=False):
+def work(number, products=(), exchanges=(), chained=False, summed=False):
     contexts = lax.axis_size("context")
     made = [Product(left.shape, right.shape) for left, right in products]
     swaps = [Exchange(array.shape[0], contexts // array.shape[0]) for array in exchanges]
@@ -663,20 +715,288 @@
             jax.ShapeDtypeStruct((contexts, made[0].rows // contexts, made[0].wide), jnp.bfloat16)
         )
     scratch = [shape for part in made + swaps for shape in part.scratch()]
+    totals = []
+    if summed:
+        block = exchanges[0].shape[1:]
+        totals = [jax.ShapeDtypeStruct(block, jnp.float32)]
+        moved[0] = jax.ShapeDtypeStruct((8, LANES), jnp.float32)
+        scratch += [
+            pltpu.VMEM(exchanges[0].shape, jnp.float32),
+            pltpu.VMEM((2, *block), jnp.float32),
+            pltpu.VMEM((2, *block), jnp.float32),
+            pltpu.SemaphoreType.DMA((2,)),
+            pltpu.SemaphoreType.DMA((2,)),
+        ]
     vmem = pl.BlockSpec(memory_space=pltpu.VMEM)
     hbm = pl.BlockSpec(memory_space=pl.ANY)
     outs = pl.pallas_call(
-        functools.partial(work_kernel, made, swaps, chained),
+        functools.partial(work_kernel, made, swaps, chained, summed),
         in_specs=[vmem] * (2 * len(made)) + [hbm] * len(exchanges),
-        out_specs=[vmem] * len(made) + [hbm] * len(swaps),
-        out_shape=results + moved,
+        out_specs=[vmem] * len(made) + [hbm] * len(swaps) + [vmem] * len(totals),
+        out_shape=results + moved + totals,
         scratch_shapes=scratch,
         cost_estimate=pl.CostEstimate(flops=0, transcendentals=0, bytes_accessed=150_000_000),
         compiler_params=pltpu.CompilerParams(
             collective_id=number, has_side_effects=True, vmem_limit_bytes=VMEM_LIMIT
         ),
     )(*[operand for pair in products for operand in pair], *exchanges)
-    return outs[: len(made)], outs[len(made) :]
+    others = outs[len(made) :]
+    if summed:
+        others = [others[-1], *others[1:-1]]
+    return outs[1 if chained else 0 : len(made)], others
+
+
+def norm_back(field, gain, grad):
+    scale = lax.rsqrt(jnp.mean(field * field, axis=1, keepdims=True) + EPS)
+    normed = field * scale
+    bent = grad * gain
+    back = scale * (bent - normed * jnp.mean(bent * normed, axis=1, keepdims=True))
+    return back, jnp.sum(grad * normed, axis=0, keepdims=True)
+
+
+def back_kernel(gate, up, swaps, *refs):
+    refs = list(refs)
+
+    def take(count):
+        taken = refs[:count]
+        del refs[:count]
+        return taken
+
+    output_ref, query_ref, keyval_ref, feed_ref, gate_ref, up_ref, down_ref = take(7)
+    grad_ref, resid_ref, cotangent_ref, source_ref, gains_ref = take(5)
+    queries_ref, keyval_of, mask_ref, cosine_ref, sine_ref = take(5)
+    input_grad_ref, sums_ref, up_out, rows_out, back_out, down_out, gate_out = take(7)
+    left, gate_right, up_right, big, small = take(5)
+    own_grad, swapped, part, part_came, tail_came, mixed_back, query_back = take(7)
+    pieces, pieces_mate, pieces_low, pieces_came = take(4)
+    keyval_back, rows_blocks, back_blocks, gate_sum = take(4)
+    load, mate_send, mate_receive = take(3)
+    made = take(2)
+    gate_scratch, up_scratch = take(4), take(4)
+    rows_swap, back_swap, down_swap, gate_swap, piece_swap = swaps
+    rows_sems, back_sems, down_sems, gate_sems, piece_sems = (take(3) for _ in swaps)
+    me = lax.axis_index("context")
+    chip, core = me // 2, lax.rem(me, 2)
+    mate = me + 1 - 2 * core
+    tok, model = resid_ref.shape
+    half = model // 2
+    rows = 2 * tok
+    shards = lax.axis_size("shard")
+    contexts = lax.axis_size("context")
+    owned = model // (shards * contexts)
+    mine = pl.ds(pl.multiple_of(core * tok, tok), tok)
+    theirs = pl.ds(pl.multiple_of((1 - core) * tok, tok), tok)
+    full = jnp.float32
+    loads = []
+
+    def fetch(source, target):
+        loads.append(pltpu.make_async_copy(source, target, load.at[len(loads)]))
+        loads[-1].start()
+        return loads[-1]
+
+    mates = []
+
+    def to_mate(source, target):
+        step = len(mates)
+        mates.append(
+            to_device("context", source, target, mate_send.at[step], mate_receive.at[step], mate)
+        )
+        mates[-1].start()
+        return mates[-1]
+
+    left_load, gate_load = fetch(feed_ref, left), fetch(gate_ref, gate_right)
+    output_load, up_load = fetch(output_ref, big), fetch(up_ref, up_right)
+    small_load = fetch(keyval_ref, small)
+    _, along_x, along_y, _ = shard_places()
+    greet((along_x, along_y), rows_swap.peers()[1][1:])
+    finishes = [down_swap.start(lambda j: down_ref.at[j], down_out, *down_sems)]
+
+    resid = resid_ref[...]
+    cotangent = cotangent_ref[...].astype(full)
+    resid_part, gain_two_grad = norm_back(resid, gains_ref[1:2], grad_ref[...])
+    resid_grad = cotangent + resid_part
+    input_grad_ref[...] = resid_grad
+    attn_grad = resid_grad.astype(jnp.bfloat16)
+    own_grad[...] = attn_grad
+    swapped[core] = own_grad[:, pl.ds(pl.multiple_of(core * half, LANES), half)]
+    first = to_mate(
+        own_grad.at[:, pl.ds(pl.multiple_of((1 - core) * half, LANES), half)], swapped.at[core]
+    )
+    left_load.wait()
+    gate_load.wait()
+    gate.bind(left, gate_right, *made, *gate_scratch)
+    gate.begin()
+    sums_ref[...] = jnp.zeros_like(sums_ref)
+    sums_ref[1:2] = jnp.sum(attn_grad.astype(full), axis=0, keepdims=True)
+    sums_ref[2:3] = gain_two_grad
+    sums_ref[3:4] = jnp.sum(cotangent, axis=0, keepdims=True)
+    wide = rows_blocks.shape[2] // shards
+    rows_blocks[...] = jnp.zeros_like(rows_blocks)
+    for j in range(contexts):
+        for shard in range(shards):
+            start = (shard * contexts + j) * owned
+            rows_blocks[j, :, shard * wide : shard * wide + owned] = attn_grad[
+                :, start : start + owned
+            ]
+    finishes.append(rows_swap.start(lambda j: rows_blocks.at[j], rows_out, *rows_sems))
+
+    first.wait_recv()
+    output_load.wait()
+    pair_grad = swapped[...].reshape(rows, half)
+    for side in range(2):
+        part[side] = against(pair_grad, big[side * half : (side + 1) * half])
+    second = to_mate(part.at[1 - core], part_came)
+    query_load = fetch(query_ref, big)
+    second.wait_recv()
+    mixed_back[...] = (part[core] + part_came[...]).astype(jnp.bfloat16)
+    cosine, sine = cosine_ref[...], sine_ref[...]
+
+    def unturned(field):
+        return field * cosine - pltpu.roll(field, DH // 4, 1) * sine
+
+    keys, values = keyval_of[0], keyval_of[1]
+    for h in range(half // DH):
+        at = slice(h * DH, (h + 1) * DH)
+        queries, grad = queries_ref[:, at], mixed_back[:, at]
+        weights = masked_weights(queries, keys, mask_ref[...])
+        value_score = against(grad, values)
+        delta = jnp.sum(weights * value_score, axis=1, keepdims=True)
+        score_back = (weights * (value_score - delta)).astype(jnp.bfloat16)
+        back = jnp.dot(score_back, keys, preferred_element_type=full) * DH ** (-0.5)
+        query_back[:, h * DH : h * DH + DH // 2] = unturned(back[:, : DH // 2]).astype(jnp.bfloat16)
+        query_back[:, h * DH + DH // 2 : (h + 1) * DH] = back[:, DH // 2 :].astype(jnp.bfloat16)
+        key_piece = over_rows(score_back, queries)
+        value_piece = over_rows(weights.astype(jnp.bfloat16), grad)
+        if h == 0:
+            pieces[0], pieces[1] = key_piece, value_piece
+        else:
+            pieces[0] += key_piece
+            pieces[1] += value_piece
+    fourth = to_mate(pieces.at[1 - core], pieces_mate)
+    gate.middle()
+    fourth.wait_recv()
+    pieces_low[...] = (pieces[core] + pieces_mate[...]).astype(jnp.bfloat16)
+    pieces_done = piece_swap.start(
+        lambda j: pieces_low.at[pl.ds(pl.multiple_of(j * rows, rows), rows)],
+        pieces_came,
+        *piece_sems,
+    )
+
+    gate.drain(0, 4)
+    up_load.wait()
+    up.bind(left, up_right, *made, *up_scratch)
+    up.begin()
+    gate.finish(gate_sum)
+    tall = gate.rows // contexts
+    finishes.append(
+        gate_swap.start(
+            lambda j: gate_sum.at[pl.ds(pl.multiple_of(j * tall, 16), tall)], gate_out, *gate_sems
+        )
+    )
+
+    pieces_done()
+    total = jnp.sum(pieces_came[...].astype(full), axis=0)
+    keyval_back[:, : DH // 2] = jnp.where(
+        core == 0, unturned(total[:, : DH // 2]), total[:, : DH // 2]
+    ).astype(jnp.bfloat16)
+    keyval_back[:, DH // 2 :] = total[:, DH // 2 :].astype(jnp.bfloat16)
+    chips = contexts // 2
+    head_part, keyval_part = half // chips, DH // chips
+    back_blocks[...] = jnp.zeros_like(back_blocks)
+    for j in range(chips):
+        back_blocks[j, :, :head_part] = query_back[:, j * head_part : (j + 1) * head_part]
+        back_blocks[j, :, head_part : head_part + keyval_part] = keyval_back[
+            :, j * keyval_part : (j + 1) * keyval_part
+        ]
+    finishes.append(back_swap.start(lambda j: back_blocks.at[j], back_out, *back_sems))
+    query_load.wait()
+    small_load.wait()
+    second.wait_send()
+    for side in range(2):
+        at = slice(side * half, (side + 1) * half)
+        part[side] = against(query_back[...], big[at]) + against(keyval_back[...], small[at])
+    third = [to_mate(part.at[side, theirs], tail_came.at[side]) for side in range(2)]
+    gate.drain(4, 6)
+    up.middle()
+    for copy in third:
+        copy.wait_recv()
+    attn_in_grad = jnp.concatenate([part[side, mine] + tail_came[side] for side in range(2)], axis=1)
+    input_part, gain_one_grad = norm_back(
+        source_ref[...].astype(full), gains_ref[0:1], attn_in_grad
+    )
+    input_grad_ref[...] += input_part
+    sums_ref[0:1] = gain_one_grad
+    up.finish(up_out)
+    up.drain(0, 6)
+    for copy in [first, fourth] + third:
+        copy.wait_send()
+    for finish in finishes:
+        finish()
+
+
+def back(number, weights, feed_group, gate_back, up_back, down_rows, tokens, attention):
+    contexts, shards = lax.axis_size("context"), lax.axis_size("shard")
+    tok, model = tokens[1].shape
+    slots = attention[2].shape[1]
+    half, rows, chips = model // 2, 2 * tok, contexts // 2
+    owned = model // (shards * contexts)
+    wide = -(-owned // LANES) * LANES
+    gate = Product(feed_group.shape, gate_back.shape)
+    up = Product(feed_group.shape, up_back.shape)
+    cols = max(half // chips + DH // chips, 2 * LANES)
+    low, full = jnp.bfloat16, jnp.float32
+    shape = jax.ShapeDtypeStruct
+    swaps = [Exchange(n, contexts // n) for n in (contexts, chips, contexts, contexts, chips)]
+    tall = gate.rows // contexts
+    vmem, hbm = pl.BlockSpec(memory_space=pltpu.VMEM), pl.BlockSpec(memory_space=pl.ANY)
+    dma = pltpu.SemaphoreType.DMA
+    return pl.pallas_call(
+        functools.partial(back_kernel, gate, up, swaps),
+        in_specs=[hbm] * 7 + [vmem] * 10,
+        out_specs=[vmem] * 3 + [hbm] * 4,
+        out_shape=[
+            shape((tok, model), full),
+            shape((8, model), full),
+            shape((up.rows, up.wide), low),
+            shape((contexts, tok, shards * wide), low),
+            shape((chips, rows, cols), low),
+            shape(down_rows.shape, low),
+            shape((contexts, tall, gate.wide), low),
+        ],
+        scratch_shapes=[
+            pltpu.VMEM(feed_group.shape, low),
+            pltpu.VMEM(gate_back.shape, low),
+            pltpu.VMEM(up_back.shape, low),
+            pltpu.VMEM((model, half), low),
+            pltpu.VMEM((model, DH), low),
+            pltpu.VMEM((tok, model), low),
+            pltpu.VMEM((2, tok, half), low),
+            pltpu.VMEM((2, rows, half), full),
+            pltpu.VMEM((rows, half), full),
+            pltpu.VMEM((2, tok, half), full),
+            pltpu.VMEM((rows, half), low),
+            pltpu.VMEM((rows, half), low),
+            pltpu.VMEM((2, slots, DH), full),
+            pltpu.VMEM((slots, DH), full),
+            pltpu.VMEM((slots, DH), low),
+            pltpu.VMEM((chips, rows, DH), low),
+            pltpu.VMEM((rows, DH), low),
+            pltpu.VMEM((contexts, tok, shards * wide), low),
+            pltpu.VMEM((chips, rows, cols), low),
+            pltpu.VMEM((gate.rows, gate.wide), low),
+            dma((6,)),
+            dma((5,)),
+            dma((5,)),
+        ]
+        + gate.buffers()
+        + (gate.buffers() + [dma((6,))] * 2)
+        + (up.buffers() + [dma((6,))] * 2)
+        + [each for swap in swaps for each in swap.scratch()],
+        cost_estimate=pl.CostEstimate(flops=0, transcendentals=0, bytes_accessed=400_000_000),
+        compiler_params=pltpu.CompilerParams(
+            collective_id=number, has_side_effects=True, vmem_limit_bytes=BACK_LIMIT
+        ),
+    )(*weights, feed_group, gate_back, up_back, down_rows, *tokens, *attention)
 
 
 def masked_weights(q, k, mask):
@@ -812,6 +1132,187 @@
     )(feed_group, grad_group, gate_up, gate_up, down, bias, bias, live)
 
 
+def middle_kernel(*refs):
+    refs = list(refs)
+
+    def take(count):
+        taken = refs[:count]
+        del refs[:count]
+        return taken
+
+    feed_ref, grad_ref, weight_ref, down_ref, bias_ref, live_ref = take(6)
+    hidden_ref, gate_back_ref, up_back_ref, sums_ref, down_out_ref, feed_grad_ref = take(6)
+    gate_weight, up_weight, down_weight, feed_rows, grad_rows = take(5)
+    own_part, mate_out, mate_in, sent_out, came, swap_in = take(6)
+    weight_load, row_load, mate_send, mate_receive, send, receive = take(6)
+    me = lax.axis_index("context")
+    chips = lax.axis_size("context") // 2
+    chip, core = me // 2, lax.rem(me, 2)
+    mate = me + 1 - 2 * core
+    units, model = down_weight.shape
+    rows, half, wide = feed_rows.shape[1], model // 2, 256
+    blocks = units // wide
+    full, low = jnp.float32, jnp.bfloat16
+    mine = pl.ds(pl.multiple_of(core * half, LANES), half)
+    theirs = pl.ds(pl.multiple_of((1 - core) * half, LANES), half)
+    targets = [lax.rem(chip + 1 + i, chips) for i in range(chips)]
+
+    def token_rows(i):
+        return pl.ds(pl.multiple_of(targets[i] * rows, rows), rows)
+
+    def weight_loads(j):
+        at = pl.ds(pl.multiple_of(j * wide, wide), wide)
+        later = pl.ds(pl.multiple_of(units + j * wide, wide), wide)
+        return [
+            pltpu.make_async_copy(weight_ref.at[:, at], gate_weight.at[:, at], weight_load.at[j, 0]),
+            pltpu.make_async_copy(weight_ref.at[:, later], up_weight.at[:, at], weight_load.at[j, 1]),
+            pltpu.make_async_copy(down_ref.at[at], down_weight.at[at], weight_load.at[j, 2]),
+        ]
+
+    def row_loads(i):
+        at = token_rows(i)
+        return [
+            pltpu.make_async_copy(feed_ref.at[at], feed_rows.at[i % 2], row_load.at[i, 0]),
+            pltpu.make_async_copy(grad_ref.at[at], grad_rows.at[i % 2], row_load.at[i, 1]),
+        ]
+
+    for copy in row_loads(0):
+        copy.start()
+    for j in range(blocks):
+        for copy in weight_loads(j):
+            copy.start()
+    greet((), [mate] + [2 * targets[i] + core for i in range(chips - 1)])
+    sums_ref[...] = jnp.zeros_like(sums_ref)
+    to_mate, to_chips = [], []
+    for i in range(chips):
+        for copy in row_loads(i):
+            copy.wait()
+        if i + 1 < chips:
+            for copy in row_loads(i + 1):
+                copy.start()
+        at = token_rows(i)
+
+        def block(j, carry, i=i, at=at):
+            if i == 0:
+                for copy in weight_loads(j):
+                    copy.wait()
+            cut = pl.ds(pl.multiple_of(j * wide, wide), wide)
+            later = pl.ds(pl.multiple_of(units + j * wide, wide), wide)
+            feed = feed_rows[i % 2]
+            gate = jnp.dot(feed, gate_weight[:, cut], preferred_element_type=full) + bias_ref[:, cut]
+            up = jnp.dot(feed, up_weight[:, cut], preferred_element_type=full) + bias_ref[:, later]
+            back = against(grad_rows[i % 2], down_weight[cut])
+            live = live_ref[:, cut]
+            square = gate * gate
+            bend = jnp.tanh(GELU * gate * (1.0 + CUBE * square))
+            share = 0.5 * (1.0 + bend)
+            gelu = gate * share * live
+            slope = share + 0.5 * gate * (1.0 - bend * bend) * (GELU * (1.0 + 3.0 * CUBE * square))
+            hidden_ref[at, cut] = (gelu * up).astype(low)
+            gate_back = (back * up * slope * live).astype(low)
+            up_back = (back * gelu).astype(low)
+            gate_back_ref[at, cut] = gate_back
+            up_back_ref[at, cut] = up_back
+            sums_ref[0:1, cut] += jnp.sum(gate_back.astype(full), axis=0, keepdims=True)
+            sums_ref[1:2, cut] += jnp.sum(up_back.astype(full), axis=0, keepdims=True)
+            return carry
+
+        lax.fori_loop(0, blocks, block, 0)
+
+        def feed_part(columns):
+            return against(gate_back_ref[at, :], gate_weight[columns, :]) + against(
+                up_back_ref[at, :], up_weight[columns, :]
+            )
+
+        mate_out[i] = feed_part(theirs).astype(low)
+        to_mate.append(
+            to_device(
+                "context", mate_out.at[i], mate_in.at[i], mate_send.at[i], mate_receive.at[i], mate
+            )
+        )
+        to_mate[-1].start()
+        own_part[...] = feed_part(mine)
+        to_mate[-1].wait_recv()
+        if i + 1 < chips:
+            sent_out[i] = (own_part[...] + mate_in[i].astype(full)).astype(low)
+            to_chips.append(
+                to_device(
+                    "context",
+                    sent_out.at[i],
+                    came.at[i],
+                    send.at[i],
+                    receive.at[i],
+                    2 * targets[i] + core,
+                )
+            )
+            to_chips[-1].start()
+        else:
+            own_part[...] += mate_in[i].astype(full)
+        down_out_ref[at, :] = jnp.dot(
+            hidden_ref[at, :], down_weight[...], preferred_element_type=full
+        ).astype(low)
+    for i, copy in enumerate(to_chips):
+        copy.wait_recv()
+        own_part[...] += came[i].astype(full)
+    tok = rows // 2
+    own_rows = pl.ds(pl.multiple_of(core * tok, tok), tok)
+    mate_rows = pl.ds(pl.multiple_of((1 - core) * tok, tok), tok)
+    last = to_device(
+        "context",
+        own_part.at[mate_rows],
+        swap_in,
+        mate_send.at[chips],
+        mate_receive.at[chips],
+        mate,
+    )
+    last.start()
+    feed_grad_ref[:, mine] = own_part[own_rows, :]
+    last.wait_recv()
+    feed_grad_ref[:, theirs] = swap_in[...]
+    for copy in to_mate + to_chips + [last]:
+        copy.wait_send()
+
+
+def middle(number, feed_group, grad_group, gate_up, down, bias, live):
+    group, model = feed_group.shape
+    units, contexts = down.shape[0], lax.axis_size("context")
+    chips, half = contexts // 2, model // 2
+    rows = group // chips
+    low, full = jnp.bfloat16, jnp.float32
+    shape, dma = jax.ShapeDtypeStruct, pltpu.SemaphoreType.DMA
+    vmem, hbm = pl.BlockSpec(memory_space=pltpu.VMEM), pl.BlockSpec(memory_space=pl.ANY)
+    return pl.pallas_call(
+        middle_kernel,
+        in_specs=[hbm] * 4 + [vmem] * 2,
+        out_specs=[vmem] * 6,
+        out_shape=[shape((group, units), low)] * 3
+        + [shape((8, units), full), shape((group, model), low), shape((rows // 2, model), full)],
+        scratch_shapes=[
+            pltpu.VMEM((model, units), low),
+            pltpu.VMEM((model, units), low),
+            pltpu.VMEM((units, model), low),
+            pltpu.VMEM((2, rows, model), low),
+            pltpu.VMEM((2, rows, model), low),
+            pltpu.VMEM((rows, half), full),
+            pltpu.VMEM((chips, rows, half), low),
+            pltpu.VMEM((chips, rows, half), low),
+            pltpu.VMEM((chips, rows, half), low),
+            pltpu.VMEM((chips, rows, half), low),
+            pltpu.VMEM((rows // 2, half), full),
+            dma((units // 256, 3)),
+            dma((chips, 2)),
+            dma((chips + 1,)),
+            dma((chips + 1,)),
+            dma((chips,)),
+            dma((chips,)),
+        ],
+        cost_estimate=pl.CostEstimate(flops=0, transcendentals=0, bytes_accessed=200_000_000),
+        compiler_params=pltpu.CompilerParams(
+            collective_id=number, has_side_effects=True, vmem_limit_bytes=BACK_LIMIT
+        ),
+    )(feed_group, grad_group, gate_up, down, bias, live)
+
+
 def body(
     inputs,
     doc_ids,
@@ -871,32 +1372,32 @@
     ).astype(jnp.float32)
     angles = pair_slots.astype(jnp.float32)[:, None] * frequencies(DH)[None, :]
     cosine, sine = jnp.cos(angles), jnp.sin(angles)
-    vectors = jnp.concatenate([attn_gain, output_bias, feed_gain, down_bias, gate_up_bias])
-    vector_rows = vectors.shape[0] // shard_rows
+    turns = (jnp.concatenate([cosine, cosine], axis=1), jnp.concatenate([-sine, sine], axis=1))
+    vectors = [
+        each.reshape(1, each.shape[0])
+        for each in (attn_gain, output_bias, feed_gain, down_bias, gate_up_bias)
+    ]
+    vector_rows = 4 + gate_up_bias.shape[0] // shard_rows
     vector_tall = -(-vector_rows // 32) * 32
-    vectors = jnp.pad(
-        vectors.reshape(vector_rows, shard_rows), ((0, vector_tall - vector_rows), (0, 0))
-    )
     core_cols, core_heads = keyval_weight.shape[1] // 2, query_weight.shape[1] // 2
     (vectors, keyval_half, query_half, output_half, gate_up_part, down_part), (
-        queries, keyval, resid, mixed_group, feed_group
+        queries, keyval, resid, mixed_group, feed_group, attn_group
     ) = opening(
         0,
         (
-            (vectors, vector_tall, lambda: [(0, 0, shard_rows, 0)], shard_rows),
+            (None, vector_tall, lambda: [(0, 0, shard_rows, 0)], shard_rows),
             (keyval_weight, shard_rows, half_of(core_cols), core_cols),
             (query_weight, shard_rows, half_of(core_heads), core_heads),
             (output_weight, shard_rows, half_of(model // 2), model // 2),
             (gate_up_weight, shard_rows, gate_up_pieces, 2 * units),
             (down_weight, block, down_pieces, model),
         ),
+        vectors,
         inputs,
         mask,
-        jnp.concatenate([cosine, cosine], axis=1),
-        jnp.concatenate([-sine, sine], axis=1),
+        *turns,
     )
     grad_group = gather(cotangent, "context")
-    source_group = gather(inputs, "context")
     vectors = vectors.reshape(shards, vector_tall, shard_rows).astype(jnp.float32)
     gain_one, gain_two, bias_down = (vectors[:, i].reshape(1, model) for i in (0, 2, 3))
     bias_gate_up = vectors[:, 4:vector_rows].reshape(2 * shards, per_shard * LANES)
@@ -906,143 +1407,168 @@
     source = inputs.astype(jnp.float32)
     keys, values = keyval[0], keyval[1]
     heads = core_heads // DH
-    mixed_group, feed_group = mixed_group.reshape(group, model), feed_group.reshape(group, model)
-
-    hidden, gate_back, up_back, gate_sums, up_sums = feed(
-        feed_group, after(grad_group, source_group), gate_up_part, down_part, bias_gate_up, unit_live
-    )
-    gate_up_low = jnp.concatenate([gate_back, up_back], axis=1)
-    feed_part = against(gate_up_low, gate_up_part).astype(jnp.bfloat16)
-    feed_in_grad = lax.psum_scatter(feed_part, "context", scatter_dimension=0, tiled=True)
-    (down_sum,), _ = work(2, [(grad_group, after(hidden, feed_part))])
-    down_part_out = jnp.dot(
-        after(hidden, down_sum), down_part, preferred_element_type=jnp.float32
-    ).astype(jnp.bfloat16)
-    feed_in_grad = after(feed_in_grad, down_part_out)
+    mixed_group, feed_group, attn_group = (
+        field.reshape(group, model) for field in (mixed_group, feed_group, attn_group)
+    )
+
+    if group <= 1024:
+        hidden, gate_back, up_back, unit_sums, down_part_out, feed_in_grad = middle(
+            8,
+            feed_group,
+            grad_group,
+            gate_up_part,
+            down_part,
+            bias_gate_up,
+            unit_live,
+        )
+        gate_sums, up_sums = unit_sums[0], unit_sums[1]
+    else:
+        hidden, gate_back, up_back, gate_sums, up_sums = feed(
+            feed_group, grad_group, gate_up_part, down_part, bias_gate_up, unit_live
+        )
+        feed_part = against(
+            jnp.concatenate([gate_back, up_back], axis=1), gate_up_part
+        ).astype(jnp.bfloat16)
+        feed_in_grad = lax.psum_scatter(feed_part, "context", scatter_dimension=0, tiled=True)
+        feed_in_grad = feed_in_grad.astype(jnp.float32)
+        down_part_out = jnp.dot(hidden, down_part, preferred_element_type=jnp.float32).astype(
+            jnp.bfloat16
+        )
     down_out = lax.psum_scatter(
-        after(down_part_out, feed_in_grad), "context", scatter_dimension=0, tiled=True
+        down_part_out, "context", scatter_dimension=0, tiled=True
     ).astype(jnp.float32)
     block_out = (resid + down_out + bias_down).astype(jnp.bfloat16)
-    feed_in_grad = feed_in_grad.astype(jnp.float32)
-
-    grad_out = cotangent.astype(jnp.float32)
-    resid_part, gain_two_grad = jax.vjp(rms_norm, resid, gain_two)[1](feed_in_grad)
-    resid_grad = grad_out + resid_part
-    attn_grad_low = resid_grad.astype(jnp.bfloat16)
-    mixed_back = summed_half(
-        against(swap_columns(attn_grad_low, core), output_half), core, 1
-    ).astype(jnp.bfloat16)
-    query_acc, key_acc, value_acc = mix_back(mask, queries, keys, values, mixed_back)
-    keyval_acc = jnp.stack(
-        [key_acc.reshape(contexts // 2, 2 * tok, DH), value_acc.reshape(contexts // 2, 2 * tok, DH)],
-        axis=1,
-    ).reshape(contexts, 2 * tok, DH).astype(jnp.bfloat16)
+    (down_sum,), _ = work(2, [(grad_group, after(hidden, feed_in_grad))])
+
+    chips = contexts // 2
     rows_wide = -(-owned // LANES) * LANES
-    attn_grad_rows = jnp.pad(
-        attn_grad_low.reshape(tok, shards, contexts, owned).transpose(2, 0, 1, 3),
-        ((0, 0), (0, 0), (0, 0), (0, rows_wide - owned)),
-    ).reshape(contexts, tok, shards * rows_wide)
-    (gate_sum,), (keyval_acc, attn_grad_rows) = work(
-        3, [(feed_group, gate_back)], [keyval_acc, attn_grad_rows]
-    )
-    attn_grad_rows = attn_grad_rows.reshape(group, shards * rows_wide)
-    keyval_acc = jnp.sum(keyval_acc.astype(jnp.float32), axis=0)
-    keyval_back = jnp.where(core == 0, rotate(keyval_acc, cosine, -sine), keyval_acc).astype(
-        jnp.bfloat16
-    )
-    query_back = (
-        rotate(query_acc.reshape(2 * tok, heads, DH), cosine[:, None, :], -sine[:, None, :])
-        * DH ** (-0.5)
-    ).reshape(2 * tok, heads * DH).astype(jnp.bfloat16)
-    attn_in_grad = summed_half(
-        against(query_back, query_half) + against(keyval_back, keyval_half), core, 0
-    )
-    input_part, gain_one_grad = jax.vjp(rms_norm, source, gain_one)[1](attn_in_grad)
-    input_grad = resid_grad + input_part
-
-    chips = contexts // 2
-
-    def by_chips(field):
-        return field.reshape(2 * tok, chips, field.shape[1] // chips).transpose(1, 0, 2)
+    head_part, keyval_part = HEADS * DH // contexts, DH // chips
 
     def by_owners(field):
         return field.reshape(contexts, owned, field.shape[1])
 
-    attn_group = rms_norm(source_group.astype(jnp.float32), gain_one).astype(jnp.bfloat16)
-    head_part, keyval_part = query_back.shape[1] // chips, keyval_back.shape[1] // chips
-    spare = max(2 * LANES - head_part - keyval_part, 0)
-    back_cols = jnp.concatenate([by_chips(query_back), by_chips(keyval_back)], axis=2)
-    back_cols = jnp.pad(back_cols, ((0, 0), (0, 0), (0, spare)))
-    moving = [back_cols, by_owners(down_sum), by_owners(gate_sum)]
     if group <= 1024:
-        (up_sum, output_sum), (back_cols, down_rows, gate_rows) = work(
-            4, [(feed_group, up_back), (attn_grad_rows, mixed_group)], moving
-        )
+        gains = jnp.concatenate([gain_one, gain_two, jnp.zeros((6, model), jnp.float32)], axis=0)
+        input_grad, sums, up_sum, attn_grad_rows, back_cols, down_rows, gate_rows = back(
+            3,
+            (output_half, query_half, keyval_half),
+            feed_group,
+            gate_back,
+            up_back,
+            by_owners(down_sum),
+            (feed_in_grad, resid, cotangent, inputs, gains),
+            (queries, keyval, mask, *turns),
+        )
+        sums = sums[:4].reshape(4 * model)
+        attn_grad_rows = attn_grad_rows.reshape(group, shards * rows_wide)
+        back_cols = back_cols.reshape(group, back_cols.shape[2])
     else:
+        grad_out = cotangent.astype(jnp.float32)
+        resid_part, gain_two_grad = jax.vjp(rms_norm, resid, gain_two)[1](feed_in_grad)
+        resid_grad = grad_out + resid_part
+        attn_grad_low = resid_grad.astype(jnp.bfloat16)
+        mixed_back = summed_half(
+            against(swap_columns(attn_grad_low, core), output_half), core, 1
+        ).astype(jnp.bfloat16)
+        query_acc, key_acc, value_acc = mix_back(mask, queries, keys, values, mixed_back)
+        keyval_acc = jnp.stack(
+            [key_acc.reshape(contexts // 2, 2 * tok, DH), value_acc.reshape(contexts // 2, 2 * tok, DH)],
+            axis=1,
+        ).reshape(contexts, 2 * tok, DH).astype(jnp.bfloat16)
+        attn_grad_rows = jnp.pad(
+            attn_grad_low.reshape(tok, shards, contexts, owned).transpose(2, 0, 1, 3),
+            ((0, 0), (0, 0), (0, 0), (0, rows_wide - owned)),
+        ).reshape(contexts, tok, shards * rows_wide)
+        (gate_sum,), (keyval_acc, attn_grad_rows) = work(
+            3, [(feed_group, gate_back)], [keyval_acc, attn_grad_rows]
+        )
+        attn_grad_rows = attn_grad_rows.reshape(group, shards * rows_wide)
+        keyval_acc = jnp.sum(keyval_acc.astype(jnp.float32), axis=0)
+        keyval_back = jnp.where(core == 0, rotate(keyval_acc, cosine, -sine), keyval_acc).astype(
+            jnp.bfloat16
+        )
+        query_back = (
+            rotate(query_acc.reshape(2 * tok, heads, DH), cosine[:, None, :], -sine[:, None, :])
+            * DH ** (-0.5)
+        ).reshape(2 * tok, heads * DH).astype(jnp.bfloat16)
+        attn_in_grad = summed_half(
+            against(query_back, query_half) + against(keyval_back, keyval_half), core, 0
+        )
+        input_part, gain_one_grad = jax.vjp(rms_norm, source, gain_one)[1](attn_in_grad)
+        input_grad = resid_grad + input_part
+
+        def by_chips(field):
+            return field.reshape(2 * tok, chips, field.shape[1] // chips).transpose(1, 0, 2)
+
+        spare = max(2 * LANES - head_part - keyval_part, 0)
+        back_cols = jnp.concatenate([by_chips(query_back), by_chips(keyval_back)], axis=2)
+        back_cols = jnp.pad(back_cols, ((0, 0), (0, 0), (0, spare)))
+        moving = [back_cols, by_owners(down_sum), by_owners(gate_sum)]
         (up_sum,), (back_cols, down_rows, gate_rows) = work(4, [(feed_group, up_back)], moving)
-        (output_sum,), _ = work(6, [(attn_grad_rows, mixed_group)])
-    back_cols = back_cols.reshape(group, back_cols.shape[2])
-
-    sums = jnp.concatenate(
-        [
-            gain_one_grad.reshape(model),
-            jnp.sum(attn_grad_low.astype(jnp.float32), axis=0),
-            gain_two_grad.reshape(model),
-            jnp.sum(grad_out, axis=0),
-            gate_sums.reshape(units),
-            up_sums.reshape(units),
-        ]
-    )
-    sums = sums + across(sums, 1)
-    sums = sums + across(sums, 2)
-    mine = [
-        lax.dynamic_index_in_dim(
-            sums[i * model : (i + 1) * model].reshape(shards, contexts, owned), shard, 0, False
-        )
-        for i in range(4)
-    ]
-    wide = 4 * owned + 2 * units
+        back_cols = back_cols.reshape(group, back_cols.shape[2])
+
+        sums = jnp.concatenate(
+            [
+                gain_one_grad.reshape(model),
+                jnp.sum(attn_grad_low.astype(jnp.float32), axis=0),
+                gain_two_grad.reshape(model),
+                jnp.sum(grad_out, axis=0),
+            ]
+        )
+
+    sums = jnp.concatenate([sums, gate_sums.reshape(units), up_sums.reshape(units)])
+    unit_owned = 2 * ff // (shards * contexts)
+    mine = sums[: 4 * model].reshape(4, shards, contexts, owned).transpose(2, 0, 1, 3)
+    unit_sums = lax.dynamic_update_slice_in_dim(
+        jnp.zeros((2 * shards, per_shard * LANES), jnp.float32),
+        sums[4 * model :].reshape(2 * shards, block),
+        unit_start * LANES,
+        1,
+    )
+    unit_sums = unit_sums.reshape(shards, contexts, unit_owned).transpose(1, 0, 2)
+    at = 4 * shards * owned
+    wide = at + shards * unit_owned
     tall = -(-wide // (8 * LANES)) * LANES
     vectors = jnp.concatenate(
-        mine
-        + [
-            jnp.broadcast_to(sums[4 * model :], (contexts, 2 * units)),
+        [
+            mine.reshape(contexts, at),
+            unit_sums.reshape(contexts, wide - at),
             jnp.zeros((contexts, 8 * tall - wide), jnp.float32),
         ],
         axis=1,
     ).reshape(contexts, 8, tall)
     if owned % 16 == 0:
-        _, (up_rows, vectors, back_rows) = work(
-            5, [(attn_group, back_cols)], [by_owners(up_sum), vectors], True
+        (output_sum,), (vectors, up_rows, back_rows) = work(
+            5,
+            [(attn_group, back_cols), (attn_grad_rows, mixed_group)],
+            [vectors, by_owners(up_sum)],
+            True,
+            True,
         )
     else:
-        (back_sum,), (up_rows, vectors) = work(
-            5, [(attn_group, back_cols)], [by_owners(up_sum), vectors]
+        (back_sum,), (vectors, up_rows) = work(
+            5, [(attn_group, back_cols)], [vectors, by_owners(up_sum)], False, True
         )
         _, (back_rows,) = work(7, [], [by_owners(back_sum)])
-    vectors = vectors.reshape(contexts, 8 * tall)
-    own = jnp.sum(vectors[:, : 4 * owned], axis=0).reshape(4, owned)
-    unit_sums = join_units(
-        vectors[:, 4 * owned : wide], 2, shards, width, per_shard
-    )
-    unit_owned = 2 * ff // (shards * contexts)
-    gate_up_bias_grad = lax.dynamic_slice_in_dim(
-        unit_sums, (shard * contexts + place) * unit_owned, unit_owned
+        (output_sum,), _ = work(6, [(attn_grad_rows, mixed_group)])
+    vectors = vectors.reshape(8 * tall)
+    own = vectors[:at].reshape(4, shards, owned)
+    own = lax.dynamic_index_in_dim(own, shard, 1, False)
+    gate_up_bias_grad = lax.dynamic_index_in_dim(
+        vectors[at:wide].reshape(shards, unit_owned), shard, 0, False
     )
     pieces = unit_pieces(contexts, shards, width, per_shard)
-    down_weight_grad = lay([down_rows], pieces, ff, True)
-    gate_up_grad = lay([gate_rows, up_rows], pieces, ff)
-    def by_columns(field):
-        return (
-            field.reshape(chips, 2, owned, field.shape[2])
-            .transpose(2, 1, 0, 3)
-            .reshape(owned, contexts * field.shape[2])
-            .astype(jnp.float32)
-        )
-
-    query_grad = by_columns(back_rows[:, :, :head_part])
-    keyval_grad = by_columns(back_rows[:, :, head_part : head_part + keyval_part])
-    output_weight_grad = output_sum[:owned].astype(jnp.float32).T
+    down_grad, gate_up_grad, query_grad, keyval_grad, output_grad = lay(
+        pieces,
+        owned,
+        (ff, 2 * ff, HEADS * DH, 2 * DH, model),
+        down_rows,
+        gate_rows,
+        up_rows,
+        back_rows,
+        output_sum,
+    )
+    output_weight_grad, down_weight_grad = output_grad.T, down_grad.T
     return (
         block_out,
         input_grad,

time: 691 us -> 619 us (0.90)
  matrix products: 35 us -> 0 us
  Pallas kernels: 545 us -> 573 us
  local copies, waits for them, and re-layouts: 41.3 us -> 14.6 us
  other arithmetic: 31.2 us -> 7.29 us
  waiting for transfers between devices: 7.94 us -> 0.7 us
    dot_general x5 -> x0, matrix products: 35 us -> none  [the longest x4 27.3 us: against(): lax.dot_general(left, weight, (((1,), (1,)), ((), ())), preferred_element...]
    pallas_call x8 -> x5, Pallas kernels: 281 us -> 308 us  [the longest x1 120 us: back(): pl.pallas_call(functools.partial(back_kernel, gate, up, swaps), in_specs=...]
    unnamed x103 -> x11, local copies, waits for them, and re-layouts: 14.9 us -> 3.75 us
    convert_element_type x7 -> x0, local copies, waits for them, and re-layouts: 8.51 us -> none  [the longest x3 2.27 us: by_columns(): return field.reshape(chips, 2, owned, field.shape[2]).transpose(2, 1, 0,...]
    reduce_sum x8 -> x0, other arithmetic: 7.84 us -> none  [the longest x2 3.85 us: rms_norm(): field * lax.rsqrt(jnp.mean(field * field, axis=-1, keepdims=True) + EPS)]
  transfers between devices with their start and end apart: 9 -> 2, of which waited for: 2 -> 0; matrix products, arithmetic and copies ran while one was open for 11% -> 3% of each run, Pallas kernels for 68% -> 82%
where the time goes in v5:
time: 619 us; the launch traced here: 610 us
  Pallas kernels  573 us (93%)
  local copies, waits for them, and re-layouts  14.6 us (2%)
  between operations  14.5 us (2%)
  other arithmetic  7.29 us (1%)
    pallas_call x1, Pallas kernels, opening(): pl.pallas_call(functools.partial(opening_kernel, gathers, spreads), in_sp...  264 us
    pallas_call x1, Pallas kernels, back(): pl.pallas_call(functools.partial(back_kernel, gate, up, swaps), in_specs=...  120 us
    pallas_call x2, Pallas kernels, work(): pl.pallas_call(functools.partial(work_kernel, made, swaps, chained, summe...  108 us
    pallas_call x1, Pallas kernels, middle(): pl.pallas_call(middle_kernel, in_specs=[hbm] * 4 + [vmem] * 2, out_specs=...  73.7 us
  transfers between devices with their start and end apart: 2, of which 0 were waited for; matrix products, arithmetic and copies ran while one was open for 3% of the time, Pallas kernels for 82%

profile of v5, /device:TPU:0, one launch (start us, length us, event | category | flops | bytes accessed | tf_op | source)
XLA Modules:
  0.0 609.8 jit_solution(6554178884160912313)
XLA Ops:
  7.2 0.7 all-gather.2.cloned.1.call-update
  8.0 1.3 reshape.137.refs_5_
  9.2 1.3 reshape.138.refs_6_
  10.5 1.3 reshape.139.refs_7_
  11.8 1.3 reshape.140.refs_8_
  13.1 0.6 copy.32
  13.7 1.3 reshape.141.refs_9_
  15.0 0.8 dynamic_slice.14
  15.7 0.5 fusion.5
  16.3 0.8 pad_maximum_fusion
  17.1 2.1 fusion.4.refs_11_.refs_14_
  19.3 264.5 %shard_map.220 = (bf16[128,640]{1,0:T(8,128)(2,1)}, bf16[2560,256]{1,0:T(8,128)(2,1)}, bf16[2560,1280]{1,0:T(8,128)(2,1)}, bf16[2560,1280]{1,0:T(8,128)(2,1)}, b...) custom-call(bf16[640,512]{1,0:T(8,128)(2,1)} %refs_0_.1, ...), custom_call_target="tpu_custom_call" | custom-call | bytes 700000000 | tf_op jit(solution)/shard_map/pallas_call | solution.py:481
  283.8 0.9 bitcast_convert_fusion
  284.8 0.6 copy.31
  285.4 73.7 %shard_map.221 = (bf16[1024,1024]{1,0:T(8,128)(2,1)}, bf16[1024,1024]{1,0:T(8,128)(2,1)}, bf16[1024,1024]{1,0:T(8,128)(2,1)}, f32[8,1024]{1,0:T(8,128)}, bf16[10...) custom-call(bf16[1024,2560]{1,0:T(8,128)(2,1)} %bitcast.39, bf16[1024,2560]{1,0:T(8,128)(2,1)} %all-gather.2.cloned.1.call-done.refs_1_.refs_0_, ...), custom_call_target="tpu_custom_call" | custom-call | bytes 200000000 | tf_op jit(solution)/shard_map/pallas_call | solution.py:1284
  359.3 0.7 maximum_maximum_fusion.1.refs_11_
  360.0 0.9 slice_reduce_fusion.2
  360.9 0.1 reshape.151
  361.1 0.1 reshape.152
  361.2 52.6 %shard_map.222 = bf16[640,1024]{1,0:T(8,128)(2,1)} custom-call(bf16[1024,2560]{1,0:T(8,128)(2,1)} %all-gather.2.cloned.1.call-done.refs_1_.refs_0_, bf16[1024,1024]{1,0:T(8,128)(2,1)} %get-tuple-element.60.refs_1_), custom_call_target="tpu_custom_call" | custom-call | bytes 150000000 | tf_op jit(solution)/shard_map/pallas_call | solution.py:732
  413.7 119.6 %shard_map.223 = (f32[128,2560]{1,0:T(8,128)}, f32[8,2560]{1,0:T(8,128)}, bf16[640,1024]{1,0:T(8,128)(2,1)}, bf16[8,128,512]{2,1,0:T(8,128)(2,1)}, bf16[4,256,38...) custom-call(bf16[2560,1280]{1,0:T(8,128)(2,1)} %get-tuple-element.53.refs_0_, ...), custom_call_target="tpu_custom_call" | custom-call | bytes 400000000 | tf_op jit(solution)/shard_map/pallas_call | solution.py:953
  533.3 0.9 slice.47
  534.2 0.1 reshape_reshape.3
  534.3 0.1 reshape.150
  534.5 0.7 copy.36
  535.2 55.8 %shard_map.224 = (bf16[640,384]{1,0:T(8,128)(2,1)}, bf16[128,2560]{1,0:T(8,128)(2,1)}, f32[8,128]{1,0:T(8,128)}, bf16[8,80,1024]{2,1,0:T(8,128)(2,1)}, bf16[8,80,384]{2,1,0:T(8,128)(2,1)}, /*index=5*/f32[8,512]{1,0:T(8,128)}) custom-call(bf16[1024,2560]{1,0:T(8,128)(2,1)} %bitcast.43, bf16[1024,384]{1,0:T(8,128)(2,1)} %bitcast.46, ...), custom_call_target="tpu_custom_call" | custom-call | bytes 150000000 | tf_op jit(solution)/shard_map/pallas_call | solution.py:732
  591.0 0.7 copy.34
  591.9 6.5 %shard_map.225 = (f32[80,7680]{1,0:T(8,128)}, f32[80,15360]{1,0:T(8,128)}, f32[80,2560]{1,0:T(8,128)}, f32[80,512]{1,0:T(8,128)}, f32[80,2560]{1,0:T(8,128)}) custom-call(bf16[8,80,1024]{2,1,0:T(8,128)(2,1)} %get-tuple-element.72.down_ref, bf16[8,80,1024]{2,1,0:T(8,128)(2,1)} %get-tuple-element.73.gate_ref, bf16[8,80,1024]{2,1,0:T(8,128)(2,1)} %get-tuple-element.74.up_ref, ...), custom_call_target="tpu_custom_call" | custom-call | tf_op jit(solution)/shard_map/pallas_call | solution.py:161
  598.4 0.6 constant_dynamic-slice_fusion.3
  599.0 0.5 fusion.6
  599.6 2.1 add_convert_fusion
  601.6 1.1 copy.39
  (34 shorter events, 0.6 us)
Async XLA Ops:
  7.2 278.2 %all-gather.2.cloned.1.call-start = ((), (), s32[]{:S(2)}) async-start(), calls=%async_computation.1 | async-start | bytes 5898240 | tf_op jit(solution)/shard_map/all_gather | solution.py:69
  7.9 591.7 %reduce-scatter.2.cloned.1.call-start = ((), (), s32[]{:S(2)}) async-start(), calls=%async_computation.2 | async-start | bytes 5898240 | tf_op jit(solution)/shard_map/reduce_scatter | solution.py:1437
  591.9 7.6 %copy-start = (f32[128,2560]{1,0:T(8,128)S(1)}, f32[128,2560]{1,0:T(8,128)}, u32[]{:S(2)}) copy-start(f32[128,2560]{1,0:T(8,128)} %get-tuple-element.47.refs_8_) | copy-start | bytes 3932164
  598.4 3.2 copy-start.1
Sparse Core Ops, SparseCore 0:
  9.7 58.7 all-gather.1
  359.2 66.0 reduce-scatter.1

commit v6 on v5

--- a/solution.py
+++ b/solution.py
@@ -58,9 +58,15 @@
 
 
 VMEM_LIMIT = 56 * 1024 * 1024
-BACK_LIMIT = 60 * 1024 * 1024
+BACK_LIMIT = 61 * 1024 * 1024
 LANES = 128
 MESH = pl.DeviceIdType.MESH
+LINE = (
+    ((1, 0), (1, 2), (1, 3)),
+    ((2, 1), (0, 4), (2, 3)),
+    ((1, 1), (3, 3), (1, 4)),
+    ((2, 0), (2, 2), (2, 4)),
+)
 GELU = 0.7978845608028654
 CUBE = 0.044715
 
@@ -134,19 +140,25 @@
 
 
 def lay_kernel(pieces, down_ref, gate_ref, up_ref, back_ref, output_ref, *outs):
-    down_out, gate_up_out, query_out, keyval_out, output_out = outs
+    down_leaves, gate_up_leaves, query_out, keyval_out, output_out, down_out, gate_up_out, leave = outs
     units, owned = down_out.shape[1], down_out.shape[0]
     contexts = back_ref.shape[0]
     head_part, keyval_part = query_out.shape[1] // contexts, keyval_out.shape[1] // contexts
-    for source, out, offset in (
-        (down_ref, down_out, 0),
-        (gate_ref, gate_up_out, 0),
-        (up_ref, gate_up_out, units),
+    copies = []
+    for i, (source, out, leaves, offset) in enumerate(
+        (
+            (down_ref, down_out, down_leaves, 0),
+            (gate_ref, gate_up_out, gate_up_leaves, 0),
+            (up_ref, gate_up_out, gate_up_leaves, units),
+        )
     ):
         for at, column, wide, first in pieces:
             out[:, offset + first : offset + first + wide] = source[
                 at, :, column : column + wide
             ].astype(jnp.float32)
+        whole = pl.ds(offset, units)
+        copies.append(pltpu.make_async_copy(out.at[:, whole], leaves.at[:, whole], leave.at[i]))
+        copies[-1].start()
     for at in range(contexts):
         slot = (at % 2) * (contexts // 2) + at // 2
         part = back_ref[at].astype(jnp.float32)
@@ -155,14 +167,19 @@
             :, head_part : head_part + keyval_part
         ]
     output_out[...] = output_ref[:owned].astype(jnp.float32)
+    for copy in copies:
+        copy.wait()
 
 
 def lay(pieces, owned, widths, *fields):
     return pl.pallas_call(
         functools.partial(lay_kernel, pieces),
         in_specs=[pl.BlockSpec(memory_space=pltpu.VMEM)] * len(fields),
-        out_specs=[pl.BlockSpec(memory_space=pltpu.VMEM)] * len(widths),
+        out_specs=[pl.BlockSpec(memory_space=pl.ANY)] * 2
+        + [pl.BlockSpec(memory_space=pltpu.VMEM)] * (len(widths) - 2),
         out_shape=[jax.ShapeDtypeStruct((owned, wide), jnp.float32) for wide in widths],
+        scratch_shapes=[pltpu.VMEM((owned, wide), jnp.float32) for wide in widths[:2]]
+        + [pltpu.SemaphoreType.DMA((3,))],
         compiler_params=pltpu.CompilerParams(vmem_limit_bytes=VMEM_LIMIT),
     )(*fields)
 
@@ -274,31 +291,62 @@
         self.sent.append(to_device("context", source, target, send, receive, place))
         self.sent[-1].start()
 
-    def came(self, k, core):
-        return 2 * lax.rem(self.chip + self.chips - k, self.chips) + core
+    def other(self, k):
+        if self.chips == 4:
+            beside = self.chip + 1 - 2 * lax.rem(self.chip, 2)
+            return (self.chip, beside, lax.rem(self.chip + 2, 4), 3 - self.chip)[k]
+        return lax.rem(self.chip + self.chips - k, self.chips)
+
+    def to_chip(self, block, k, place):
+        self.push(block, block, self.send.at[k], self.receive.at[k], 2 * place + self.core)
 
     def post(self):
-        self.kept = pltpu.make_async_copy(self.own, self.group.at[self.me], self.local)
+        mine = self.group.at[self.me]
+        self.kept = pltpu.make_async_copy(self.own, mine, self.local)
         self.kept.start()
-        for k in range(1, self.chips):
-            place = 2 * lax.rem(self.chip + k, self.chips) + self.core
-            self.push(self.own, self.group.at[self.me], self.send.at[k], self.receive.at[k], place)
-        self.push(
-            self.own, self.group.at[self.me], self.send_on.at[0], self.receive_on.at[0], self.mate
-        )
+        first = len(self.sent)
+        for k in range(1, 3 if self.chips == 4 else self.chips):
+            place = self.other(k) if self.chips == 4 else lax.rem(self.chip + k, self.chips)
+            self.sent.append(
+                to_device(
+                    "context",
+                    self.own,
+                    mine,
+                    self.send.at[k],
+                    self.receive.at[k],
+                    2 * place + self.core,
+                )
+            )
+        posted = self.sent[first:]
+        for core, order in enumerate((posted, posted[::-1])):
+
+            @pl.when(self.core == core)
+            def _(order=order):
+                for copy in order:
+                    copy.start()
+
+        self.push(self.own, mine, self.send_on.at[0], self.receive_on.at[0], self.mate)
+
+    def arrived(self, k):
+        block = self.group.at[2 * self.other(k) + self.core]
+        to_device(
+            "context", block, block, self.send.at[k], self.receive.at[k], self.mate
+        ).wait_recv()
+        self.push(block, block, self.send_on.at[k], self.receive_on.at[k], self.mate)
+
+    def relay(self):
+        if self.chips == 4:
+            self.arrived(2)
+            self.to_chip(self.group.at[2 * self.other(2) + self.core], 3, self.other(1))
 
     def pass_on(self):
-        for k in range(1, self.chips):
-            block = self.group.at[self.came(k, self.core)]
-            to_device(
-                "context", block, block, self.send.at[k], self.receive.at[k], self.mate
-            ).wait_recv()
-            self.push(block, block, self.send_on.at[k], self.receive_on.at[k], self.mate)
+        for k in (1, 3) if self.chips == 4 else range(1, self.chips):
+            self.arrived(k)
 
     def finish(self):
         self.kept.wait()
         for k in range(self.chips):
-            block = self.group.at[self.came(k, 1 - self.core)]
+            block = self.group.at[2 * (self.other(k) if k else self.chip) + 1 - self.core]
             to_device(
                 "context", block, block, self.send_on.at[k], self.receive_on.at[k], self.mate
             ).wait_recv()
@@ -429,8 +477,8 @@
     swap(1, mixed.at[core], mixed.at[core])
 
     output_of.pass_on()
+    gate_up_of.post()
     output_of.finish()
-    gate_up_of.post()
     down_of.post()
     fetch(3, output_of.whole, big)
     swaps[1].wait_recv()
@@ -452,10 +500,13 @@
     feed_own[...] = rms_norm(resid, vector(2)).astype(jnp.bfloat16)
     spreads[1].post()
     spreads[0].post()
+    spreads[2].relay()
     spreads[2].pass_on()
     keyval_ref[...] = keyval[...]
     gate_up_of.pass_on()
+    spreads[1].relay()
     down_of.pass_on()
+    spreads[0].relay()
     spreads[1].pass_on()
     spreads[0].pass_on()
     for part in spreads:
@@ -629,7 +680,7 @@
         return finish
 
 
-def work_kernel(products, exchanges, chained, summed, *refs):
+def work_kernel(products, exchanges, chained, summed, packed, *refs):
     refs = list(refs)
 
     def take(count):
@@ -642,6 +693,15 @@
     results = take(len(products))
     moved = take(len(exchanges))
     total_ref = take(1)[0] if summed else None
+    held = [take(2) for _ in products]
+    loads = take(1)[0] if products else None
+    copies = []
+    for i, (pair, targets) in enumerate(zip(operands, held)):
+        for j in range(2):
+            copies.append(pltpu.make_async_copy(pair[j], targets[j], loads.at[i, j]))
+            copies[-1].start()
+    if packed:
+        apart = take(1)[0]
     product_scratch = [take(len(p.scratch())) for p in products]
     exchange_scratch = [take(len(e.scratch())) for e in exchanges]
     _, along_x, along_y, _ = shard_places()
@@ -668,21 +728,33 @@
 
     for exchange, array, out, scratch in zip(exchanges, arrays, moved, exchange_scratch):
         finishes.append(exchange.start(lambda j, array=array: array.at[j], out, *scratch))
-    for product, (left, right), scratch in zip(products, operands, product_scratch):
+    for i, (product, (left, right), scratch) in enumerate(zip(products, held, product_scratch)):
         product.bind(left, right, *scratch)
+        copies[2 * i].wait()
+        copies[2 * i + 1].wait()
+        if i == 1:
+            if packed:
+                wide = apart.shape[1] // 4
+                apart[...] = jnp.zeros_like(apart)
+                for j in range(4):
+                    apart[:, j * wide : j * wide + packed] = left[:, j * packed : (j + 1) * packed]
+                product.left = apart
+            products[0].middle()
         product.begin()
     if summed:
         finishes.pop(0)()
         stage[0] = jnp.sum(arrived[...], axis=0)
         hop(0, along_x)
-    for product in products:
-        product.middle()
-    if summed:
-        steps[0].wait_recv()
-        stage[1] = stage[0] + stage_came[0]
-        hop(1, along_y)
+    if len(products) == 1:
+        products[0].middle()
     for i, product in enumerate(products):
+        if i == 1:
+            product.middle()
         product.finish(results[i])
+        if i == 0 and summed:
+            steps[0].wait_recv()
+            stage[1] = stage[0] + stage_came[0]
+            hop(1, along_y)
         if chained and i == 0:
             rows = product.rows // exchanges[-1].count
             finishes.append(
@@ -703,9 +775,14 @@
         finish()
 
 
-def work(number, products=(), exchanges=(), chained=False, summed=False):
+def work(number, products=(), exchanges=(), chained=False, summed=False, packed=0):
     contexts = lax.axis_size("context")
     made = [Product(left.shape, right.shape) for left, right in products]
+    apart = []
+    if packed:
+        rows, right = products[1][0].shape[0], products[1][1]
+        apart = [(rows, 4 * -(-packed // LANES) * LANES)]
+        made[1] = Product(apart[0], right.shape)
     swaps = [Exchange(array.shape[0], contexts // array.shape[0]) for array in exchanges]
     results = [jax.ShapeDtypeStruct((p.rows, p.wide), jnp.bfloat16) for p in made]
     moved = [jax.ShapeDtypeStruct(array.shape, array.dtype) for array in exchanges]
@@ -714,7 +791,11 @@
         moved.append(
             jax.ShapeDtypeStruct((contexts, made[0].rows // contexts, made[0].wide), jnp.bfloat16)
         )
-    scratch = [shape for part in made + swaps for shape in part.scratch()]
+    scratch = [pltpu.VMEM(operand.shape, operand.dtype) for pair in products for operand in pair]
+    if made:
+        scratch.append(pltpu.SemaphoreType.DMA((len(made), 2)))
+    scratch += [pltpu.VMEM(each, jnp.bfloat16) for each in apart]
+    scratch += [shape for part in made + swaps for shape in part.scratch()]
     totals = []
     if summed:
         block = exchanges[0].shape[1:]
@@ -730,8 +811,8 @@
     vmem = pl.BlockSpec(memory_space=pltpu.VMEM)
     hbm = pl.BlockSpec(memory_space=pl.ANY)
     outs = pl.pallas_call(
-        functools.partial(work_kernel, made, swaps, chained, summed),
-        in_specs=[vmem] * (2 * len(made)) + [hbm] * len(exchanges),
+        functools.partial(work_kernel, made, swaps, chained, summed, packed),
+        in_specs=[hbm] * (2 * len(made) + len(exchanges)),
         out_specs=[vmem] * len(made) + [hbm] * len(swaps) + [vmem] * len(totals),
         out_shape=results + moved + totals,
         scratch_shapes=scratch,
@@ -830,12 +911,11 @@
     sums_ref[1:2] = jnp.sum(attn_grad.astype(full), axis=0, keepdims=True)
     sums_ref[2:3] = gain_two_grad
     sums_ref[3:4] = jnp.sum(cotangent, axis=0, keepdims=True)
-    wide = rows_blocks.shape[2] // shards
     rows_blocks[...] = jnp.zeros_like(rows_blocks)
     for j in range(contexts):
         for shard in range(shards):
             start = (shard * contexts + j) * owned
-            rows_blocks[j, :, shard * wide : shard * wide + owned] = attn_grad[
+            rows_blocks[j, :, shard * owned : (shard + 1) * owned] = attn_grad[
                 :, start : start + owned
             ]
     finishes.append(rows_swap.start(lambda j: rows_blocks.at[j], rows_out, *rows_sems))
@@ -940,7 +1020,7 @@
     slots = attention[2].shape[1]
     half, rows, chips = model // 2, 2 * tok, contexts // 2
     owned = model // (shards * contexts)
-    wide = -(-owned // LANES) * LANES
+    wide = -(-shards * owned // LANES) * LANES
     gate = Product(feed_group.shape, gate_back.shape)
     up = Product(feed_group.shape, up_back.shape)
     cols = max(half // chips + DH // chips, 2 * LANES)
@@ -958,7 +1038,7 @@
             shape((tok, model), full),
             shape((8, model), full),
             shape((up.rows, up.wide), low),
-            shape((contexts, tok, shards * wide), low),
+            shape((contexts, tok, wide), low),
             shape((chips, rows, cols), low),
             shape(down_rows.shape, low),
             shape((contexts, tall, gate.wide), low),
@@ -981,7 +1061,7 @@
             pltpu.VMEM((slots, DH), low),
             pltpu.VMEM((chips, rows, DH), low),
             pltpu.VMEM((rows, DH), low),
-            pltpu.VMEM((contexts, tok, shards * wide), low),
+            pltpu.VMEM((contexts, tok, wide), low),
             pltpu.VMEM((chips, rows, cols), low),
             pltpu.VMEM((gate.rows, gate.wide), low),
             dma((6,)),
@@ -1141,7 +1221,8 @@
         return taken
 
     feed_ref, grad_ref, weight_ref, down_ref, bias_ref, live_ref = take(6)
-    hidden_ref, gate_back_ref, up_back_ref, sums_ref, down_out_ref, feed_grad_ref = take(6)
+    *leaving, down_out_ref, sums_ref, feed_grad_ref = take(6)
+    hidden_ref, gate_back_ref, up_back_ref, down_rows, leave, down_leave = take(6)
     gate_weight, up_weight, down_weight, feed_rows, grad_rows = take(5)
     own_part, mate_out, mate_in, sent_out, came, swap_in = take(6)
     weight_load, row_load, mate_send, mate_receive, send, receive = take(6)
@@ -1150,12 +1231,13 @@
     chip, core = me // 2, lax.rem(me, 2)
     mate = me + 1 - 2 * core
     units, model = down_weight.shape
-    rows, half, wide = feed_rows.shape[1], model // 2, 256
+    rows, half, wide = feed_rows.shape[0], model // 2, 256
     blocks = units // wide
     full, low = jnp.float32, jnp.bfloat16
     mine = pl.ds(pl.multiple_of(core * half, LANES), half)
     theirs = pl.ds(pl.multiple_of((1 - core) * half, LANES), half)
-    targets = [lax.rem(chip + 1 + i, chips) for i in range(chips)]
+    targets = [3 * (1 - chip // 2), lax.rem(2 + 3 * chip, 5), 1 + lax.rem(chip, 2), chip]
+    inner = lax.rem(chip + 1, 4) // 2
 
     def token_rows(i):
         return pl.ds(pl.multiple_of(targets[i] * rows, rows), rows)
@@ -1172,8 +1254,8 @@
     def row_loads(i):
         at = token_rows(i)
         return [
-            pltpu.make_async_copy(feed_ref.at[at], feed_rows.at[i % 2], row_load.at[i, 0]),
-            pltpu.make_async_copy(grad_ref.at[at], grad_rows.at[i % 2], row_load.at[i, 1]),
+            pltpu.make_async_copy(feed_ref.at[at], feed_rows, row_load.at[i, 0]),
+            pltpu.make_async_copy(grad_ref.at[at], grad_rows.at[at], row_load.at[i, 1]),
         ]
 
     for copy in row_loads(0):
@@ -1181,15 +1263,64 @@
     for j in range(blocks):
         for copy in weight_loads(j):
             copy.start()
-    greet((), [mate] + [2 * targets[i] + core for i in range(chips - 1)])
+    greet((), [lax.rem(me + k, 2 * chips) for k in range(1, 2 * chips)])
     sums_ref[...] = jnp.zeros_like(sums_ref)
-    to_mate, to_chips = [], []
+    to_mate, left = [], []
+
+    def passed(which, i, chip_at):
+        receiver, slot = LINE[chip_at][i]
+        return to_device(
+            "context",
+            sent_out.at[which, i],
+            came.at[which, slot],
+            send.at[which, i],
+            receive.at[which, slot],
+            2 * receiver + core,
+        )
+
+    def arrived(which, slot):
+        part = came.at[which, slot]
+        to_device(
+            "context", part, part, send.at[which, 0], receive.at[which, slot], mate
+        ).wait_recv()
+        own_part[which] += part[...].astype(full)
+
+    def reduce(i, which, part):
+        step = i
+        if step >= 1:
+            to_mate[step - 1].wait_send()
+        mate_out[which] = part(theirs).astype(low)
+        to_mate.append(
+            to_device(
+                "context",
+                mate_out.at[which],
+                mate_in.at[i % 2],
+                mate_send.at[step],
+                mate_receive.at[step],
+                mate,
+            )
+        )
+        to_mate[-1].start()
+        own_part[which] = part(mine)
+        to_mate[-1].wait_recv()
+        own_part[which] += mate_in[i % 2].astype(full)
+        if i + 1 == chips:
+            return
+
+        @pl.when(inner == 1)
+        def _():
+            arrived(which, i)
+
+        sent_out[which, i] = own_part[which].astype(low)
+        for chip_at in range(chips):
+
+            @pl.when(chip == chip_at)
+            def _(chip_at=chip_at):
+                passed(which, i, chip_at).start()
+
     for i in range(chips):
         for copy in row_loads(i):
             copy.wait()
-        if i + 1 < chips:
-            for copy in row_loads(i + 1):
-                copy.start()
         at = token_rows(i)
 
         def block(j, carry, i=i, at=at):
@@ -1198,10 +1329,10 @@
                     copy.wait()
             cut = pl.ds(pl.multiple_of(j * wide, wide), wide)
             later = pl.ds(pl.multiple_of(units + j * wide, wide), wide)
-            feed = feed_rows[i % 2]
+            feed = feed_rows[...]
             gate = jnp.dot(feed, gate_weight[:, cut], preferred_element_type=full) + bias_ref[:, cut]
             up = jnp.dot(feed, up_weight[:, cut], preferred_element_type=full) + bias_ref[:, later]
-            back = against(grad_rows[i % 2], down_weight[cut])
+            back = against(grad_rows[at, :], down_weight[cut])
             live = live_ref[:, cut]
             square = gate * gate
             bend = jnp.tanh(GELU * gate * (1.0 + CUBE * square))
@@ -1218,58 +1349,61 @@
             return carry
 
         lax.fori_loop(0, blocks, block, 0)
-
-        def feed_part(columns):
+        if i + 1 < chips:
+            for copy in row_loads(i + 1):
+                copy.start()
+        for j, made in enumerate((hidden_ref, gate_back_ref, up_back_ref)):
+            left.append(pltpu.make_async_copy(made.at[at], leaving[j].at[at], leave.at[i, j]))
+            left[-1].start()
+
+        def feed_part(columns, at=at):
             return against(gate_back_ref[at, :], gate_weight[columns, :]) + against(
                 up_back_ref[at, :], up_weight[columns, :]
             )
 
-        mate_out[i] = feed_part(theirs).astype(low)
-        to_mate.append(
-            to_device(
-                "context", mate_out.at[i], mate_in.at[i], mate_send.at[i], mate_receive.at[i], mate
-            )
-        )
-        to_mate[-1].start()
-        own_part[...] = feed_part(mine)
-        to_mate[-1].wait_recv()
-        if i + 1 < chips:
-            sent_out[i] = (own_part[...] + mate_in[i].astype(full)).astype(low)
-            to_chips.append(
-                to_device(
-                    "context",
-                    sent_out.at[i],
-                    came.at[i],
-                    send.at[i],
-                    receive.at[i],
-                    2 * targets[i] + core,
-                )
-            )
-            to_chips[-1].start()
-        else:
-            own_part[...] += mate_in[i].astype(full)
-        down_out_ref[at, :] = jnp.dot(
+        reduce(i, 0, feed_part)
+    for i in range(chips):
+        at = token_rows(i)
+        if i >= 2:
+            left[-2].wait()
+        down_rows[i % 2] = jnp.dot(
             hidden_ref[at, :], down_weight[...], preferred_element_type=full
         ).astype(low)
-    for i, copy in enumerate(to_chips):
-        copy.wait_recv()
-        own_part[...] += came[i].astype(full)
+        left.append(pltpu.make_async_copy(down_rows.at[i % 2], down_out_ref.at[at], down_leave.at[i]))
+        left[-1].start()
     tok = rows // 2
     own_rows = pl.ds(pl.multiple_of(core * tok, tok), tok)
     mate_rows = pl.ds(pl.multiple_of((1 - core) * tok, tok), tok)
-    last = to_device(
-        "context",
-        own_part.at[mate_rows],
-        swap_in,
-        mate_send.at[chips],
-        mate_receive.at[chips],
-        mate,
-    )
-    last.start()
-    feed_grad_ref[:, mine] = own_part[own_rows, :]
-    last.wait_recv()
-    feed_grad_ref[:, theirs] = swap_in[...]
-    for copy in to_mate + to_chips + [last]:
+    lasts = []
+
+    def complete(which, out):
+        for slot, missing in ((3, 0), (4, chips - 1)):
+
+            @pl.when(chip != missing)
+            def _(slot=slot):
+                arrived(which, slot)
+
+        lasts.append(
+            to_device(
+                "context",
+                own_part.at[which, mate_rows],
+                swap_in.at[which],
+                mate_send.at[chips + which],
+                mate_receive.at[chips + which],
+                mate,
+            )
+        )
+        lasts[-1].start()
+        out[:, mine] = own_part[which, own_rows]
+
+    complete(0, feed_grad_ref)
+    lasts[0].wait_recv()
+    feed_grad_ref[:, theirs] = swap_in[0]
+    for copy in left[: 3 * chips] + left[-2:]:
+        copy.wait()
+    for i in range(chips - 1):
+        passed(0, i, 0).wait_send()
+    for copy in to_mate[-1:] + lasts:
         copy.wait_send()
 
 
@@ -1284,27 +1418,29 @@
     return pl.pallas_call(
         middle_kernel,
         in_specs=[hbm] * 4 + [vmem] * 2,
-        out_specs=[vmem] * 6,
+        out_specs=[hbm] * 4 + [vmem] * 2,
         out_shape=[shape((group, units), low)] * 3
-        + [shape((8, units), full), shape((group, model), low), shape((rows // 2, model), full)],
-        scratch_shapes=[
+        + [shape((group, model), low), shape((8, units), full), shape((rows // 2, model), full)],
+        scratch_shapes=[pltpu.VMEM((group, units), low)] * 3
+        + [pltpu.VMEM((2, rows, model), low), dma((chips, 3)), dma((chips,))]
+        + [
             pltpu.VMEM((model, units), low),
             pltpu.VMEM((model, units), low),
             pltpu.VMEM((units, model), low),
-            pltpu.VMEM((2, rows, model), low),
-            pltpu.VMEM((2, rows, model), low),
-            pltpu.VMEM((rows, half), full),
-            pltpu.VMEM((chips, rows, half), low),
-            pltpu.VMEM((chips, rows, half), low),
-            pltpu.VMEM((chips, rows, half), low),
-            pltpu.VMEM((chips, rows, half), low),
-            pltpu.VMEM((rows // 2, half), full),
+            pltpu.VMEM((rows, model), low),
+            pltpu.VMEM((group, model), low),
+            pltpu.VMEM((1, rows, half), full),
+            pltpu.VMEM((1, rows, half), low),
+            pltpu.VMEM((2, rows, half), low),
+            pltpu.VMEM((1, chips - 1, rows, half), low),
+            pltpu.VMEM((1, chips + 1, rows, half), low),
+            pltpu.VMEM((1, rows // 2, half), full),
             dma((units // 256, 3)),
             dma((chips, 2)),
             dma((chips + 1,)),
             dma((chips + 1,)),
-            dma((chips,)),
-            dma((chips,)),
+            dma((1, chips)),
+            dma((1, chips + 1)),
         ],
         cost_estimate=pl.CostEstimate(flops=0, transcendentals=0, bytes_accessed=200_000_000),
         compiler_params=pltpu.CompilerParams(
@@ -1411,15 +1547,9 @@
         field.reshape(group, model) for field in (mixed_group, feed_group, attn_group)
     )
 
-    if group <= 1024:
-        hidden, gate_back, up_back, unit_sums, down_part_out, feed_in_grad = middle(
-            8,
-            feed_group,
-            grad_group,
-            gate_up_part,
-            down_part,
-            bias_gate_up,
-            unit_live,
+    if group <= 1024 and contexts == 8:
+        hidden, gate_back, up_back, down_part_out, unit_sums, feed_in_grad = middle(
+            8, feed_group, grad_group, gate_up_part, down_part, bias_gate_up, unit_live
         )
         gate_sums, up_sums = unit_sums[0], unit_sums[1]
     else:
@@ -1437,8 +1567,8 @@
     down_out = lax.psum_scatter(
         down_part_out, "context", scatter_dimension=0, tiled=True
     ).astype(jnp.float32)
+    (down_sum,), _ = work(2, [(grad_group, after(hidden, feed_in_grad))])
     block_out = (resid + down_out + bias_down).astype(jnp.bfloat16)
-    (down_sum,), _ = work(2, [(grad_group, after(hidden, feed_in_grad))])
 
     chips = contexts // 2
     rows_wide = -(-owned // LANES) * LANES
@@ -1447,7 +1577,7 @@
     def by_owners(field):
         return field.reshape(contexts, owned, field.shape[1])
 
-    if group <= 1024:
+    if group <= 1024 and contexts == 8:
         gains = jnp.concatenate([gain_one, gain_two, jnp.zeros((6, model), jnp.float32)], axis=0)
         input_grad, sums, up_sum, attn_grad_rows, back_cols, down_rows, gate_rows = back(
             3,
@@ -1460,7 +1590,7 @@
             (queries, keyval, mask, *turns),
         )
         sums = sums[:4].reshape(4 * model)
-        attn_grad_rows = attn_grad_rows.reshape(group, shards * rows_wide)
+        attn_grad_rows = attn_grad_rows.reshape(group, attn_grad_rows.shape[2])
         back_cols = back_cols.reshape(group, back_cols.shape[2])
     else:
         grad_out = cotangent.astype(jnp.float32)
@@ -1544,6 +1674,7 @@
             [vectors, by_owners(up_sum)],
             True,
             True,
+            owned,
         )
     else:
         (back_sum,), (vectors, up_rows) = work(

time: 619 us -> 606 us (0.979)
  Pallas kernels: 573 us -> 561 us
    pallas_call x1, Pallas kernels: 73.7 us -> 65 us  [middle(): pl.pallas_call(middle_kernel, in_specs=[hbm] * 4 + [vmem] * 2, out_specs=...]
  transfers between devices with their start and end apart: 2 -> 2, of which waited for: 0 -> 0; matrix products, arithmetic and copies ran while one was open for 3% -> 3% of each run, Pallas kernels for 82% -> 83%
where the time goes in v6:
time: 606 us; the launch traced here: 598 us
  Pallas kernels  561 us (93%)
  between operations  14.7 us (2%)
  local copies, waits for them, and re-layouts  14.6 us (2%)
  other arithmetic  7.29 us (1%)
    pallas_call x1, Pallas kernels, opening(): pl.pallas_call(functools.partial(opening_kernel, gathers, spreads), in_sp...  264 us
    pallas_call x1, Pallas kernels, back(): pl.pallas_call(functools.partial(back_kernel, gate, up, swaps), in_specs=...  120 us
    pallas_call x2, Pallas kernels, work(): pl.pallas_call(functools.partial(work_kernel, made, swaps, chained, summe...  104 us
    pallas_call x1, Pallas kernels, middle(): pl.pallas_call(middle_kernel, in_specs=[hbm] * 4 + [vmem] * 2, out_specs=...  65 us
  transfers between devices with their start and end apart: 2, of which 0 were waited for; matrix products, arithmetic and copies ran while one was open for 3% of the time, Pallas kernels for 83%

profile of v6, /device:TPU:0, one launch (start us, length us, event | category | flops | bytes accessed | tf_op | source)
XLA Modules:
  0.0 598.3 jit_solution(2200944494305774117)
XLA Ops:
  7.2 0.7 all-gather.2.cloned.1.call-update
  8.0 1.3 reshape.137.refs_5_
  9.2 1.3 reshape.138.refs_6_
  10.5 1.3 reshape.139.refs_7_
  11.8 1.3 reshape.140.refs_8_
  13.1 0.6 copy.32
  13.7 1.3 reshape.141.refs_9_
  15.0 0.8 dynamic_slice.14
  15.7 0.5 fusion.5
  16.3 0.8 pad_maximum_fusion
  17.1 2.1 fusion.4.refs_11_.refs_14_
  19.3 264.5 %shard_map.220 = (bf16[128,640]{1,0:T(8,128)(2,1)}, bf16[2560,256]{1,0:T(8,128)(2,1)}, bf16[2560,1280]{1,0:T(8,128)(2,1)}, bf16[2560,1280]{1,0:T(8,128)(2,1)}, b...) custom-call(bf16[640,512]{1,0:T(8,128)(2,1)} %refs_0_.1, ...), custom_call_target="tpu_custom_call" | custom-call | bytes 700000000 | tf_op jit(solution)/shard_map/pallas_call | solution.py:532
  283.8 0.9 bitcast_convert_fusion
  284.8 0.6 copy.31
  285.4 65.0 %shard_map.221 = (bf16[1024,1024]{1,0:T(8,128)(2,1)}, bf16[1024,1024]{1,0:T(8,128)(2,1)}, bf16[1024,1024]{1,0:T(8,128)(2,1)}, bf16[1024,2560]{1,0:T(8,128)(2,1)}...) custom-call(bf16[1024,2560]{1,0:T(8,128)(2,1)} %bitcast.39, bf16[1024,2560]{1,0:T(8,128)(2,1)} %all-gather.2.cloned.1.call-done.refs_1_.refs_0_, ...), custom_call_target="tpu_custom_call" | custom-call | bytes 200000000 | tf_op jit(solution)/shard_map/pallas_call | solution.py:1418
  350.5 0.7 maximum_maximum_fusion.1.refs_11_
  351.2 0.9 slice_reduce_fusion.2
  352.2 0.1 reshape.151
  352.3 0.1 reshape.152
  352.4 51.2 %shard_map.222 = bf16[640,1024]{1,0:T(8,128)(2,1)} custom-call(bf16[1024,2560]{1,0:T(8,128)(2,1)} %all-gather.2.cloned.1.call-done.refs_1_.refs_0_, bf16[1024,1024]{1,0:T(8,128)(2,1)} %get-tuple-element.60.refs_1_), custom_call_target="tpu_custom_call" | custom-call | bytes 150000000 | tf_op jit(solution)/shard_map/pallas_call | solution.py:813
  403.6 120.1 %shard_map.223 = (f32[128,2560]{1,0:T(8,128)}, f32[8,2560]{1,0:T(8,128)}, bf16[640,1024]{1,0:T(8,128)(2,1)}, bf16[8,128,384]{2,1,0:T(8,128)(2,1)}, bf16[4,256,38...) custom-call(bf16[2560,1280]{1,0:T(8,128)(2,1)} %get-tuple-element.53.refs_0_, ...), custom_call_target="tpu_custom_call" | custom-call | bytes 400000000 | tf_op jit(solution)/shard_map/pallas_call | solution.py:1033
  523.8 0.9 slice.47
  524.7 0.1 reshape_reshape.3
  524.8 0.1 reshape.150
  524.9 0.7 copy.36
  525.7 52.9 %shard_map.224 = (bf16[640,384]{1,0:T(8,128)(2,1)}, bf16[128,2560]{1,0:T(8,128)(2,1)}, f32[8,128]{1,0:T(8,128)}, bf16[8,80,1024]{2,1,0:T(8,128)(2,1)}, bf16[8,80,384]{2,1,0:T(8,128)(2,1)}, /*index=5*/f32[8,512]{1,0:T(8,128)}) custom-call(bf16[1024,2560]{1,0:T(8,128)(2,1)} %bitcast.42, bf16[1024,384]{1,0:T(8,128)(2,1)} %bitcast.46, ...), custom_call_target="tpu_custom_call" | custom-call | bytes 150000000 | tf_op jit(solution)/shard_map/pallas_call | solution.py:813
  578.6 0.7 copy.34
  579.5 7.2 %shard_map.225 = (f32[80,7680]{1,0:T(8,128)}, f32[80,15360]{1,0:T(8,128)}, f32[80,2560]{1,0:T(8,128)}, f32[80,512]{1,0:T(8,128)}, f32[80,2560]{1,0:T(8,128)}) custom-call(bf16[8,80,1024]{2,1,0:T(8,128)(2,1)} %get-tuple-element.72.down_ref, bf16[8,80,1024]{2,1,0:T(8,128)(2,1)} %get-tuple-element.73.gate_ref, bf16[8,80,1024]{2,1,0:T(8,128)(2,1)} %get-tuple-element.74.up_ref, ...), custom_call_target="tpu_custom_call" | custom-call | tf_op jit(solution)/shard_map/pallas_call | solution.py:175
  586.7 0.6 constant_dynamic-slice_fusion.3
  587.3 0.5 fusion.6
  587.9 2.1 add_convert_fusion
  589.9 1.1 copy.39
  (34 shorter events, 0.6 us)
Async XLA Ops:
  7.2 278.2 %all-gather.2.cloned.1.call-start = ((), (), s32[]{:S(2)}) async-start(), calls=%async_computation.1 | async-start | bytes 5898240 | tf_op jit(solution)/shard_map/all_gather | solution.py:75
  7.9 579.9 %reduce-scatter.2.cloned.1.call-start = ((), (), s32[]{:S(2)}) async-start(), calls=%async_computation.2 | async-start | bytes 5898240 | tf_op jit(solution)/shard_map/reduce_scatter | solution.py:1567
  579.5 8.3 %copy-start = (f32[128,2560]{1,0:T(8,128)S(1)}, f32[128,2560]{1,0:T(8,128)}, u32[]{:S(2)}) copy-start(f32[128,2560]{1,0:T(8,128)} %get-tuple-element.47.refs_8_) | copy-start | bytes 3932164
  586.7 3.2 copy-start.1
Sparse Core Ops, SparseCore 0:
  9.7 58.7 all-gather.1
  350.5 70.1 reduce-scatter.1

commit v7 on v6

--- a/solution.py
+++ b/solution.py
@@ -363,7 +363,7 @@
         return taken
 
     sources = take(len(gathers) - 1)
-    vector_refs = take(5)
+    vector_refs = take(2)
     source_ref, mask_ref, cosine_ref, sine_ref = take(4)
     wholes = take(len(gathers))
     queries_ref, keyval_ref, resid_ref = take(3)
@@ -384,11 +384,10 @@
     half = model // 2
     others = [lax.rem(me + k, contexts) for k in range(1, contexts)]
     vectors_own[...] = jnp.zeros_like(vectors_own)
-    row, across_row = 0, vectors_own.shape[1]
+    row = 0
     for ref in vector_refs:
-        for start in range(0, ref.shape[1], across_row):
-            vectors_own[row : row + 1, :] = ref[:, start : start + across_row]
-            row += 1
+        vectors_own[row : row + ref.shape[0], :] = ref[...]
+        row += ref.shape[0]
     greet(gathers[0].near, others)
     vector_of, keyval_of, query_of, output_of, gate_up_of, down_of = gathers
     swaps = []
@@ -532,7 +531,7 @@
     outs = pl.pallas_call(
         functools.partial(opening_kernel, gathers, spreads),
         in_specs=[pl.BlockSpec(memory_space=pl.ANY)] * (len(cuts) - 1)
-        + [pl.BlockSpec(memory_space=pltpu.VMEM)] * 9,
+        + [pl.BlockSpec(memory_space=pltpu.VMEM)] * 6,
         out_specs=[pl.BlockSpec(memory_space=pl.ANY)] * len(cuts)
         + [pl.BlockSpec(memory_space=pltpu.VMEM)] * 3
         + [pl.BlockSpec(memory_space=pl.ANY)] * 3,
@@ -1510,8 +1509,8 @@
     cosine, sine = jnp.cos(angles), jnp.sin(angles)
     turns = (jnp.concatenate([cosine, cosine], axis=1), jnp.concatenate([-sine, sine], axis=1))
     vectors = [
-        each.reshape(1, each.shape[0])
-        for each in (attn_gain, output_bias, feed_gain, down_bias, gate_up_bias)
+        jnp.stack([attn_gain, output_bias, feed_gain, down_bias]),
+        gate_up_bias.reshape(-1, shard_rows),
     ]
     vector_rows = 4 + gate_up_bias.shape[0] // shard_rows
     vector_tall = -(-vector_rows // 32) * 32

time: 606 us -> 604 us (level)
  no operation moved by 1% of the time
where the time goes in v7:
time: 604 us; the launch traced here: 597 us
  Pallas kernels  561 us (93%)
  between operations  14.7 us (2%)
  local copies, waits for them, and re-layouts  12.3 us (2%)
  other arithmetic  7.9 us (1%)
    pallas_call x1, Pallas kernels, opening(): pl.pallas_call(functools.partial(opening_kernel, gathers, spreads), in_sp...  264 us
    pallas_call x1, Pallas kernels, back(): pl.pallas_call(functools.partial(back_kernel, gate, up, swaps), in_specs=...  120 us
    pallas_call x2, Pallas kernels, work(): pl.pallas_call(functools.partial(work_kernel, made, swaps, chained, summe...  104 us
    pallas_call x1, Pallas kernels, middle(): pl.pallas_call(middle_kernel, in_specs=[hbm] * 4 + [vmem] * 2, out_specs=...  64.9 us
  transfers between devices with their start and end apart: 2, of which 0 were waited for; matrix products, arithmetic and copies ran while one was open for 3% of the time, Pallas kernels for 83%

profile of v7, /device:TPU:0, one launch (start us, length us, event | category | flops | bytes accessed | tf_op | source)
XLA Modules:
  0.0 596.5 jit_solution(2859540252338706260)
XLA Ops:
  7.2 0.7 all-gather.2.cloned.1.call-update
  8.0 0.7 stack.15
  8.7 0.7 stack.16
  9.4 0.7 stack.17
  10.0 0.7 stack.18
  10.7 0.6 copy.32
  11.3 1.3 reshape.125.refs_6_
  12.6 0.8 dynamic_slice.14
  13.4 0.6 pad_maximum_fusion.2.refs_5_
  14.0 0.5 fusion.5
  14.6 0.8 pad_maximum_fusion
  15.4 2.1 fusion.4.refs_8_.refs_14_
  17.6 264.4 %shard_map.220 = (bf16[128,640]{1,0:T(8,128)(2,1)}, bf16[2560,256]{1,0:T(8,128)(2,1)}, bf16[2560,1280]{1,0:T(8,128)(2,1)}, bf16[2560,1280]{1,0:T(8,128)(2,1)}, b...) custom-call(bf16[640,512]{1,0:T(8,128)(2,1)} %refs_0_.1, ...), custom_call_target="tpu_custom_call" | custom-call | bytes 700000000 | tf_op jit(solution)/shard_map/pallas_call | solution.py:531
  282.0 0.9 bitcast_convert_fusion
  283.0 0.6 copy.31
  283.6 64.9 %shard_map.221 = (bf16[1024,1024]{1,0:T(8,128)(2,1)}, bf16[1024,1024]{1,0:T(8,128)(2,1)}, bf16[1024,1024]{1,0:T(8,128)(2,1)}, bf16[1024,2560]{1,0:T(8,128)(2,1)}...) custom-call(bf16[1024,2560]{1,0:T(8,128)(2,1)} %bitcast.39, bf16[1024,2560]{1,0:T(8,128)(2,1)} %all-gather.2.cloned.1.call-done.refs_1_.refs_0_, ...), custom_call_target="tpu_custom_call" | custom-call | bytes 200000000 | tf_op jit(solution)/shard_map/pallas_call | solution.py:1417
  348.7 0.7 maximum_maximum_fusion.1.refs_11_
  349.4 0.9 slice_reduce_fusion.2
  350.5 0.1 reshape.136
  350.6 50.9 %shard_map.222 = bf16[640,1024]{1,0:T(8,128)(2,1)} custom-call(bf16[1024,2560]{1,0:T(8,128)(2,1)} %all-gather.2.cloned.1.call-done.refs_1_.refs_0_, bf16[1024,1024]{1,0:T(8,128)(2,1)} %get-tuple-element.60.refs_1_), custom_call_target="tpu_custom_call" | custom-call | bytes 150000000 | tf_op jit(solution)/shard_map/pallas_call | solution.py:812
  401.5 120.5 %shard_map.223 = (f32[128,2560]{1,0:T(8,128)}, f32[8,2560]{1,0:T(8,128)}, bf16[640,1024]{1,0:T(8,128)(2,1)}, bf16[8,128,384]{2,1,0:T(8,128)(2,1)}, bf16[4,256,38...) custom-call(bf16[2560,1280]{1,0:T(8,128)(2,1)} %get-tuple-element.53.refs_0_, ...), custom_call_target="tpu_custom_call" | custom-call | bytes 400000000 | tf_op jit(solution)/shard_map/pallas_call | solution.py:1032
  522.0 0.9 slice.47
  522.9 0.1 reshape_reshape.3
  523.0 0.1 reshape.134
  523.2 0.7 copy.36
  523.9 53.0 %shard_map.224 = (bf16[640,384]{1,0:T(8,128)(2,1)}, bf16[128,2560]{1,0:T(8,128)(2,1)}, f32[8,128]{1,0:T(8,128)}, bf16[8,80,1024]{2,1,0:T(8,128)(2,1)}, bf16[8,80,384]{2,1,0:T(8,128)(2,1)}, /*index=5*/f32[8,512]{1,0:T(8,128)}) custom-call(bf16[1024,2560]{1,0:T(8,128)(2,1)} %bitcast.42, bf16[1024,384]{1,0:T(8,128)(2,1)} %bitcast.46, ...), custom_call_target="tpu_custom_call" | custom-call | bytes 150000000 | tf_op jit(solution)/shard_map/pallas_call | solution.py:812
  576.9 0.7 copy.34
  577.8 7.2 %shard_map.225 = (f32[80,7680]{1,0:T(8,128)}, f32[80,15360]{1,0:T(8,128)}, f32[80,2560]{1,0:T(8,128)}, f32[80,512]{1,0:T(8,128)}, f32[80,2560]{1,0:T(8,128)}) custom-call(bf16[8,80,1024]{2,1,0:T(8,128)(2,1)} %get-tuple-element.72.down_ref, bf16[8,80,1024]{2,1,0:T(8,128)(2,1)} %get-tuple-element.73.gate_ref, bf16[8,80,1024]{2,1,0:T(8,128)(2,1)} %get-tuple-element.74.up_ref, ...), custom_call_target="tpu_custom_call" | custom-call | tf_op jit(solution)/shard_map/pallas_call | solution.py:175
  585.0 0.6 constant_dynamic-slice_fusion.3
  585.6 0.5 fusion.6
  586.1 2.1 add_convert_fusion
  588.2 1.1 copy.39
  (35 shorter events, 0.7 us)
Async XLA Ops:
  7.2 276.4 %all-gather.2.cloned.1.call-start = ((), (), s32[]{:S(2)}) async-start(), calls=%async_computation.1 | async-start | bytes 5898240 | tf_op jit(solution)/shard_map/all_gather | solution.py:75
  7.9 578.2 %reduce-scatter.2.cloned.1.call-start = ((), (), s32[]{:S(2)}) async-start(), calls=%async_computation.2 | async-start | bytes 5898240 | tf_op jit(solution)/shard_map/reduce_scatter | solution.py:1566
  577.8 8.3 %copy-start = (f32[128,2560]{1,0:T(8,128)S(1)}, f32[128,2560]{1,0:T(8,128)}, u32[]{:S(2)}) copy-start(f32[128,2560]{1,0:T(8,128)} %get-tuple-element.47.refs_8_) | copy-start | bytes 3932164
  585.0 3.2 copy-start.1
Sparse Core Ops, SparseCore 0:
  9.7 58.7 all-gather.1
  348.7 70.1 reduce-scatter.1
